TPU v7x, 128 devices: a whole 4x4x4 slice. The times are simulated.
128 devices in a mesh: grp: 8 (over y, x_lo), tp: 16 (over z, x_hi, core).
Axes of the slice: x: 4 (x_hi: 2, x_lo: 2; x = x_hi * 2 + x_lo), y: 4, z: 4, core: 2. Of those that a mesh axis runs over, the one named last changes fastest.
Arguments:
- low_state: bfloat16 [16384, 16384], P('grp', 'tp'), may hold values from -6 to 6
- mid_state: bfloat16 [16384, 16384], P('grp', 'tp'), may hold values from -6 to 6
- high_state: bfloat16 [16384, 16384], P('grp', 'tp'), may hold values from -6 to 6
- w_low: bfloat16 [16384, 1024], P('tp', 'grp'), may hold values from -0.02734375 to 0.02734375
- w_mid: bfloat16 [16384, 1024], P('tp', 'grp'), may hold values from -0.02734375 to 0.02734375
- w_high: bfloat16 [16384, 1024], P('tp', 'grp'), may hold values from -0.02734375 to 0.02734375
- kv_grad: bfloat16 [16384, 1024], P(('grp', 'tp')), may hold values from -24 to 24
- loss_mask: int32 [16384], P(('grp', 'tp')), may hold values 0 or 1
Outputs:
- keys_values: bfloat16 [16384, 1024], P(('grp', 'tp'))
- grad_low: bfloat16 [16384, 1024], P('tp', 'grp')
- grad_mid: bfloat16 [16384, 1024], P('tp', 'grp')
- grad_high: bfloat16 [16384, 1024], P('tp', 'grp')
All inputs are finite; a program needn't handle non-finite values. No bound on the sum of `loss_mask` on one device may be relied on, other than what follows from the above.
Results may differ from a plain program's by a relative error of at most 0.019.
Values may be sent and summed in bfloat16 or wider, within the bound.
No kernel may reach another device: no remote copies, remote signals or barrier semaphores. Data moves between devices by JAX's collectives and lax.ppermute only.
A program may use at most 128 MiB of HBM per device.

v0:
```python
import jax
import jax.numpy as jnp
from jax import lax
from jax.sharding import PartitionSpec as P


def body(low_state, mid_state, high_state, w_low, w_mid, w_high, kv_grad, loss_mask):
    states = (low_state, mid_state, high_state)
    scale = (kv_grad.shape[0] * lax.axis_size("tp") * lax.axis_size("grp")) ** (-0.5)
    contrib = jnp.dot(
        states[0],
        lax.all_gather(w_low, "grp", axis=1, tiled=True),
        preferred_element_type=jnp.float32,
    )
    contrib = contrib + jnp.dot(
        states[1],
        lax.all_gather(w_mid, "grp", axis=1, tiled=True),
        preferred_element_type=jnp.float32,
    )
    contrib = contrib + jnp.dot(
        states[2],
        lax.all_gather(w_high, "grp", axis=1, tiled=True),
        preferred_element_type=jnp.float32,
    )
    keys_values = lax.psum_scatter(
        contrib.astype(jnp.bfloat16), "tp", scatter_dimension=0, tiled=True
    )
    masked = (kv_grad.astype(jnp.float32) * loss_mask.astype(jnp.float32)[:, None]).astype(
        jnp.bfloat16
    )
    gathered = lax.all_gather(masked, "tp", axis=0, tiled=True)

    def stream_term(state):
        product = lax.dot_general(
            state, gathered, (((0,), (0,)), ((), ())), preferred_element_type=jnp.float32
        )
        return lax.optimization_barrier((product * scale).astype(jnp.bfloat16)).astype(jnp.float32)

    return (
        keys_values,
        lax.psum_scatter(
            stream_term(states[0]).astype(jnp.bfloat16), "grp", scatter_dimension=1, tiled=True
        ),
        lax.psum_scatter(
            stream_term(states[1]).astype(jnp.bfloat16), "grp", scatter_dimension=1, tiled=True
        ),
        lax.psum_scatter(
            stream_term(states[2]).astype(jnp.bfloat16), "grp", scatter_dimension=1, tiled=True
        ),
    )


def solution(mesh):
    in_specs = (
        P("grp", "tp"),
        P("grp", "tp"),
        P("grp", "tp"),
        P("tp", "grp"),
        P("tp", "grp"),
        P("tp", "grp"),
        P(("grp", "tp"), None),
        P(("grp", "tp")),
    )
    out_specs = (P(("grp", "tp"), None), P("tp", "grp"), P("tp", "grp"), P("tp", "grp"))
    return jax.shard_map(body, mesh=mesh, in_specs=in_specs, out_specs=out_specs, check_vma=False)
```

profile of v0, /device:TPU:0, one launch (start us, length us, event | category | flops | bytes accessed | tf_op | source)
XLA Modules:
  0.0 481.8 jit_solution(13493969472436964121)
XLA Ops:
  7.2 0.0 all-gather.11.cloned.1.call-start
  7.2 0.7 convert_element_type.38
  7.9 1.8 multiply_convert_fusion.3
  9.6 0.0 all-gather.11.cloned.1.call-update
  9.7 0.0 all-gather.5.cloned.1.call-start
  9.7 0.7 all-gather.5.cloned.1.call-update
  10.4 0.0 all-gather.7.cloned.1.call-start
  10.5 0.7 all-gather.7.cloned.1.call-update
  11.1 0.0 all-gather.9.cloned.1.call-start
  11.2 0.5 all-gather.9.cloned.1.call-update
  11.7 0.0 reduce-scatter.7.cloned.1.call-start
  11.8 57.2 %all-gather.11.cloned.1.call-done = bf16[2048,1024]{1,0:T(8,128)(2,1)} async-done(((bf16[128,1024]{1,0:T(8,128)(2,1)}), bf16[2048,1024]{1,0:T(8,128)(2,1)}) %all-gather.11.cloned.1.call-update) | async-done | bytes 4194320 | tf_op jit(solution)/shard_map/all_gather | solution.py:31
  69.0 9.4 %fusion = bf16[1024,1024]{0,1:T(8,128)(2,1)} fusion(bf16[2048,1024]{1,0:T(8,128)(2,1)} %all-gather.11.cloned.1.call-done, bf16[2048,1024]{1,0:T(8,128)(2,1)} %param.8), kind=kOutput, calls=%fused_computation.4 | convolution fusion | flops 4297064448 | bytes 10485760 | tf_op jit(solution)/shard_map/dot_general | solution.py:34
  78.3 0.0 reduce-scatter.7.cloned.1.call-update
  78.4 0.0 reduce-scatter.9.cloned.1.call-start
  78.4 9.4 %fusion.1 = bf16[1024,1024]{0,1:T(8,128)(2,1)} fusion(bf16[2048,1024]{1,0:T(8,128)(2,1)} %all-gather.11.cloned.1.call-done, bf16[2048,1024]{1,0:T(8,128)(2,1)} %param.9), kind=kOutput, calls=%fused_computation.5 | convolution fusion | flops 4297064448 | bytes 10485760 | tf_op jit(solution)/shard_map/dot_general | solution.py:34
  87.8 0.2 reduce-scatter.11.cloned.1.call-start
  88.1 9.4 %fusion.2 = bf16[1024,1024]{0,1:T(8,128)(2,1)} fusion(bf16[2048,1024]{1,0:T(8,128)(2,1)} %all-gather.11.cloned.1.call-done, bf16[2048,1024]{1,0:T(8,128)(2,1)} %param.10), kind=kOutput, calls=%fused_computation.6 | convolution fusion | flops 4297064448 | bytes 10485760 | tf_op jit(solution)/shard_map/dot_general | solution.py:34
  97.5 0.0 reduce-scatter.5.cloned.1.call-start
  97.6 22.2 %all-gather.5.cloned.1.call-done = bf16[1024,1024]{1,0:T(8,128)(2,1)} async-done(((bf16[1024,128]{1,0:T(8,128)(2,1)}), bf16[1024,1024]{1,0:T(8,128)(2,1)}) %all-gather.5.cloned.1.call-update) | async-done | bytes 2097168 | tf_op jit(solution)/shard_map/all_gather | solution.py:12
  119.7 10.6 %fusion.3 = f32[2048,1024]{1,0:T(8,128)} fusion(bf16[2048,1024]{1,0:T(8,128)(2,1)} %param.8, bf16[1024,1024]{1,0:T(8,128)(2,1)} %all-gather.5.cloned.1.call-done), kind=kOutput, calls=%fused_computation.8 | convolution fusion | flops 4294967296 | bytes 14680064 | tf_op jit(solution)/shard_map/dot_general | solution.py:10
  130.4 43.0 %all-gather.7.cloned.1.call-done = bf16[1024,1024]{1,0:T(8,128)(2,1)} async-done(((bf16[1024,128]{1,0:T(8,128)(2,1)}), bf16[1024,1024]{1,0:T(8,128)(2,1)}) %all-gather.7.cloned.1.call-update) | async-done | bytes 2097168 | tf_op jit(solution)/shard_map/all_gather | solution.py:17
  173.4 10.6 %fusion.4 = f32[2048,1024]{1,0:T(8,128)} fusion(bf16[2048,1024]{1,0:T(8,128)(2,1)} %param.9, bf16[1024,1024]{1,0:T(8,128)(2,1)} %all-gather.7.cloned.1.call-done), kind=kOutput, calls=%fused_computation.9 | convolution fusion | flops 4294967296 | bytes 14680064 | tf_op jit(solution)/shard_map/dot_general | solution.py:15
  184.0 42.8 %all-gather.9.cloned.1.call-done = bf16[1024,1024]{1,0:T(8,128)(2,1)} async-done(((bf16[1024,128]{1,0:T(8,128)(2,1)}), bf16[1024,1024]{1,0:T(8,128)(2,1)}) %all-gather.9.cloned.1.call-update) | async-done | bytes 2097168 | tf_op jit(solution)/shard_map/all_gather | solution.py:22
  226.8 14.3 %add_convert_fusion = bf16[2048,1024]{1,0:T(8,128)(2,1)} fusion(f32[2048,1024]{1,0:T(8,128)} %fusion.3, f32[2048,1024]{1,0:T(8,128)} %fusion.4, bf16[2048,1024]{1,0:T(8,128)(2,1)} %param.10, bf16[1024,1024]{1,0:T(8,128)(2,1)} %all-gather.9.cloned.1.call-done), kind=kOutput, calls=%fused_computation | convolution fusion | flops 4301258752 | bytes 27262976 | tf_op jit(solution)/shard_map/dot_general | solution.py:20
  241.1 41.1 %reduce-scatter.7.cloned.1.call-done = bf16[1024,128]{0,1:T(8,128)(2,1)} async-done(((bf16[1024,1024]{0,1:T(8,128)(2,1)}), bf16[1024,128]{0,1:T(8,128)(2,1)}) %reduce-scatter.7.cloned.1.call-update) | async-done | bytes 262160 | tf_op jit(solution)/shard_map/reduce_scatter | solution.py:41
  282.2 1.8 copy.12
  284.0 52.2 %reduce-scatter.9.cloned.1.call-done = bf16[1024,128]{0,1:T(8,128)(2,1)} async-done(((bf16[1024,1024]{0,1:T(8,128)(2,1)}), bf16[1024,128]{0,1:T(8,128)(2,1)}) %reduce-scatter.9.cloned.1.call-update) | async-done | bytes 262160 | tf_op jit(solution)/shard_map/reduce_scatter | solution.py:44
  336.2 1.8 copy.13
  338.0 52.4 %reduce-scatter.11.cloned.1.call-done = bf16[1024,128]{0,1:T(8,128)(2,1)} async-done(((bf16[1024,1024]{0,1:T(8,128)(2,1)}), bf16[1024,128]{0,1:T(8,128)(2,1)}) %reduce-scatter.11.cloned.1.call-update) | async-done | bytes 262160 | tf_op jit(solution)/shard_map/reduce_scatter | solution.py:47
  390.4 1.8 copy.14
  392.1 82.8 %reduce-scatter.5.cloned.1.call-done = bf16[128,1024]{1,0:T(8,128)(2,1)} async-done(((bf16[2048,1024]{1,0:T(8,128)(2,1)}), bf16[128,1024]{1,0:T(8,128)(2,1)}) %reduce-scatter.5.cloned.1.call-update) | async-done | bytes 262160 | tf_op jit(solution)/shard_map/reduce_scatter | solution.py:25
  (3 shorter events, 0.0 us)
Async XLA Ops:
  7.2 61.8 %all-gather.11.cloned.1.call-start = ((), (), s32[]{:S(2)}) async-start(), calls=%async_computation.8 | async-start | bytes 4456448 | tf_op jit(solution)/shard_map/all_gather | solution.py:31
  9.7 110.1 %all-gather.5.cloned.1.call-start = ((), (), s32[]{:S(2)}) async-start(), calls=%async_computation.4 | async-start | bytes 2359296 | tf_op jit(solution)/shard_map/all_gather | solution.py:12
  10.4 163.0 %all-gather.7.cloned.1.call-start = ((), (), s32[]{:S(2)}) async-start(), calls=%async_computation.5 | async-start | bytes 2359296 | tf_op jit(solution)/shard_map/all_gather | solution.py:17
  11.1 215.7 %all-gather.9.cloned.1.call-start = ((), (), s32[]{:S(2)}) async-start(), calls=%async_computation.6 | async-start | bytes 2359296 | tf_op jit(solution)/shard_map/all_gather | solution.py:22
  11.7 270.4 %reduce-scatter.7.cloned.1.call-start = ((), (), s32[]{:S(2)}) async-start(), calls=%async_computation.9 | async-start | bytes 2359296 | tf_op jit(solution)/shard_map/reduce_scatter | solution.py:41
  78.4 257.8 %reduce-scatter.9.cloned.1.call-start = ((), (), s32[]{:S(2)}) async-start(), calls=%async_computation.10 | async-start | bytes 2359296 | tf_op jit(solution)/shard_map/reduce_scatter | solution.py:44
  87.8 302.5 %reduce-scatter.11.cloned.1.call-start = ((), (), s32[]{:S(2)}) async-start(), calls=%async_computation.11 | async-start | bytes 2359296 | tf_op jit(solution)/shard_map/reduce_scatter | solution.py:47
  97.5 377.4 %reduce-scatter.5.cloned.1.call-start = ((), (), s32[]{:S(2)}) async-start(), calls=%async_computation.7 | async-start | bytes 4456448 | tf_op jit(solution)/shard_map/reduce_scatter | solution.py:25
Sparse Core Ops, SparseCore 0:
  11.0 57.8 all-gather.10
  70.5 49.1 all-gather.4
  121.3 51.9 all-gather.6
  174.8 51.9 all-gather.8
  229.1 53.0 reduce-scatter.6
  284.4 51.7 reduce-scatter.8
  338.6 51.7 reduce-scatter.10
  394.9 79.9 reduce-scatter.4
where the time goes:
time: 482 us
  waiting for transfers between devices  396 us (82%)
  matrix products  63.7 us (13%)
  between operations  14.1 us (3%)
  local copies, waits for them, and re-layouts  5.37 us (1%)
    reduce_scatter x1, waiting for transfers between devices, body(): lax.psum_scatter(contrib.astype(jnp.bfloat16), 'tp', scatter_dimension=0,...  82.8 us
    all_gather x1, waiting for transfers between devices, body(): gathered = lax.all_gather(masked, 'tp', axis=0, tiled=True)  57.2 us
    reduce_scatter x1, waiting for transfers between devices, body(): lax.psum_scatter(stream_term(states[2]).astype(jnp.bfloat16), 'grp', scat...  52.4 us
    reduce_scatter x1, waiting for transfers between devices, body(): lax.psum_scatter(stream_term(states[1]).astype(jnp.bfloat16), 'grp', scat...  52.2 us
    all_gather x1, waiting for transfers between devices, body(): lax.all_gather(w_mid, 'grp', axis=1, tiled=True)  43 us
    all_gather x1, waiting for transfers between devices, body(): lax.all_gather(w_high, 'grp', axis=1, tiled=True)  42.8 us
    reduce_scatter x1, waiting for transfers between devices, body(): lax.psum_scatter(stream_term(states[0]).astype(jnp.bfloat16), 'grp', scat...  41.1 us
    dot_general x3, matrix products, stream_term(): lax.dot_general(state, gathered, (((0,), (0,)), ((), ())), preferred_elem...  28.2 us
  transfers between devices with their start and end apart: 8, of which 8 were waited for; matrix products, arithmetic and copies ran while one was open for 14% of the time, Pallas kernels for 0%

commit v1 on v0

v1 whole, which is shorter than its diff:
```python
import jax
import jax.numpy as jnp
from jax import lax
from jax.experimental import pallas as pl
from jax.experimental.pallas import tpu as pltpu
from jax.sharding import PartitionSpec as P

BF = jnp.bfloat16
F32 = jnp.float32
VMEM_LIMIT = 48 * 1024 * 1024
GRP, TP = 8, 16
FULL = ("grp", "tp")


def full_perm(move):
    pairs = []
    for g in range(GRP):
        for t in range(TP):
            y, xl, z, xh, c = move(g // 2, g % 2, t // 4, t // 2 % 2, t % 2)
            pairs.append((g * TP + t, (y % 4 * 2 + xl % 2) * TP + z % 4 * 4 + xh % 2 * 2 + c % 2))
    return pairs


Y1 = full_perm(lambda y, xl, z, xh, c: (y + 1 - 2 * c, xl, z, xh, c))
Y2 = full_perm(lambda y, xl, z, xh, c: (y - 1 + 2 * c, xl, z, xh, c))
Z1 = full_perm(lambda y, xl, z, xh, c: (y, xl, z + 1 - 2 * c, xh, c))
Z2 = full_perm(lambda y, xl, z, xh, c: (y, xl, z - 1 + 2 * c, xh, c))
XL = full_perm(lambda y, xl, z, xh, c: (y, xl + 1, z, xh, c))
XH = full_perm(lambda y, xl, z, xh, c: (y, xl, z, xh + 1, c))
CORE = full_perm(lambda y, xl, z, xh, c: (y, xl, z, xh, c + 1))


def send(array, pairs):
    return lax.ppermute(array, FULL, pairs)


def add(*arrays):
    total = arrays[0].astype(F32)
    for array in arrays[1:]:
        total = total + array.astype(F32)
    return total.astype(BF)


def place():
    g = lax.axis_index("grp")
    t = lax.axis_index("tp")
    c = t % 2
    return g // 2, g % 2, t // 4, t // 2 % 2, c, 1 - 2 * c


def params():
    return pltpu.CompilerParams(vmem_limit_bytes=VMEM_LIMIT)


def whole(*shape):
    return pl.BlockSpec(shape, lambda *_: (0,) * len(shape))


def mask_kernel(grad_ref, mask_ref, out_ref):
    turned = grad_ref[...].astype(F32).T
    out_ref[...] = (turned * mask_ref[...].astype(F32)).astype(BF)


def masked_turned(kv_grad, loss_mask):
    rows, cols = kv_grad.shape
    return pl.pallas_call(
        mask_kernel,
        out_shape=jax.ShapeDtypeStruct((cols, rows), BF),
        compiler_params=params(),
        cost_estimate=pl.CostEstimate(flops=rows * cols, bytes_accessed=4 * rows * cols, transcendentals=0),
        name="masked",
    )(kv_grad, loss_mask.reshape(1, rows))


def forward_kernel(s0, s1, s2, w0, w1, w2, w3, even_ref, odd_ref, w_all):
    @pl.when(pl.program_id(0) == 0)
    def _():
        c = lax.axis_index("tp") % 2
        for i, w in ((0, w0), (1, w1), (2 + c, w2), (3 - c, w3)):
            w_all[:, pl.ds(pl.multiple_of(i * 128, 128), 128)] = w[...]

    depth = s0.shape[1]
    total = jnp.dot(s0[...], w_all[0:depth, :], preferred_element_type=F32)
    total += jnp.dot(s1[...], w_all[depth:2 * depth, :], preferred_element_type=F32)
    total += jnp.dot(s2[...], w_all[2 * depth:3 * depth, :], preferred_element_type=F32)
    total = total.astype(BF)
    mine = lax.axis_index("tp") % 2 == 0
    for h in range(2):
        first = total[h * 256:h * 256 + 128]
        second = total[h * 256 + 128:h * 256 + 256]
        even_ref[0, h] = jnp.where(mine, first, second)
        odd_ref[0, h] = jnp.where(mine, second, first)


def forward(states, blocks):
    tokens, depth = states[0].shape
    cols = 128 * len(blocks)
    state_spec = pl.BlockSpec((512, depth), lambda i: (i, 0))
    out_spec = pl.BlockSpec((1, 2, 128, cols), lambda i: (i, 0, 0, 0))
    out = jax.ShapeDtypeStruct((4, 2, 128, cols), BF)
    return pl.pallas_call(
        forward_kernel,
        grid=(4,),
        in_specs=[state_spec] * 3 + [whole(3 * depth, 128)] * 4,
        out_specs=[out_spec, out_spec],
        out_shape=[out, out],
        scratch_shapes=[pltpu.VMEM((3 * depth, cols), BF)],
        compiler_params=params(),
        cost_estimate=pl.CostEstimate(
            flops=6 * tokens * depth * cols, bytes_accessed=6 * tokens * depth + 8 * depth * cols, transcendentals=0
        ),
        name="forward",
    )(*states, *blocks)


def backward_kernel(other, m0, m1, m2, m3, s0, s1, s2, p2, pm, pp, p0, turned):
    y, xl, z, xh, c, d = place()
    half = (xl + 1) % 2 if other else xl

    @pl.when(pl.program_id(0) == 0)
    def _():
        for ref, flip, second in ((m0, 0, 0), (m1, 1, 0), (m2, 0, 1), (m3, 1, 1)):
            core = (c + flip) % 2
            way = 1 - 2 * core
            if second:
                spots = ((z + 2, xh), (z - way, xh + 1), (z + way, xh + 1), (z + 2, xh + 1))
            else:
                spots = ((z, xh), (z - way, xh), (z + way, xh), (z, xh + 1))
            for j, (zz, hh) in enumerate(spots):
                token = (zz + 4) % 4 * 4 + hh % 2 * 2 + core
                lanes = pl.ds(pl.multiple_of(token * 128, 128), 128)
                for r, yy in enumerate((y + 2, y - d, y + d, y)):
                    rows = pl.ds(pl.multiple_of(((yy + 4) % 4 * 2 + half) * 128, 128), 128)
                    turned[r * 128:(r + 1) * 128, lanes] = ref[j, rows, :]

    for s, state in enumerate((s0, s1, s2)):
        product = jnp.dot(turned[...], state[...], preferred_element_type=F32) * (16384 ** -0.5)
        product = product.astype(BF)
        for r, out in enumerate((p2, pm, pp, p0)):
            out[s] = product[r * 128:(r + 1) * 128]


def backward(states, masked, other):
    tokens, depth = states[0].shape
    tile = 256
    out_spec = pl.BlockSpec((3, 128, tile), lambda i: (0, 0, i))
    out = jax.ShapeDtypeStruct((3, 128, depth), BF)

    def kernel(*refs):
        backward_kernel(other, *refs)

    return pl.pallas_call(
        kernel,
        grid=(depth // tile,),
        in_specs=[whole(*masked[0].shape)] * 4 + [pl.BlockSpec((tokens, tile), lambda i: (0, i))] * 3,
        out_specs=[out_spec] * 4,
        out_shape=[out] * 4,
        scratch_shapes=[pltpu.VMEM((512, tokens), BF)],
        compiler_params=params(),
        cost_estimate=pl.CostEstimate(
            flops=6 * tokens * depth * 512, bytes_accessed=6 * tokens * depth + 16 * tokens * 256, transcendentals=0
        ),
        name="backward_other" if other else "backward_own",
    )(*masked, *states)


def pick_kernel(mine, theirs, q2, qm, qp, q0):
    _, _, z, _, _, d = place()
    for out, zz in ((q2, z + 2), (qm, z - d), (qp, z + d), (q0, z)):
        k = (zz + 4) % 4
        out[...] = (mine[k].astype(F32) + theirs[k].astype(F32)).astype(BF)


def pick(mine, theirs):
    out = jax.ShapeDtypeStruct(mine.shape[1:], BF)
    return pl.pallas_call(
        pick_kernel,
        out_shape=[out] * 4,
        compiler_params=params(),
        cost_estimate=pl.CostEstimate(flops=mine.size, bytes_accessed=6 * mine.size, transcendentals=0),
        name="pick",
    )(mine, theirs)


def split_kernel(a, b, c, mine, theirs):
    h = lax.axis_index("tp") // 2 % 2
    for out, k in ((mine, h), (theirs, (h + 1) % 2)):
        out[...] = (a[k].astype(F32) + b[k].astype(F32) + c[k].astype(F32)).astype(BF)


def split(a, b, c):
    out = jax.ShapeDtypeStruct(a.shape[1:], BF)
    return pl.pallas_call(
        split_kernel,
        out_shape=[out] * 2,
        compiler_params=params(),
        cost_estimate=pl.CostEstimate(flops=2 * a.size, bytes_accessed=8 * a.size, transcendentals=0),
        name="split",
    )(a, b, c)


def join_kernel(a0, b0, a1, b1, out):
    y, xl, _, _, _, _ = place()
    first = ((y, xl), (y, xl + 1), (y - 1, xl), (y + 1, xl))
    second = ((y + 2, xl), (y + 2, xl + 1), (y - 1, xl + 1), (y + 1, xl + 1))
    for a, b, spots in ((a0, b0, first), (a1, b1, second)):
        for j, (yy, hh) in enumerate(spots):
            lanes = pl.ds(pl.multiple_of(((yy + 4) % 4 * 2 + hh % 2) * 128, 128), 128)
            cut = slice(j * 128, (j + 1) * 128)
            out[:, lanes] = (a[:, cut].astype(F32) + b[:, cut].astype(F32)).astype(BF)


def join(a0, b0, a1, b1):
    rows, cols = a0.shape
    return pl.pallas_call(
        join_kernel,
        out_shape=jax.ShapeDtypeStruct((rows, 2 * cols), BF),
        compiler_params=params(),
        cost_estimate=pl.CostEstimate(flops=2 * a0.size, bytes_accessed=12 * a0.size, transcendentals=0),
        name="join",
    )(a0, b0, a1, b1)


def finish_kernel(a, b, c, e, g0, g1, g2):
    for s, out in enumerate((g0, g1, g2)):
        total = a[s].astype(F32) + b[s].astype(F32) + c[s].astype(F32) + e[s].astype(F32)
        out[...] = total.T.astype(BF)


def finish(a, b, c, e):
    _, cols, depth = a.shape
    return pl.pallas_call(
        finish_kernel,
        out_shape=[jax.ShapeDtypeStruct((depth, cols), BF)] * 3,
        compiler_params=params(),
        cost_estimate=pl.CostEstimate(flops=4 * a.size, bytes_accessed=10 * a.size, transcendentals=0),
        name="finish",
    )(a, b, c, e)


def scatter_tokens(mine, theirs):
    theirs = send(theirs, CORE)
    q2, qm, qp, q0 = pick(mine, theirs)
    t3 = send(q2, Z2)
    t2 = send(qp, Z1)
    t1 = send(add(qm, t3), Z2)
    kept, given = split(q0, t1, t2)
    return kept, send(given, XH)


def body(low_state, mid_state, high_state, w_low, w_mid, w_high, kv_grad, loss_mask):
    states = (low_state, mid_state, high_state)
    w = jnp.concatenate((w_low, w_mid, w_high), axis=0)
    mt = masked_turned(kv_grad, loss_mask)

    x1 = send(w, XL)
    a1 = send(w, Y1)
    a2 = send(w, Y2)
    m_h = send(mt, XH)
    m_1 = send(mt, Z1)
    m_2 = send(mt, Z2)
    m_3 = send(m_1, Z1)
    h_1 = send(m_h, Z1)
    h_2 = send(m_h, Z2)
    h_3 = send(h_1, Z1)
    near = jnp.stack((mt, m_1, m_2, m_h))
    near_other = send(near, CORE)
    far = jnp.stack((m_3, h_1, h_2, h_3))
    far_other = send(far, CORE)
    masked = (near, near_other, far, far_other)

    a3 = send(a1, Y1)
    b1 = send(x1, Y1)
    b2 = send(x1, Y2)
    b3 = send(a3, XL)

    mine, theirs = forward(states, (w, x1, a1, a2))
    kept_a, got_a = scatter_tokens(mine, theirs)

    p2x, pmx, ppx, p0x = backward(states, masked, True)
    e1 = send(p2x, XL)
    e2 = send(pmx, Y2)
    e3 = send(ppx, Y1)
    p2, pm, pp, p0 = backward(states, masked, False)
    f3 = send(add(p2, e1), Y2)
    f2 = send(pp, Y1)
    fx = send(add(p0x, e2, e3), XL)
    f1 = send(add(pm, f3), Y2)

    mine, theirs = forward(states, (a3, b3, b1, b2))
    kept_b, got_b = scatter_tokens(mine, theirs)

    keys_values = join(kept_a, got_a, kept_b, got_b)
    return (keys_values, *finish(p0, fx, f1, f2))


def solution(mesh):
    in_specs = (
        P("grp", "tp"),
        P("grp", "tp"),
        P("grp", "tp"),
        P("tp", "grp"),
        P("tp", "grp"),
        P("tp", "grp"),
        P(("grp", "tp"), None),
        P(("grp", "tp")),
    )
    out_specs = (P(("grp", "tp"), None), P("tp", "grp"), P("tp", "grp"), P("tp", "grp"))
    return jax.shard_map(body, mesh=mesh, in_specs=in_specs, out_specs=out_specs, check_vma=False)
```

time: 482 us -> 150 us (0.31)
  waiting for transfers between devices: 396 us -> 32 us
  matrix products: 63.7 us -> 0 us
  starting transfers between devices: 0.5 us -> 58.2 us
  Pallas kernels: 0 us -> 46.2 us
  between operations: 14.1 us -> 0.87 us
    reduce_scatter x4 -> x0, waiting for transfers between devices: 228 us -> none  [the longest x1 82.8 us: body(): lax.psum_scatter(contrib.astype(jnp.bfloat16), 'tp', scatter_dimension=0,...]
    all_gather x4 -> x0, waiting for transfers between devices: 165 us -> none  [the longest x1 57.2 us: body(): gathered = lax.all_gather(masked, 'tp', axis=0, tiled=True)]
    dot_general x6 -> x0, matrix products: 63.7 us -> none  [the longest x3 28.2 us: stream_term(): lax.dot_general(state, gathered, (((0,), (0,)), ((), ())), preferred_elem...]
    ppermute x0 -> x33, starting transfers between devices: none -> 58.2 us  [send(): return lax.ppermute(array, FULL, pairs)]
    pallas_call x0 -> x11, Pallas kernels: none -> 46.2 us  [the longest x2 23.1 us: backward(): pl.pallas_call(kernel, grid=(depth // tile,), in_specs=[whole(*masked[0]....]
    ppermute x0 -> x33, waiting for transfers between devices: none -> 32 us  [send(): return lax.ppermute(array, FULL, pairs)]
  transfers between devices with their start and end apart: 8 -> 33, of which waited for: 8 -> 10; matrix products, arithmetic and copies ran while one was open for 14% -> 4% of each run, Pallas kernels for 0% -> 30%
where the time goes in v1:
time: 150 us
  starting transfers between devices  58.2 us (39%)
  Pallas kernels  46.2 us (31%)
  waiting for transfers between devices  32 us (21%)
  local copies, waits for them, and re-layouts  7.62 us (5%)
  other arithmetic  4.61 us (3%)
    ppermute x33, starting transfers between devices, send(): return lax.ppermute(array, FULL, pairs)  58.2 us
    ppermute x33, waiting for transfers between devices, send(): return lax.ppermute(array, FULL, pairs)  32 us
    pallas_call x2, Pallas kernels, backward(): pl.pallas_call(kernel, grid=(depth // tile,), in_specs=[whole(*masked[0]....  23.1 us
    pallas_call x2, Pallas kernels, forward(): pl.pallas_call(forward_kernel, grid=(4,), in_specs=[state_spec] * 3 + [wh...  20.3 us
    unnamed x18, local copies, waits for them, and re-layouts  7.58 us
    convert_element_type x5, other arithmetic, add(): return total.astype(BF)  4.35 us
  transfers between devices with their start and end apart: 33, of which 10 were waited for; matrix products, arithmetic and copies ran while one was open for 4% of the time, Pallas kernels for 30%

profile of v1, /device:TPU:0, one launch (start us, length us, event | category | flops | bytes accessed | tf_op | source)
XLA Modules:
  0.0 149.6 jit_solution(10314416837439948339)
XLA Ops:
  2.4 3.2 %collective-permute-start.19 = (bf16[1024,128]{1,0:T(8,128)(2,1)S(1)}, bf16[1024,128]{1,0:T(8,128)(2,1)S(1)}, u32[]{:S(2)}, u32[]{:S(2)}) collective-permute-start(bf16[1024,128]{1,0:T(8,128)(2,1)S(1)} %masked.1), channel_id=1, source_target_pairs={{0,2},{1,3},{2,0},{3,1},{4,6},{5,7},{6,4},{7,5},{8,10},{9,11},{10,... | collective-permute-start | bytes 786440 | tf_op jit(solution)/shard_map/ppermute | solution.py:34
  5.6 1.9 %collective-permute-start.17 = (bf16[1024,128]{1,0:T(8,128)(2,1)S(1)}, bf16[1024,128]{1,0:T(8,128)(2,1)S(1)}, u32[]{:S(2)}, u32[]{:S(2)}) collective-permute-start(bf16[1024,128]{1,0:T(8,128)(2,1)S(1)} %masked.1), channel_id=1, source_target_pairs={{0,4},{1,13},{2,6},{3,15},{4,8},{5,1},{6,10},{7,3},{8,12},{9,5},{1... | collective-permute-start | bytes 786440 | tf_op jit(solution)/shard_map/ppermute | solution.py:34
  7.5 2.1 %collective-permute-start.18 = (bf16[1024,128]{1,0:T(8,128)(2,1)S(1)}, bf16[1024,128]{1,0:T(8,128)(2,1)S(1)}, u32[]{:S(2)}, u32[]{:S(2)}) collective-permute-start(bf16[1024,128]{1,0:T(8,128)(2,1)S(1)} %masked.1), channel_id=1, source_target_pairs={{0,12},{1,5},{2,14},{3,7},{4,0},{5,9},{6,2},{7,11},{8,4},{9,13},{1... | collective-permute-start | bytes 786440 | tf_op jit(solution)/shard_map/ppermute | solution.py:34
  11.9 2.1 %collective-permute-start.22 = (bf16[1024,128]{1,0:T(8,128)(2,1)S(1)}, bf16[1024,128]{1,0:T(8,128)(2,1)S(1)}, u32[]{:S(2)}, u32[]{:S(2)}) collective-permute-start(bf16[1024,128]{1,0:T(8,128)(2,1)S(1)} %collective-permute-done.19), channel_id=1, source_target_pairs={{0,4},{1,13},{2,6},{3,15},{4,8},{5,1},{6,10},{7,3},{8,12},{9,5},{1... | collective-permute-start | bytes 786440 | tf_op jit(solution)/shard_map/ppermute | solution.py:34
  15.0 2.2 %collective-permute-start.23 = (bf16[1024,128]{1,0:T(8,128)(2,1)S(1)}, bf16[1024,128]{1,0:T(8,128)(2,1)S(1)}, u32[]{:S(2)}, u32[]{:S(2)}) collective-permute-start(bf16[1024,128]{1,0:T(8,128)(2,1)S(1)} %collective-permute-done.19), channel_id=1, source_target_pairs={{0,12},{1,5},{2,14},{3,7},{4,0},{5,9},{6,2},{7,11},{8,4},{9,13},{1... | collective-permute-start | bytes 786440 | tf_op jit(solution)/shard_map/ppermute | solution.py:34
  17.2 1.6 %collective-permute-start.1 = (bf16[3072,128]{1,0:T(8,128)(2,1)S(1)}, bf16[3072,128]{1,0:T(8,128)(2,1)S(1)}, u32[]{:S(2)}, u32[]{:S(2)}) collective-permute-start(bf16[3072,128]{1,0:T(8,128)(2,1)S(1)} %constant_dynamic-update-slice_fusion.w0), channel_id=1, source_target_pairs={{0,32},{1,97},{2,34},{3,99},{4,36},{5,101},{6,38},{7,103},{8,40},{... | collective-permute-start | bytes 2359304 | tf_op jit(solution)/shard_map/ppermute | solution.py:34
  18.9 2.3 %collective-permute-done.22 = bf16[1024,128]{1,0:T(8,128)(2,1)S(1)} collective-permute-done((bf16[1024,128]{1,0:T(8,128)(2,1)S(1)}, bf16[1024,128]{1,0:T(8,128)(2,1)S(1)}, u32[]{:S(2)}, u32[]{:S(2)}) %collective-permute-start.22) | collective-permute-done | bytes 262176 | tf_op jit(solution)/shard_map/ppermute | solution.py:34
  23.5 3.4 %collective-permute-start.2 = (bf16[3072,128]{1,0:T(8,128)(2,1)S(1)}, bf16[3072,128]{1,0:T(8,128)(2,1)S(1)}, u32[]{:S(2)}, u32[]{:S(2)}) collective-permute-start(bf16[3072,128]{1,0:T(8,128)(2,1)S(1)} %constant_dynamic-update-slice_fusion.w0), channel_id=1, source_target_pairs={{0,96},{1,33},{2,98},{3,35},{4,100},{5,37},{6,102},{7,39},{8,104},... | collective-permute-start | bytes 2359304 | tf_op jit(solution)/shard_map/ppermute | solution.py:34
  27.1 2.1 %collective-permute-done.24 = bf16[1024,128]{1,0:T(8,128)(2,1)S(1)} collective-permute-done((bf16[1024,128]{1,0:T(8,128)(2,1)S(1)}, bf16[1024,128]{1,0:T(8,128)(2,1)S(1)}, u32[]{:S(2)}, u32[]{:S(2)}) %collective-permute-start.24) | collective-permute-done | bytes 262176 | tf_op jit(solution)/shard_map/ppermute | solution.py:34
  29.5 3.2 %collective-permute-done.1.w2 = bf16[3072,128]{1,0:T(8,128)(2,1)S(1)} collective-permute-done((bf16[3072,128]{1,0:T(8,128)(2,1)S(1)}, bf16[3072,128]{1,0:T(8,128)(2,1)S(1)}, u32[]{:S(2)}, u32[]{:S(2)}) %collective-permute-start.1) | collective-permute-done | bytes 786464 | tf_op jit(solution)/shard_map/ppermute | solution.py:34
  32.7 1.6 %collective-permute-start.8 = (bf16[3072,128]{1,0:T(8,128)(2,1)S(1)}, bf16[3072,128]{1,0:T(8,128)(2,1)S(1)}, u32[]{:S(2)}, u32[]{:S(2)}) collective-permute-start(bf16[3072,128]{1,0:T(8,128)(2,1)S(1)} %collective-permute-done.1.w2), channel_id=1, source_target_pairs={{0,32},{1,97},{2,34},{3,99},{4,36},{5,101},{6,38},{7,103},{8,40},{... | collective-permute-start | bytes 2359304 | tf_op jit(solution)/shard_map/ppermute | solution.py:34
  34.4 6.5 %collective-permute-done.w1 = bf16[3072,128]{1,0:T(8,128)(2,1)S(1)} collective-permute-done((bf16[3072,128]{1,0:T(8,128)(2,1)S(1)}, bf16[3072,128]{1,0:T(8,128)(2,1)S(1)}, u32[]{:S(2)}, u32[]{:S(2)}) %collective-permute-start) | collective-permute-done | bytes 786464 | tf_op jit(solution)/shard_map/ppermute | solution.py:34
  40.9 9.9 %forward.2 = (bf16[4,2,128,512]{3,2,1,0:T(8,128)(2,1)S(1)}, bf16[4,2,128,512]{3,2,1,0:T(8,128)(2,1)S(1)}) custom-call(bf16[2048,1024]{1,0:T(8,128)(2,1)} %refs_4_.3, bf16[2048,1024]{1,0:T(8,128)(2,1)} %refs_5_.3, bf16[2048,1024]{1,0:T(8,128)(2,1)} %refs_6_.3, bf16[3072,128]{1,0:T(8,128)(2,1)S(1)} %constant_dynamic-update-slice_fusion.w0, ...), custom_call_target="tpu_custom_call" | custom-call | flops 6442450944 | bytes 16777216 | tf_op jit(solution)/shard_map/forward/pallas_call | solution.py:101
  52.4 1.9 %collective-permute-start.11 = (bf16[3072,128]{1,0:T(8,128)(2,1)S(1)}, bf16[3072,128]{1,0:T(8,128)(2,1)}, u32[]{:S(2)}, u32[]{:S(2)}) collective-permute-start(bf16[3072,128]{1,0:T(8,128)(2,1)S(1)} %collective-permute-done.w1), channel_id=1, source_target_pairs={{0,96},{1,33},{2,98},{3,35},{4,100},{5,37},{6,102},{7,39},{8,104},... | collective-permute-start | bytes 2359304 | tf_op jit(solution)/shard_map/ppermute | solution.py:34
  55.8 11.8 %backward_other.1 = (bf16[3,128,1024]{2,1,0:T(8,128)(2,1)S(1)}, bf16[3,128,1024]{2,1,0:T(8,128)(2,1)}, bf16[3,128,1024]{2,1,0:T(8,128)(2,1)S(1)}, bf16[3,128,1024]{2,1,0:T(8,128)(2,1)S(1)}) custom-call(bf16[4,1024,128]{2,1,0:T(8,128)(2,1)S(1)} %pad_maximum_fusion.refs_0_, bf16[4,1024,128]{2,1,0:T(8,128)(2,1)S(1)} %collective-permute-done.20.refs_1_, ...), custom_call_target="tpu_custom_call" | custom-call | flops 6442450944 | bytes 20971520 | tf_op jit(solution)/shard_map/backward_other/pallas_call | solution.py:152
  68.1 11.3 %backward_own.1 = (bf16[3,128,1024]{2,1,0:T(8,128)(2,1)S(1)}, bf16[3,128,1024]{2,1,0:T(8,128)(2,1)S(1)}, bf16[3,128,1024]{2,1,0:T(8,128)(2,1)S(1)}, bf16[3,128,1024]{2,1,0:T(8,128)(2,1)S(1)}) custom-call(bf16[4,1024,128]{2,1,0:T(8,128)(2,1)S(1)} %pad_maximum_fusion.refs_0_, bf16[4,1024,128]{2,1,0:T(8,128)(2,1)S(1)} %collective-permute-done.20.refs_1_, ...), custom_call_target="tpu_custom_call" | custom-call | flops 6442450944 | bytes 20971520 | tf_op jit(solution)/shard_map/backward_own/pallas_call | solution.py:152
  80.3 1.6 %collective-permute-start.26 = (bf16[3,128,1024]{2,1,0:T(8,128)(2,1)}, bf16[3,128,1024]{2,1,0:T(8,128)(2,1)S(1)}, u32[]{:S(2)}, u32[]{:S(2)}) collective-permute-start(bf16[3,128,1024]{2,1,0:T(8,128)(2,1)} %get-tuple-element.49), channel_id=1, source_target_pairs={{0,96},{1,33},{2,98},{3,35},{4,100},{5,37},{6,102},{7,39},{8,104},... | collective-permute-start | bytes 2359304 | tf_op jit(solution)/shard_map/ppermute | solution.py:34
  85.5 10.3 %forward.3 = (bf16[4,2,128,512]{3,2,1,0:T(8,128)(2,1)S(1)}, bf16[4,2,128,512]{3,2,1,0:T(8,128)(2,1)S(1)}) custom-call(bf16[2048,1024]{1,0:T(8,128)(2,1)} %refs_4_.3, bf16[2048,1024]{1,0:T(8,128)(2,1)} %refs_5_.3, bf16[2048,1024]{1,0:T(8,128)(2,1)} %refs_6_.3, bf16[3072,128]{1,0:T(8,128)(2,1)S(1)} %collective-permute-done.8.w0, ...), custom_call_target="tpu_custom_call" | custom-call | flops 6442450944 | bytes 16777216 | tf_op jit(solution)/shard_map/forward/pallas_call | solution.py:101
  95.9 2.3 %add_convert_fusion.1 = bf16[3,128,1024]{2,1,0:T(8,128)(2,1)} fusion(bf16[3,128,1024]{2,1,0:T(8,128)(2,1)} %collective-permute-done.29, bf16[3,128,1024]{2,1,0:T(8,128)(2,1)S(1)} %get-tuple-element.52), kind=kLoop, calls=%fused_computation.1 | loop fusion | flops 1572864 | bytes 2359296 | tf_op jit(solution)/shard_map/convert_element_type | solution.py:41
  98.3 2.8 %collective-permute-start.30 = (bf16[3,128,1024]{2,1,0:T(8,128)(2,1)}, bf16[3,128,1024]{2,1,0:T(8,128)(2,1)S(1)}, u32[]{:S(2)}, u32[]{:S(2)}) collective-permute-start(bf16[3,128,1024]{2,1,0:T(8,128)(2,1)} %add_convert_fusion.1), channel_id=1, source_target_pairs={{0,96},{1,33},{2,98},{3,35},{4,100},{5,37},{6,102},{7,39},{8,104},... | collective-permute-start | bytes 2359304 | tf_op jit(solution)/shard_map/ppermute | solution.py:34
  101.3 3.1 %collective-permute-start.4 = (bf16[2,128,512]{2,1,0:T(8,128)(2,1)S(1)}, bf16[2,128,512]{2,1,0:T(8,128)(2,1)S(1)}, u32[]{:S(2)}, u32[]{:S(2)}) collective-permute-start(bf16[2,128,512]{2,1,0:T(8,128)(2,1)S(1)} %get-tuple-element.35), channel_id=1, source_target_pairs={{0,12},{1,5},{2,14},{3,7},{4,0},{5,9},{6,2},{7,11},{8,4},{9,13},{1... | collective-permute-start | bytes 786440 | tf_op jit(solution)/shard_map/ppermute | solution.py:34
  104.4 1.8 %collective-permute-start.6 = (bf16[2,128,512]{2,1,0:T(8,128)(2,1)S(1)}, bf16[2,128,512]{2,1,0:T(8,128)(2,1)S(1)}, u32[]{:S(2)}, u32[]{:S(2)}) collective-permute-start(bf16[2,128,512]{2,1,0:T(8,128)(2,1)S(1)} %get-tuple-element.36), channel_id=1, source_target_pairs={{0,4},{1,13},{2,6},{3,15},{4,8},{5,1},{6,10},{7,3},{8,12},{9,5},{1... | collective-permute-start | bytes 786440 | tf_op jit(solution)/shard_map/ppermute | solution.py:34
  107.8 1.6 %collective-permute-start.28 = (bf16[3,128,1024]{2,1,0:T(8,128)(2,1)S(1)}, bf16[3,128,1024]{2,1,0:T(8,128)(2,1)S(1)}, u32[]{:S(2)}, u32[]{:S(2)}) collective-permute-start(bf16[3,128,1024]{2,1,0:T(8,128)(2,1)S(1)} %add_convert_fusion.2), channel_id=1, source_target_pairs={{0,16},{1,17},{2,18},{3,19},{4,20},{5,21},{6,22},{7,23},{8,24},{9,... | collective-permute-start | bytes 2359304 | tf_op jit(solution)/shard_map/ppermute | solution.py:34
  109.6 9.2 %collective-permute-done.30 = bf16[3,128,1024]{2,1,0:T(8,128)(2,1)S(1)} collective-permute-done((bf16[3,128,1024]{2,1,0:T(8,128)(2,1)}, bf16[3,128,1024]{2,1,0:T(8,128)(2,1)S(1)}, u32[]{:S(2)}, u32[]{:S(2)}) %collective-permute-start.30) | collective-permute-done | bytes 786464 | tf_op jit(solution)/shard_map/ppermute | solution.py:34
  118.8 2.8 %collective-permute-start.13 = (bf16[2,128,512]{2,1,0:T(8,128)(2,1)S(1)}, bf16[2,128,512]{2,1,0:T(8,128)(2,1)S(1)}, u32[]{:S(2)}, u32[]{:S(2)}) collective-permute-start(bf16[2,128,512]{2,1,0:T(8,128)(2,1)S(1)} %get-tuple-element.43), channel_id=1, source_target_pairs={{0,12},{1,5},{2,14},{3,7},{4,0},{5,9},{6,2},{7,11},{8,4},{9,13},{1... | collective-permute-start | bytes 786440 | tf_op jit(solution)/shard_map/ppermute | solution.py:34
  122.0 3.7 %collective-permute-start.31 = (bf16[3,128,1024]{2,1,0:T(8,128)(2,1)S(1)}, bf16[3,128,1024]{2,1,0:T(8,128)(2,1)S(1)}, u32[]{:S(2)}, u32[]{:S(2)}) collective-permute-start(bf16[3,128,1024]{2,1,0:T(8,128)(2,1)S(1)} %add_convert_fusion), channel_id=1, source_target_pairs={{0,96},{1,33},{2,98},{3,35},{4,100},{5,37},{6,102},{7,39},{8,104},... | collective-permute-start | bytes 2359304 | tf_op jit(solution)/shard_map/ppermute | solution.py:34
  125.7 3.6 %collective-permute-start.5 = (bf16[2,128,512]{2,1,0:T(8,128)(2,1)S(1)}, bf16[2,128,512]{2,1,0:T(8,128)(2,1)S(1)}, u32[]{:S(2)}, u32[]{:S(2)}) collective-permute-start(bf16[2,128,512]{2,1,0:T(8,128)(2,1)S(1)} %add_convert_fusion.4), channel_id=1, source_target_pairs={{0,12},{1,5},{2,14},{3,7},{4,0},{5,9},{6,2},{7,11},{8,4},{9,13},{1... | collective-permute-start | bytes 786440 | tf_op jit(solution)/shard_map/ppermute | solution.py:34
  130.3 3.0 %collective-permute-done.5.b = bf16[2,128,512]{2,1,0:T(8,128)(2,1)S(1)} collective-permute-done((bf16[2,128,512]{2,1,0:T(8,128)(2,1)S(1)}, bf16[2,128,512]{2,1,0:T(8,128)(2,1)S(1)}, u32[]{:S(2)}, u32[]{:S(2)}) %collective-permute-start.5) | collective-permute-done | bytes 262176 | tf_op jit(solution)/shard_map/ppermute | solution.py:34
  133.3 3.6 %collective-permute-start.14 = (bf16[2,128,512]{2,1,0:T(8,128)(2,1)S(1)}, bf16[2,128,512]{2,1,0:T(8,128)(2,1)S(1)}, u32[]{:S(2)}, u32[]{:S(2)}) collective-permute-start(bf16[2,128,512]{2,1,0:T(8,128)(2,1)S(1)} %add_convert_fusion.3), channel_id=1, source_target_pairs={{0,12},{1,5},{2,14},{3,7},{4,0},{5,9},{6,2},{7,11},{8,4},{9,13},{1... | collective-permute-start | bytes 786440 | tf_op jit(solution)/shard_map/ppermute | solution.py:34
  137.1 3.0 %collective-permute-start.7 = (bf16[128,512]{1,0:T(8,128)(2,1)S(1)}, bf16[128,512]{1,0:T(8,128)(2,1)S(1)}, u32[]{:S(2)}, u32[]{:S(2)}) collective-permute-start(bf16[128,512]{1,0:T(8,128)(2,1)S(1)} %get-tuple-element.38), channel_id=1, source_target_pairs={{0,2},{1,3},{2,0},{3,1},{4,6},{5,7},{6,4},{7,5},{8,10},{9,11},{10,... | collective-permute-start | bytes 393224 | tf_op jit(solution)/shard_map/ppermute | solution.py:34
  140.9 3.1 %collective-permute-start.16 = (bf16[128,512]{1,0:T(8,128)(2,1)S(1)}, bf16[128,512]{1,0:T(8,128)(2,1)S(1)}, u32[]{:S(2)}, u32[]{:S(2)}) collective-permute-start(bf16[128,512]{1,0:T(8,128)(2,1)S(1)} %get-tuple-element.46), channel_id=1, source_target_pairs={{0,2},{1,3},{2,0},{3,1},{4,6},{5,7},{6,4},{7,5},{8,10},{9,11},{10,... | collective-permute-start | bytes 393224 | tf_op jit(solution)/shard_map/ppermute | solution.py:34
  144.0 3.4 %collective-permute-done.16.b1 = bf16[128,512]{1,0:T(8,128)(2,1)S(1)} collective-permute-done((bf16[128,512]{1,0:T(8,128)(2,1)S(1)}, bf16[128,512]{1,0:T(8,128)(2,1)S(1)}, u32[]{:S(2)}, u32[]{:S(2)}) %collective-permute-start.16) | collective-permute-done | bytes 131104 | tf_op jit(solution)/shard_map/ppermute | solution.py:34
  (71 shorter events, 22.3 us)
Async XLA Ops:
  2.4 9.5 %collective-permute-start.19 = (bf16[1024,128]{1,0:T(8,128)(2,1)S(1)}, bf16[1024,128]{1,0:T(8,128)(2,1)S(1)}, u32[]{:S(2)}, u32[]{:S(2)}) collective-permute-start(bf16[1024,128]{1,0:T(8,128)(2,1)S(1)} %masked.1), channel_id=1, source_target_pairs={{0,2},{1,3},{2,0},{3,1},{4,6},{5,7},{6,4},{7,5},{8,10},{9,11},{10,... | collective-permute-start | bytes 786440 | tf_op jit(solution)/shard_map/ppermute | solution.py:34
  5.6 13.3 %collective-permute-start.17 = (bf16[1024,128]{1,0:T(8,128)(2,1)S(1)}, bf16[1024,128]{1,0:T(8,128)(2,1)S(1)}, u32[]{:S(2)}, u32[]{:S(2)}) collective-permute-start(bf16[1024,128]{1,0:T(8,128)(2,1)S(1)} %masked.1), channel_id=1, source_target_pairs={{0,4},{1,13},{2,6},{3,15},{4,8},{5,1},{6,10},{7,3},{8,12},{9,5},{1... | collective-permute-start | bytes 786440 | tf_op jit(solution)/shard_map/ppermute | solution.py:34
  7.5 14.5 %collective-permute-start.18 = (bf16[1024,128]{1,0:T(8,128)(2,1)S(1)}, bf16[1024,128]{1,0:T(8,128)(2,1)S(1)}, u32[]{:S(2)}, u32[]{:S(2)}) collective-permute-start(bf16[1024,128]{1,0:T(8,128)(2,1)S(1)} %masked.1), channel_id=1, source_target_pairs={{0,12},{1,5},{2,14},{3,7},{4,0},{5,9},{6,2},{7,11},{8,4},{9,13},{1... | collective-permute-start | bytes 786440 | tf_op jit(solution)/shard_map/ppermute | solution.py:34
  11.9 9.3 %collective-permute-start.22 = (bf16[1024,128]{1,0:T(8,128)(2,1)S(1)}, bf16[1024,128]{1,0:T(8,128)(2,1)S(1)}, u32[]{:S(2)}, u32[]{:S(2)}) collective-permute-start(bf16[1024,128]{1,0:T(8,128)(2,1)S(1)} %collective-permute-done.19), channel_id=1, source_target_pairs={{0,4},{1,13},{2,6},{3,15},{4,8},{5,1},{6,10},{7,3},{8,12},{9,5},{1... | collective-permute-start | bytes 786440 | tf_op jit(solution)/shard_map/ppermute | solution.py:34
  15.0 8.5 %collective-permute-start.23 = (bf16[1024,128]{1,0:T(8,128)(2,1)S(1)}, bf16[1024,128]{1,0:T(8,128)(2,1)S(1)}, u32[]{:S(2)}, u32[]{:S(2)}) collective-permute-start(bf16[1024,128]{1,0:T(8,128)(2,1)S(1)} %collective-permute-done.19), channel_id=1, source_target_pairs={{0,12},{1,5},{2,14},{3,7},{4,0},{5,9},{6,2},{7,11},{8,4},{9,13},{1... | collective-permute-start | bytes 786440 | tf_op jit(solution)/shard_map/ppermute | solution.py:34
  17.2 15.5 %collective-permute-start.1 = (bf16[3072,128]{1,0:T(8,128)(2,1)S(1)}, bf16[3072,128]{1,0:T(8,128)(2,1)S(1)}, u32[]{:S(2)}, u32[]{:S(2)}) collective-permute-start(bf16[3072,128]{1,0:T(8,128)(2,1)S(1)} %constant_dynamic-update-slice_fusion.w0), channel_id=1, source_target_pairs={{0,32},{1,97},{2,34},{3,99},{4,36},{5,101},{6,38},{7,103},{8,40},{... | collective-permute-start | bytes 2359304 | tf_op jit(solution)/shard_map/ppermute | solution.py:34
  18.9 8.2 %collective-permute-start.21 = (bf16[1024,128]{1,0:T(8,128)(2,1)S(1)}, bf16[1024,128]{1,0:T(8,128)(2,1)S(1)}, u32[]{:S(2)}, u32[]{:S(2)}) collective-permute-start(bf16[1024,128]{1,0:T(8,128)(2,1)S(1)} %collective-permute-done.17), channel_id=1, source_target_pairs={{0,4},{1,13},{2,6},{3,15},{4,8},{5,1},{6,10},{7,3},{8,12},{9,5},{1... | collective-permute-start | bytes 786440 | tf_op jit(solution)/shard_map/ppermute | solution.py:34
  21.2 8.1 %collective-permute-start.24 = (bf16[1024,128]{1,0:T(8,128)(2,1)S(1)}, bf16[1024,128]{1,0:T(8,128)(2,1)S(1)}, u32[]{:S(2)}, u32[]{:S(2)}) collective-permute-start(bf16[1024,128]{1,0:T(8,128)(2,1)S(1)} %collective-permute-done.22), channel_id=1, source_target_pairs={{0,4},{1,13},{2,6},{3,15},{4,8},{5,1},{6,10},{7,3},{8,12},{9,5},{1... | collective-permute-start | bytes 786440 | tf_op jit(solution)/shard_map/ppermute | solution.py:34
  22.0 18.9 %collective-permute-start = (bf16[3072,128]{1,0:T(8,128)(2,1)S(1)}, bf16[3072,128]{1,0:T(8,128)(2,1)S(1)}, u32[]{:S(2)}, u32[]{:S(2)}) collective-permute-start(bf16[3072,128]{1,0:T(8,128)(2,1)S(1)} %constant_dynamic-update-slice_fusion.w0), channel_id=1, source_target_pairs={{0,16},{1,17},{2,18},{3,19},{4,20},{5,21},{6,22},{7,23},{8,24},{9,... | collective-permute-start | bytes 2359304 | tf_op jit(solution)/shard_map/ppermute | solution.py:34
  23.5 17.4 %collective-permute-start.2 = (bf16[3072,128]{1,0:T(8,128)(2,1)S(1)}, bf16[3072,128]{1,0:T(8,128)(2,1)S(1)}, u32[]{:S(2)}, u32[]{:S(2)}) collective-permute-start(bf16[3072,128]{1,0:T(8,128)(2,1)S(1)} %constant_dynamic-update-slice_fusion.w0), channel_id=1, source_target_pairs={{0,96},{1,33},{2,98},{3,35},{4,100},{5,37},{6,102},{7,39},{8,104},... | collective-permute-start | bytes 2359304 | tf_op jit(solution)/shard_map/ppermute | solution.py:34
  27.1 25.4 %collective-permute-start.20 = (bf16[4,1024,128]{2,1,0:T(8,128)(2,1)S(1)}, bf16[4,1024,128]{2,1,0:T(8,128)(2,1)S(1)}, u32[]{:S(2)}, u32[]{:S(2)}) collective-permute-start(bf16[4,1024,128]{2,1,0:T(8,128)(2,1)S(1)} %pad_maximum_fusion.refs_0_), channel_id=1, source_target_pairs={{0,1},{1,0},{2,3},{3,2},{4,5},{5,4},{6,7},{7,6},{8,9},{9,8},{10,11... | collective-permute-start | bytes 3145736 | tf_op jit(solution)/shard_map/ppermute | solution.py:34
  29.4 26.4 %collective-permute-start.25 = (bf16[4,1024,128]{2,1,0:T(8,128)(2,1)S(1)}, bf16[4,1024,128]{2,1,0:T(8,128)(2,1)}, u32[]{:S(2)}, u32[]{:S(2)}) collective-permute-start(bf16[4,1024,128]{2,1,0:T(8,128)(2,1)S(1)} %pad_maximum_fusion.1.refs_2_), channel_id=1, source_target_pairs={{0,1},{1,0},{2,3},{3,2},{4,5},{5,4},{6,7},{7,6},{8,9},{9,8},{10,11... | collective-permute-start | bytes 3145736 | tf_op jit(solution)/shard_map/ppermute | solution.py:34
  32.7 21.6 %collective-permute-start.8 = (bf16[3072,128]{1,0:T(8,128)(2,1)S(1)}, bf16[3072,128]{1,0:T(8,128)(2,1)S(1)}, u32[]{:S(2)}, u32[]{:S(2)}) collective-permute-start(bf16[3072,128]{1,0:T(8,128)(2,1)S(1)} %collective-permute-done.1.w2), channel_id=1, source_target_pairs={{0,32},{1,97},{2,34},{3,99},{4,36},{5,101},{6,38},{7,103},{8,40},{... | collective-permute-start | bytes 2359304 | tf_op jit(solution)/shard_map/ppermute | solution.py:34
  50.9 50.1 %collective-permute-start.3 = (bf16[4,2,128,512]{3,2,1,0:T(8,128)(2,1)S(1)}, bf16[4,2,128,512]{3,2,1,0:T(8,128)(2,1)S(1)}, u32[]{:S(2)}, u32[]{:S(2)}) collective-permute-start(bf16[4,2,128,512]{3,2,1,0:T(8,128)(2,1)S(1)} %get-tuple-element.32), channel_id=1, source_target_pairs={{0,1},{1,0},{2,3},{3,2},{4,5},{5,4},{6,7},{7,6},{8,9},{9,8},{10,11... | collective-permute-start | bytes 3145736 | tf_op jit(solution)/shard_map/ppermute | solution.py:34
  51.0 28.4 %collective-permute-start.10 = (bf16[3072,128]{1,0:T(8,128)(2,1)S(1)}, bf16[3072,128]{1,0:T(8,128)(2,1)S(1)}, u32[]{:S(2)}, u32[]{:S(2)}) collective-permute-start(bf16[3072,128]{1,0:T(8,128)(2,1)S(1)} %collective-permute-done.w1), channel_id=1, source_target_pairs={{0,32},{1,97},{2,34},{3,99},{4,36},{5,101},{6,38},{7,103},{8,40},{... | collective-permute-start | bytes 2359304 | tf_op jit(solution)/shard_map/ppermute | solution.py:34
  52.4 29.5 %collective-permute-start.11 = (bf16[3072,128]{1,0:T(8,128)(2,1)S(1)}, bf16[3072,128]{1,0:T(8,128)(2,1)}, u32[]{:S(2)}, u32[]{:S(2)}) collective-permute-start(bf16[3072,128]{1,0:T(8,128)(2,1)S(1)} %collective-permute-done.w1), channel_id=1, source_target_pairs={{0,96},{1,33},{2,98},{3,35},{4,100},{5,37},{6,102},{7,39},{8,104},... | collective-permute-start | bytes 2359304 | tf_op jit(solution)/shard_map/ppermute | solution.py:34
  54.3 28.0 %collective-permute-start.9 = (bf16[3072,128]{1,0:T(8,128)(2,1)S(1)}, bf16[3072,128]{1,0:T(8,128)(2,1)S(1)}, u32[]{:S(2)}, u32[]{:S(2)}) collective-permute-start(bf16[3072,128]{1,0:T(8,128)(2,1)S(1)} %collective-permute-done.8.w0), channel_id=1, source_target_pairs={{0,16},{1,17},{2,18},{3,19},{4,20},{5,21},{6,22},{7,23},{8,24},{9,... | collective-permute-start | bytes 2359304 | tf_op jit(solution)/shard_map/ppermute | solution.py:34
  67.6 28.3 %collective-permute-start.29 = (bf16[3,128,1024]{2,1,0:T(8,128)(2,1)S(1)}, bf16[3,128,1024]{2,1,0:T(8,128)(2,1)}, u32[]{:S(2)}, u32[]{:S(2)}) collective-permute-start(bf16[3,128,1024]{2,1,0:T(8,128)(2,1)S(1)} %get-tuple-element.53), channel_id=1, source_target_pairs={{0,16},{1,17},{2,18},{3,19},{4,20},{5,21},{6,22},{7,23},{8,24},{9,... | collective-permute-start | bytes 2359304 | tf_op jit(solution)/shard_map/ppermute | solution.py:34
  80.3 21.0 %collective-permute-start.26 = (bf16[3,128,1024]{2,1,0:T(8,128)(2,1)}, bf16[3,128,1024]{2,1,0:T(8,128)(2,1)S(1)}, u32[]{:S(2)}, u32[]{:S(2)}) collective-permute-start(bf16[3,128,1024]{2,1,0:T(8,128)(2,1)} %get-tuple-element.49), channel_id=1, source_target_pairs={{0,96},{1,33},{2,98},{3,35},{4,100},{5,37},{6,102},{7,39},{8,104},... | collective-permute-start | bytes 2359304 | tf_op jit(solution)/shard_map/ppermute | solution.py:34
  81.9 22.5 %collective-permute-start.27 = (bf16[3,128,1024]{2,1,0:T(8,128)(2,1)S(1)}, bf16[3,128,1024]{2,1,0:T(8,128)(2,1)}, u32[]{:S(2)}, u32[]{:S(2)}) collective-permute-start(bf16[3,128,1024]{2,1,0:T(8,128)(2,1)S(1)} %get-tuple-element.50), channel_id=1, source_target_pairs={{0,32},{1,97},{2,34},{3,99},{4,36},{5,101},{6,38},{7,103},{8,40},{... | collective-permute-start | bytes 2359304 | tf_op jit(solution)/shard_map/ppermute | solution.py:34
  95.8 12.0 %collective-permute-start.12 = (bf16[4,2,128,512]{3,2,1,0:T(8,128)(2,1)S(1)}, bf16[4,2,128,512]{3,2,1,0:T(8,128)(2,1)S(1)}, u32[]{:S(2)}, u32[]{:S(2)}) collective-permute-start(bf16[4,2,128,512]{3,2,1,0:T(8,128)(2,1)S(1)} %get-tuple-element.40), channel_id=1, source_target_pairs={{0,1},{1,0},{2,3},{3,2},{4,5},{5,4},{6,7},{7,6},{8,9},{9,8},{10,11... | collective-permute-start | bytes 3145736 | tf_op jit(solution)/shard_map/ppermute | solution.py:34
  98.3 20.5 %collective-permute-start.30 = (bf16[3,128,1024]{2,1,0:T(8,128)(2,1)}, bf16[3,128,1024]{2,1,0:T(8,128)(2,1)S(1)}, u32[]{:S(2)}, u32[]{:S(2)}) collective-permute-start(bf16[3,128,1024]{2,1,0:T(8,128)(2,1)} %add_convert_fusion.1), channel_id=1, source_target_pairs={{0,96},{1,33},{2,98},{3,35},{4,100},{5,37},{6,102},{7,39},{8,104},... | collective-permute-start | bytes 2359304 | tf_op jit(solution)/shard_map/ppermute | solution.py:34
  101.0 47.2 %collective-permute-start.32 = (bf16[3,128,1024]{2,1,0:T(8,128)(2,1)S(1)}, bf16[3,128,1024]{2,1,0:T(8,128)(2,1)S(1)}, u32[]{:S(2)}, u32[]{:S(2)}) collective-permute-start(bf16[3,128,1024]{2,1,0:T(8,128)(2,1)S(1)} %get-tuple-element.54), channel_id=1, source_target_pairs={{0,32},{1,97},{2,34},{3,99},{4,36},{5,101},{6,38},{7,103},{8,40},{... | collective-permute-start | bytes 2359304 | tf_op jit(solution)/shard_map/ppermute | solution.py:34
  101.3 20.6 %collective-permute-start.4 = (bf16[2,128,512]{2,1,0:T(8,128)(2,1)S(1)}, bf16[2,128,512]{2,1,0:T(8,128)(2,1)S(1)}, u32[]{:S(2)}, u32[]{:S(2)}) collective-permute-start(bf16[2,128,512]{2,1,0:T(8,128)(2,1)S(1)} %get-tuple-element.35), channel_id=1, source_target_pairs={{0,12},{1,5},{2,14},{3,7},{4,0},{5,9},{6,2},{7,11},{8,4},{9,13},{1... | collective-permute-start | bytes 786440 | tf_op jit(solution)/shard_map/ppermute | solution.py:34
  104.4 21.3 %collective-permute-start.6 = (bf16[2,128,512]{2,1,0:T(8,128)(2,1)S(1)}, bf16[2,128,512]{2,1,0:T(8,128)(2,1)S(1)}, u32[]{:S(2)}, u32[]{:S(2)}) collective-permute-start(bf16[2,128,512]{2,1,0:T(8,128)(2,1)S(1)} %get-tuple-element.36), channel_id=1, source_target_pairs={{0,4},{1,13},{2,6},{3,15},{4,8},{5,1},{6,10},{7,3},{8,12},{9,5},{1... | collective-permute-start | bytes 786440 | tf_op jit(solution)/shard_map/ppermute | solution.py:34
  107.8 40.5 %collective-permute-start.28 = (bf16[3,128,1024]{2,1,0:T(8,128)(2,1)S(1)}, bf16[3,128,1024]{2,1,0:T(8,128)(2,1)S(1)}, u32[]{:S(2)}, u32[]{:S(2)}) collective-permute-start(bf16[3,128,1024]{2,1,0:T(8,128)(2,1)S(1)} %add_convert_fusion.2), channel_id=1, source_target_pairs={{0,16},{1,17},{2,18},{3,19},{4,20},{5,21},{6,22},{7,23},{8,24},{9,... | collective-permute-start | bytes 2359304 | tf_op jit(solution)/shard_map/ppermute | solution.py:34
  118.8 10.5 %collective-permute-start.13 = (bf16[2,128,512]{2,1,0:T(8,128)(2,1)S(1)}, bf16[2,128,512]{2,1,0:T(8,128)(2,1)S(1)}, u32[]{:S(2)}, u32[]{:S(2)}) collective-permute-start(bf16[2,128,512]{2,1,0:T(8,128)(2,1)S(1)} %get-tuple-element.43), channel_id=1, source_target_pairs={{0,12},{1,5},{2,14},{3,7},{4,0},{5,9},{6,2},{7,11},{8,4},{9,13},{1... | collective-permute-start | bytes 786440 | tf_op jit(solution)/shard_map/ppermute | solution.py:34
  122.0 26.3 %collective-permute-start.31 = (bf16[3,128,1024]{2,1,0:T(8,128)(2,1)S(1)}, bf16[3,128,1024]{2,1,0:T(8,128)(2,1)S(1)}, u32[]{:S(2)}, u32[]{:S(2)}) collective-permute-start(bf16[3,128,1024]{2,1,0:T(8,128)(2,1)S(1)} %add_convert_fusion), channel_id=1, source_target_pairs={{0,96},{1,33},{2,98},{3,35},{4,100},{5,37},{6,102},{7,39},{8,104},... | collective-permute-start | bytes 2359304 | tf_op jit(solution)/shard_map/ppermute | solution.py:34
  125.7 7.6 %collective-permute-start.5 = (bf16[2,128,512]{2,1,0:T(8,128)(2,1)S(1)}, bf16[2,128,512]{2,1,0:T(8,128)(2,1)S(1)}, u32[]{:S(2)}, u32[]{:S(2)}) collective-permute-start(bf16[2,128,512]{2,1,0:T(8,128)(2,1)S(1)} %add_convert_fusion.4), channel_id=1, source_target_pairs={{0,12},{1,5},{2,14},{3,7},{4,0},{5,9},{6,2},{7,11},{8,4},{9,13},{1... | collective-permute-start | bytes 786440 | tf_op jit(solution)/shard_map/ppermute | solution.py:34
  129.3 7.8 %collective-permute-start.15 = (bf16[2,128,512]{2,1,0:T(8,128)(2,1)S(1)}, bf16[2,128,512]{2,1,0:T(8,128)(2,1)S(1)}, u32[]{:S(2)}, u32[]{:S(2)}) collective-permute-start(bf16[2,128,512]{2,1,0:T(8,128)(2,1)S(1)} %get-tuple-element.44), channel_id=1, source_target_pairs={{0,4},{1,13},{2,6},{3,15},{4,8},{5,1},{6,10},{7,3},{8,12},{9,5},{1... | collective-permute-start | bytes 786440 | tf_op jit(solution)/shard_map/ppermute | solution.py:34
  133.3 7.5 %collective-permute-start.14 = (bf16[2,128,512]{2,1,0:T(8,128)(2,1)S(1)}, bf16[2,128,512]{2,1,0:T(8,128)(2,1)S(1)}, u32[]{:S(2)}, u32[]{:S(2)}) collective-permute-start(bf16[2,128,512]{2,1,0:T(8,128)(2,1)S(1)} %add_convert_fusion.3), channel_id=1, source_target_pairs={{0,12},{1,5},{2,14},{3,7},{4,0},{5,9},{6,2},{7,11},{8,4},{9,13},{1... | collective-permute-start | bytes 786440 | tf_op jit(solution)/shard_map/ppermute | solution.py:34
  137.1 6.9 %collective-permute-start.7 = (bf16[128,512]{1,0:T(8,128)(2,1)S(1)}, bf16[128,512]{1,0:T(8,128)(2,1)S(1)}, u32[]{:S(2)}, u32[]{:S(2)}) collective-permute-start(bf16[128,512]{1,0:T(8,128)(2,1)S(1)} %get-tuple-element.38), channel_id=1, source_target_pairs={{0,2},{1,3},{2,0},{3,1},{4,6},{5,7},{6,4},{7,5},{8,10},{9,11},{10,... | collective-permute-start | bytes 393224 | tf_op jit(solution)/shard_map/ppermute | solution.py:34
  (9 other events, 48.6 us)

commit v2 on v1

v2 whole, which is shorter than its diff:
```python
import jax
import jax.numpy as jnp
from jax import lax
from jax.experimental import pallas as pl
from jax.experimental.pallas import tpu as pltpu
from jax.sharding import PartitionSpec as P

BF = jnp.bfloat16
F32 = jnp.float32
MIB = 1024 * 1024
LOAD_MIB = 38
GRP, TP = 8, 16
CHEAP = 1000
FULL = ("grp", "tp")


def full_perm(move):
    pairs = []
    for g in range(GRP):
        for t in range(TP):
            y, xl, z, xh, c = move(g // 2, g % 2, t // 4, t // 2 % 2, t % 2)
            pairs.append((g * TP + t, (y % 4 * 2 + xl % 2) * TP + z % 4 * 4 + xh % 2 * 2 + c % 2))
    return pairs


Y1 = full_perm(lambda y, xl, z, xh, c: (y + 1 - 2 * c, xl, z, xh, c))
Y2 = full_perm(lambda y, xl, z, xh, c: (y - 1 + 2 * c, xl, z, xh, c))
Z1 = full_perm(lambda y, xl, z, xh, c: (y, xl, z + 1 - 2 * c, xh, c))
Z2 = full_perm(lambda y, xl, z, xh, c: (y, xl, z - 1 + 2 * c, xh, c))
XL = full_perm(lambda y, xl, z, xh, c: (y, xl + 1, z, xh, c))
XH = full_perm(lambda y, xl, z, xh, c: (y, xl, z, xh + 1, c))
CORE = full_perm(lambda y, xl, z, xh, c: (y, xl, z, xh, c + 1))


def send(array, pairs):
    return lax.ppermute(array, FULL, pairs)


def add(*arrays):
    total = arrays[0].astype(F32)
    for array in arrays[1:]:
        total = total + array.astype(F32)
    return total.astype(BF)


def place():
    g = lax.axis_index("grp")
    t = lax.axis_index("tp")
    c = t % 2
    return g // 2, g % 2, t // 4, t // 2 % 2, c, 1 - 2 * c


def params(mib=8):
    return pltpu.CompilerParams(vmem_limit_bytes=mib * MIB)


def cost(flops, bytes_accessed):
    return pl.CostEstimate(flops=flops // CHEAP, bytes_accessed=bytes_accessed // CHEAP, transcendentals=0)


def fence(*arrays):
    return lax.optimization_barrier(arrays)


VMEM = pl.BlockSpec(memory_space=pltpu.VMEM)


def collect_kernel(w0, w1, w2, w_ref, sems):
    depth = w0.shape[0]
    moves = []
    for i, w in enumerate((w0, w1, w2)):
        moves.append(pltpu.make_async_copy(w, w_ref.at[pl.ds(i * depth, depth), :], sems.at[i]))
    for move in moves:
        move.start()
    for move in moves:
        move.wait()


def collect(weights):
    depth, width = weights[0].shape
    return pl.pallas_call(
        collect_kernel,
        in_specs=[pl.BlockSpec(memory_space=pl.ANY)] * 3,
        out_specs=VMEM,
        out_shape=jax.ShapeDtypeStruct((3 * depth, width), BF),
        scratch_shapes=[pltpu.SemaphoreType.DMA((3,))],
        compiler_params=params(60),
        cost_estimate=cost(0, 12 * depth * width),
        name="collect",
    )(*weights)


def mask_kernel(grad_ref, mask_ref, turned_ref, grad, mask, sems):
    moves = [
        pltpu.make_async_copy(mask_ref, mask, sems.at[0]),
        pltpu.make_async_copy(grad_ref, grad, sems.at[1]),
    ]
    for move in moves:
        move.start()
    for move in moves:
        move.wait()
    turned_ref[...] = (grad[...].astype(F32).T * mask[...].astype(F32)).astype(BF)


def masked_turned(kv_grad, loss_mask):
    rows, cols = kv_grad.shape
    return pl.pallas_call(
        mask_kernel,
        in_specs=[pl.BlockSpec(memory_space=pl.ANY)] * 2,
        out_specs=VMEM,
        out_shape=jax.ShapeDtypeStruct((cols, rows), BF),
        scratch_shapes=[
            pltpu.VMEM((rows, cols), BF),
            pltpu.VMEM((1, rows), jnp.int32),
            pltpu.SemaphoreType.DMA((2,)),
        ],
        compiler_params=params(60),
        cost_estimate=cost(rows * cols, 4 * rows * cols),
        name="masked",
    )(kv_grad, loss_mask.reshape(1, rows))


def load_kernel(*refs):
    half = len(refs) // 2
    sems = refs[-1]
    moves = [pltpu.make_async_copy(refs[i], refs[half + i], sems.at[i]) for i in range(half)]
    for move in moves:
        move.start()
    for move in moves:
        move.wait()


def load(*arrays):
    count = len(arrays)
    return pl.pallas_call(
        load_kernel,
        in_specs=[pl.BlockSpec(memory_space=pl.ANY)] * count,
        out_specs=[VMEM] * count,
        out_shape=[jax.ShapeDtypeStruct(a.shape, BF) for a in arrays],
        scratch_shapes=[pltpu.SemaphoreType.DMA((count,))],
        compiler_params=params(LOAD_MIB),
        cost_estimate=cost(0, 4 * sum(a.size for a in arrays)),
        name="load",
    )(*arrays)


def forward_kernel(swap, s0, s1, s2, wa, wb, mine_ref, theirs_ref, w_all):
    c = lax.axis_index("tp") % 2
    for i, w in ((c, wa), (1 - c, wb)) if swap else ((0, wa), (1, wb)):
        w_all[:, pl.ds(pl.multiple_of(i * 128, 128), 128)] = w[...]
    depth = s0.shape[1]
    total = jnp.dot(s0[...], w_all[0:depth, :], preferred_element_type=F32)
    total += jnp.dot(s1[...], w_all[depth:2 * depth, :], preferred_element_type=F32)
    total += jnp.dot(s2[...], w_all[2 * depth:3 * depth, :], preferred_element_type=F32)
    total = total.astype(BF)
    for z in range(4):
        for h in range(2):
            at = (z * 2 + h) * 256
            first = total[at:at + 128]
            second = total[at + 128:at + 256]
            mine_ref[z, h] = jnp.where(c == 0, first, second)
            theirs_ref[z, h] = jnp.where(c == 0, second, first)


def forward(states, blocks, swap):
    tokens, depth = states[0].shape
    out = jax.ShapeDtypeStruct((4, 2, 128, 256), BF)

    def kernel(*refs):
        forward_kernel(swap, *refs)

    return pl.pallas_call(
        kernel,
        in_specs=[VMEM] * 5,
        out_specs=[VMEM] * 2,
        out_shape=[out, out],
        scratch_shapes=[pltpu.VMEM((3 * depth, 256), BF)],
        compiler_params=params(16),
        cost_estimate=cost(6 * tokens * depth * 256, 6 * tokens * depth + 8 * depth * 256),
        name="forward",
    )(*states, *blocks)


def backward_kernel(other, refs):
    mine, theirs, (s0, s1, s2) = refs[:4], refs[4:8], refs[8:11]
    p2, pm, pp, p0, turned = refs[11:]
    y, xl, z, xh, c, d = place()
    half = (xl + 1) % 2 if other else xl
    for pairs, core in ((mine, c), (theirs, 1 - c)):
        way = 1 - 2 * core
        for ref, zz in zip(pairs, (z, z - way, z + way, z + 2)):
            for j in range(2):
                token = (zz + 4) % 4 * 4 + (xh + j) % 2 * 2 + core
                lanes = pl.ds(pl.multiple_of(token * 128, 128), 128)
                for r, yy in enumerate((y + 2, y - d, y + d, y)):
                    rows = pl.ds(pl.multiple_of(((yy + 4) % 4 * 2 + half) * 128, 128), 128)
                    turned[r * 128:(r + 1) * 128, lanes] = ref[j, rows, :]

    @pl.loop(0, s0.shape[1] // 512)
    def _(i):
        cols = pl.ds(pl.multiple_of(i * 512, 512), 512)
        for s, state in enumerate((s0, s1, s2)):
            product = jnp.dot(turned[...], state[:, cols], preferred_element_type=F32) * (16384 ** -0.5)
            product = product.astype(BF)
            for r, out in enumerate((p2, pm, pp, p0)):
                out[s, :, cols] = product[r * 128:(r + 1) * 128]


def backward(states, masked, other):
    tokens, depth = states[0].shape
    out = jax.ShapeDtypeStruct((3, 128, depth), BF)

    def kernel(*refs):
        backward_kernel(other, refs)

    return pl.pallas_call(
        kernel,
        in_specs=[VMEM] * 11,
        out_specs=[VMEM] * 4,
        out_shape=[out] * 4,
        scratch_shapes=[pltpu.VMEM((512, tokens), BF)],
        compiler_params=params(16),
        cost_estimate=cost(6 * tokens * depth * 512, 6 * tokens * depth + 16 * tokens * 256),
        name="backward_other" if other else "backward_own",
    )(*masked, *states)


def pick_kernel(*refs):
    _, _, z, _, _, d = place()
    count = (len(refs) - 4) // 2
    for out, zz in zip(refs[2 * count:], (z + 2, z - d, z + d, z)):
        k = (zz + 4) % 4
        for i in range(count):
            total = refs[i][k].astype(F32) + refs[count + i][k].astype(F32)
            out[:, :, i * 256:(i + 1) * 256] = total.astype(BF)


def pick(mine, theirs):
    size = sum(a.size for a in mine)
    out = jax.ShapeDtypeStruct((2, 128, 256 * len(mine)), BF)
    return pl.pallas_call(
        pick_kernel,
        out_shape=[out] * 4,
        compiler_params=params(),
        cost_estimate=cost(size, 6 * size),
        name="pick",
    )(*mine, *theirs)


def split_kernel(a0, a1, b, c0, c1, mine, theirs):
    h = lax.axis_index("tp") // 2 % 2
    for out, k in ((mine, h), (theirs, (h + 1) % 2)):
        for i, (a, c) in enumerate(((a0, c0), (a1, c1))):
            total = a[k].astype(F32) + b[i, k].astype(F32) + c[k].astype(F32)
            out[:, i * 512:(i + 1) * 512] = total.astype(BF)


def split(a0, a1, b, c0, c1):
    out = jax.ShapeDtypeStruct((128, 1024), BF)
    return pl.pallas_call(
        split_kernel,
        out_shape=[out] * 2,
        compiler_params=params(),
        cost_estimate=cost(2 * b.size, 8 * b.size),
        name="split",
    )(a0, a1, b, c0, c1)


def pass_kernel(qa, ta, qb, tb, out):
    for i, (q, t) in enumerate(((qa, ta), (qb, tb))):
        out[i] = (q[...].astype(F32) + t[...].astype(F32)).astype(BF)


def pass_on(qa, ta, qb, tb):
    return pl.pallas_call(
        pass_kernel,
        out_shape=jax.ShapeDtypeStruct((2, *qa.shape), BF),
        compiler_params=params(),
        cost_estimate=cost(2 * qa.size, 12 * qa.size),
        name="pass_on",
    )(qa, ta, qb, tb)


def join_kernel(a, b, out):
    y, xl, _, _, _, _ = place()
    spots = (
        (y - 1, xl), (y + 1, xl), (y, xl), (y, xl + 1),
        (y + 2, xl), (y + 2, xl + 1), (y - 1, xl + 1), (y + 1, xl + 1),
    )
    for j, (yy, hh) in enumerate(spots):
        lanes = pl.ds(pl.multiple_of(((yy + 4) % 4 * 2 + hh % 2) * 128, 128), 128)
        cut = slice(j * 128, (j + 1) * 128)
        out[:, lanes] = (a[:, cut].astype(F32) + b[:, cut].astype(F32)).astype(BF)


def join(a, b):
    return pl.pallas_call(
        join_kernel,
        out_shape=jax.ShapeDtypeStruct(a.shape, BF),
        compiler_params=params(),
        cost_estimate=cost(a.size, 6 * a.size),
        name="join",
    )(a, b)


def finish_kernel(a, b, c, e, g0, g1, g2):
    for s, out in enumerate((g0, g1, g2)):
        total = a[s].astype(F32) + b[s].astype(F32) + c[s].astype(F32) + e[s].astype(F32)
        out[...] = total.T.astype(BF)


def finish(a, b, c, e):
    _, cols, depth = a.shape
    return pl.pallas_call(
        finish_kernel,
        out_shape=[jax.ShapeDtypeStruct((depth, cols), BF)] * 3,
        compiler_params=params(),
        cost_estimate=cost(4 * a.size, 10 * a.size),
        name="finish",
    )(a, b, c, e)


def body(low_state, mid_state, high_state, w_low, w_mid, w_high, kv_grad, loss_mask):
    states = (low_state, mid_state, high_state)
    w = collect((w_low, w_mid, w_high))
    a1 = send(w, Y1)
    a2 = send(w, Y2)
    x1 = send(w, XL)

    w, kv_grad = fence(w, kv_grad)
    mt = masked_turned(kv_grad, loss_mask)
    m_h = send(mt, XH)
    mt, *states = fence(mt, *states)
    states = load(*states)

    mt, m_h, *states = fence(mt, m_h, *states)
    pair = jnp.stack((mt, m_h))
    z1 = send(pair, Z1)
    z2 = send(pair, Z2)

    a1, a2, pair, *states = fence(a1, a2, pair, *states)
    a3 = send(a1, Y1)
    pair_o = send(pair, CORE)
    mine_a, theirs_a = forward(states, (a1, a2), True)

    x1, z1, z2, pair_o, mine_a, theirs_a = fence(x1, z1, z2, pair_o, mine_a, theirs_a)
    z3 = send(z1, Z1)
    z1_o = send(z1, CORE)
    b1 = send(x1, Y1)
    b2 = send(x1, Y2)
    b3 = send(a3, XL)
    mine_b, theirs_b = forward(states, (w, x1), False)

    z3, z1_o, z2, mine_b, theirs_b = fence(z3, z1_o, z2, mine_b, theirs_b)
    z2_o = send(z2, CORE)
    z3_o = send(z3, CORE)
    masked = [pair, z1, z2, z3, pair_o, z1_o, z2_o, z3_o]
    p2x, pmx, ppx, p0x = backward(states, masked, True)

    b1, b2, b3, p2x, pmx, ppx, p0x, pair, theirs_a, theirs_b = fence(
        b1, b2, b3, p2x, pmx, ppx, p0x, pair, theirs_a, theirs_b
    )
    e1 = send(p2x, XL)
    e2 = send(pmx, Y2)
    e3 = send(ppx, Y1)
    got_a = send(theirs_a, CORE)
    got_b = send(theirs_b, CORE)
    mine_c, theirs_c = forward(states, (a3, b3), False)
    mine_d, theirs_d = forward(states, (b1, b2), True)
    got_a, got_b, theirs_c, theirs_d, pair = fence(got_a, got_b, theirs_c, theirs_d, pair)
    q2a, qma, qpa, q0a = pick((mine_a, mine_b), (got_a, got_b))
    t3a = send(q2a, Z2)
    t2a = send(qpa, Z1)
    masked = [pair, *masked[1:]]
    p2, pm, pp, p0 = backward(states, masked, False)

    e1, e2, e3, t3a, t2a, theirs_c, theirs_d, p2, pm, pp, p0 = fence(
        e1, e2, e3, t3a, t2a, theirs_c, theirs_d, p2, pm, pp, p0
    )
    f3 = send(add(p2, e1), Y2)
    fx = send(add(p0x, e2, e3), XL)
    got_c = send(theirs_c, CORE)
    got_d = send(theirs_d, CORE)
    q2b, qmb, qpb, q0b = pick((mine_c, mine_d), (got_c, got_d))
    t3b = send(q2b, Z2)
    t2b = send(qpb, Z1)

    t3b, t2b, pm, pp = fence(t3b, t2b, pm, pp)
    t1 = send(pass_on(qma, t3a, qmb, t3b), Z2)
    f1 = send(add(pm, f3), Y2)
    f2 = send(pp, Y1)
    kept, given = split(q0a, q0b, t1, t2a, t2b)
    got, *grads = fence(send(given, XH), *finish(p0, fx, f1, f2))
    return (join(kept, got), *grads)


def solution(mesh):
    in_specs = (
        P("grp", "tp"),
        P("grp", "tp"),
        P("grp", "tp"),
        P("tp", "grp"),
        P("tp", "grp"),
        P("tp", "grp"),
        P(("grp", "tp"), None),
        P(("grp", "tp")),
    )
    out_specs = (P(("grp", "tp"), None), P("tp", "grp"), P("tp", "grp"), P("tp", "grp"))
    return jax.shard_map(body, mesh=mesh, in_specs=in_specs, out_specs=out_specs, check_vma=False)
```

time: 150 us -> 119 us (0.79)
  starting transfers between devices: 58.2 us -> 42 us
  local copies, waits for them, and re-layouts: 7.62 us -> 0.01 us
  Pallas kernels: 46.2 us -> 41.4 us
  other arithmetic: 4.61 us -> 1.1 us
  waiting for transfers between devices: 32 us -> 33.6 us
    ppermute x33 -> x32, starting transfers between devices: 58.2 us -> 42 us  [send(): return lax.ppermute(array, FULL, pairs)]
    unnamed x18 -> x4, local copies, waits for them, and re-layouts: 7.58 us -> 0.01 us
    pallas_call x6 -> x11, Pallas kernels: 44.3 us -> 39.4 us  [the longest x2 15 us: backward(): pl.pallas_call(kernel, in_specs=[VMEM] * 11, out_specs=[VMEM] * 4, out_sh...]
    convert_element_type x5 -> x3, other arithmetic: 4.35 us -> 1.05 us  [add(): return total.astype(BF)]
    ppermute x33 -> x32, waiting for transfers between devices: 32 us -> 33.6 us  [send(): return lax.ppermute(array, FULL, pairs)]
  transfers between devices with their start and end apart: 33 -> 32, of which waited for: 10 -> 13; matrix products, arithmetic and copies ran while one was open for 4% -> 1% of each run, Pallas kernels for 30% -> 32%
where the time goes in v2:
time: 119 us
  starting transfers between devices  42 us (35%)
  Pallas kernels  41.4 us (35%)
  waiting for transfers between devices  33.6 us (28%)
    ppermute x32, starting transfers between devices, send(): return lax.ppermute(array, FULL, pairs)  42 us
    ppermute x32, waiting for transfers between devices, send(): return lax.ppermute(array, FULL, pairs)  33.6 us
    pallas_call x2, Pallas kernels, backward(): pl.pallas_call(kernel, in_specs=[VMEM] * 11, out_specs=[VMEM] * 4, out_sh...  15 us
    pallas_call x4, Pallas kernels, forward(): pl.pallas_call(kernel, in_specs=[VMEM] * 5, out_specs=[VMEM] * 2, out_sha...  14.9 us
    pallas_call x1, Pallas kernels, load(): pl.pallas_call(load_kernel, in_specs=[pl.BlockSpec(memory_space=pl.ANY)]...  4.68 us
  transfers between devices with their start and end apart: 32, of which 13 were waited for; matrix products, arithmetic and copies ran while one was open for 1% of the time, Pallas kernels for 32%

profile of v2, /device:TPU:0, one launch (start us, length us, event | category | flops | bytes accessed | tf_op | source)
XLA Modules:
  0.0 119.0 jit_solution(12351755527220852527)
XLA Ops:
  0.6 2.0 %collect.1.refs_3_ = bf16[3072,128]{1,0:T(8,128)(2,1)} custom-call(bf16[1024,128]{1,0:T(8,128)(2,1)} %w0.1, bf16[1024,128]{1,0:T(8,128)(2,1)} %w1.1, bf16[1024,128]{1,0:T(8,128)(2,1)} %w2.1), custom_call_target="tpu_custom_call" | custom-call | bytes 1572 | tf_op jit(solution)/shard_map/collect/pallas_call | solution.py:81
  2.7 1.7 %collective-permute-start.4 = (bf16[3072,128]{1,0:T(8,128)(2,1)}, bf16[3072,128]{1,0:T(8,128)(2,1)S(1)}, u32[]{:S(2)}, u32[]{:S(2)}) collective-permute-start(bf16[3072,128]{1,0:T(8,128)(2,1)} %collect.1.refs_3_), channel_id=1, source_target_pairs={{0,32},{1,97},{2,34},{3,99},{4,36},{5,101},{6,38},{7,103},{8,40},{... | collective-permute-start | bytes 2359304 | tf_op jit(solution)/shard_map/ppermute | solution.py:36
  4.4 1.6 %collective-permute-start.5 = (bf16[3072,128]{1,0:T(8,128)(2,1)}, bf16[3072,128]{1,0:T(8,128)(2,1)S(1)}, u32[]{:S(2)}, u32[]{:S(2)}) collective-permute-start(bf16[3072,128]{1,0:T(8,128)(2,1)} %collect.1.refs_3_), channel_id=1, source_target_pairs={{0,96},{1,33},{2,98},{3,35},{4,100},{5,37},{6,102},{7,39},{8,104},... | collective-permute-start | bytes 2359304 | tf_op jit(solution)/shard_map/ppermute | solution.py:36
  6.0 1.8 %masked.1 = bf16[1024,128]{1,0:T(8,128)(2,1)} custom-call(bf16[128,1024]{1,0:T(8,128)(2,1)} %grad_ref, s32[1,128]{1,0:T(1,128)} %bitcast.5), custom_call_target="tpu_custom_call" | custom-call | flops 131 | bytes 524 | tf_op jit(solution)/shard_map/masked/pallas_call | solution.py:107
  7.8 3.2 %collective-permute-start.1 = (bf16[1024,128]{1,0:T(8,128)(2,1)}, bf16[1024,128]{1,0:T(8,128)(2,1)S(1)}, u32[]{:S(2)}, u32[]{:S(2)}) collective-permute-start(bf16[1024,128]{1,0:T(8,128)(2,1)} %masked.1), channel_id=1, source_target_pairs={{0,2},{1,3},{2,0},{3,1},{4,6},{5,7},{6,4},{7,5},{8,10},{9,11},{10,... | collective-permute-start | bytes 786440 | tf_op jit(solution)/shard_map/ppermute | solution.py:36
  11.6 4.7 %load.1 = (bf16[2048,1024]{1,0:T(8,128)(2,1)S(1)}, bf16[2048,1024]{1,0:T(8,128)(2,1)S(1)}, bf16[2048,1024]{1,0:T(8,128)(2,1)S(1)}) custom-call(bf16[2048,1024]{1,0:T(8,128)(2,1)} %refs_0_, bf16[2048,1024]{1,0:T(8,128)(2,1)} %refs_1_, bf16[2048,1024]{1,0:T(8,128)(2,1)} %refs_2_), custom_call_target="tpu_custom_call" | custom-call | bytes 25165 | tf_op jit(solution)/shard_map/load/pallas_call | solution.py:135
  16.3 2.6 %collective-permute-done.1 = bf16[1024,128]{1,0:T(8,128)(2,1)S(1)} collective-permute-done((bf16[1024,128]{1,0:T(8,128)(2,1)}, bf16[1024,128]{1,0:T(8,128)(2,1)S(1)}, u32[]{:S(2)}, u32[]{:S(2)}) %collective-permute-start.1) | collective-permute-done | bytes 262176 | tf_op jit(solution)/shard_map/ppermute | solution.py:36
  18.9 2.1 %collective-permute-start.2 = (bf16[2,1024,128]{2,1,0:T(8,128)(2,1)S(1)}, bf16[2,1024,128]{2,1,0:T(8,128)(2,1)S(1)}, u32[]{:S(2)}, u32[]{:S(2)}) collective-permute-start(bf16[2,1024,128]{2,1,0:T(8,128)(2,1)S(1)} %pad_maximum_fusion.refs_0_), channel_id=1, source_target_pairs={{0,4},{1,13},{2,6},{3,15},{4,8},{5,1},{6,10},{7,3},{8,12},{9,5},{1... | collective-permute-start | bytes 1572872 | tf_op jit(solution)/shard_map/ppermute | solution.py:36
  21.0 2.2 %collective-permute-start.3 = (bf16[2,1024,128]{2,1,0:T(8,128)(2,1)S(1)}, bf16[2,1024,128]{2,1,0:T(8,128)(2,1)S(1)}, u32[]{:S(2)}, u32[]{:S(2)}) collective-permute-start(bf16[2,1024,128]{2,1,0:T(8,128)(2,1)S(1)} %pad_maximum_fusion.refs_0_), channel_id=1, source_target_pairs={{0,12},{1,5},{2,14},{3,7},{4,0},{5,9},{6,2},{7,11},{8,4},{9,13},{1... | collective-permute-start | bytes 1572872 | tf_op jit(solution)/shard_map/ppermute | solution.py:36
  25.1 3.8 %forward.4 = (bf16[4,2,128,256]{3,2,1,0:T(8,128)(2,1)S(1)}, bf16[4,2,128,256]{3,2,1,0:T(8,128)(2,1)S(1)}) custom-call(bf16[2048,1024]{1,0:T(8,128)(2,1)S(1)} %get-tuple-element.112.refs_0_.refs_8_, bf16[2048,1024]{1,0:T(8,128)(2,1)S(1)} %get-tuple-element.113.refs_1_.refs_9_, bf16[2048,1024]{1,0:T(8,128)(2,1)S(1)} %get-tuple-element.114.refs_2_.refs_10_, ...), custom_call_target="tpu_custom_call" | custom-call | flops 3221225 | bytes 14680 | tf_op jit(solution)/shard_map/forward/pallas_call | solution.py:172
  28.9 5.7 %collective-permute-done.2.refs_1_ = bf16[2,1024,128]{2,1,0:T(8,128)(2,1)S(1)} collective-permute-done((bf16[2,1024,128]{2,1,0:T(8,128)(2,1)S(1)}, bf16[2,1024,128]{2,1,0:T(8,128)(2,1)S(1)}, u32[]{:S(2)}, u32[]{:S(2)}) %collective-permute-start.2) | collective-permute-done | bytes 524320 | tf_op jit(solution)/shard_map/ppermute | solution.py:36
  34.6 1.5 %collective-permute-start.7 = (bf16[2,1024,128]{2,1,0:T(8,128)(2,1)S(1)}, bf16[2,1024,128]{2,1,0:T(8,128)(2,1)S(1)}, u32[]{:S(2)}, u32[]{:S(2)}) collective-permute-start(bf16[2,1024,128]{2,1,0:T(8,128)(2,1)S(1)} %collective-permute-done.2.refs_1_), channel_id=1, source_target_pairs={{0,4},{1,13},{2,6},{3,15},{4,8},{5,1},{6,10},{7,3},{8,12},{9,5},{1... | collective-permute-start | bytes 1572872 | tf_op jit(solution)/shard_map/ppermute | solution.py:36
  36.6 4.0 %collective-permute-start.10 = (bf16[3072,128]{1,0:T(8,128)(2,1)S(1)}, bf16[3072,128]{1,0:T(8,128)(2,1)S(1)}, u32[]{:S(2)}, u32[]{:S(2)}) collective-permute-start(bf16[3072,128]{1,0:T(8,128)(2,1)S(1)} %collective-permute-done.refs_4_), channel_id=1, source_target_pairs={{0,96},{1,33},{2,98},{3,35},{4,100},{5,37},{6,102},{7,39},{8,104},... | collective-permute-start | bytes 2359304 | tf_op jit(solution)/shard_map/ppermute | solution.py:36
  40.6 1.4 %collective-permute-start.12 = (bf16[3072,128]{1,0:T(8,128)(2,1)S(1)}, bf16[3072,128]{1,0:T(8,128)(2,1)S(1)}, u32[]{:S(2)}, u32[]{:S(2)}) collective-permute-start(bf16[3072,128]{1,0:T(8,128)(2,1)S(1)} %collective-permute-done.11.refs_3_), channel_id=1, source_target_pairs={{0,16},{1,17},{2,18},{3,19},{4,20},{5,21},{6,22},{7,23},{8,24},{9,... | collective-permute-start | bytes 2359304 | tf_op jit(solution)/shard_map/ppermute | solution.py:36
  42.0 3.7 %forward.5 = (bf16[4,2,128,256]{3,2,1,0:T(8,128)(2,1)S(1)}, bf16[4,2,128,256]{3,2,1,0:T(8,128)(2,1)S(1)}) custom-call(bf16[2048,1024]{1,0:T(8,128)(2,1)S(1)} %get-tuple-element.112.refs_0_.refs_8_, bf16[2048,1024]{1,0:T(8,128)(2,1)S(1)} %get-tuple-element.113.refs_1_.refs_9_, bf16[2048,1024]{1,0:T(8,128)(2,1)S(1)} %get-tuple-element.114.refs_2_.refs_10_, ...), custom_call_target="tpu_custom_call" | custom-call | flops 3221225 | bytes 14680 | tf_op jit(solution)/shard_map/forward/pallas_call | solution.py:172
  48.5 7.5 %backward_other.1 = (bf16[3,128,1024]{2,1,0:T(8,128)(2,1)S(1)}, bf16[3,128,1024]{2,1,0:T(8,128)(2,1)S(1)}, bf16[3,128,1024]{2,1,0:T(8,128)(2,1)S(1)}, bf16[3,128,1024]{2,1,0:T(8,128)(2,1)S(1)}) custom-call(bf16[2,1024,128]{2,1,0:T(8,128)(2,1)S(1)} %pad_maximum_fusion.refs_0_, bf16[2,1024,128]{2,1,0:T(8,128)(2,1)S(1)} %collective-permute-done.2.refs_1_, ...), custom_call_target="tpu_custom_call" | custom-call | flops 6442450 | bytes 20971 | tf_op jit(solution)/shard_map/backward_other/pallas_call | solution.py:216
  57.6 2.2 %collective-permute-done.12.refs_4_ = bf16[3072,128]{1,0:T(8,128)(2,1)S(1)} collective-permute-done((bf16[3072,128]{1,0:T(8,128)(2,1)S(1)}, bf16[3072,128]{1,0:T(8,128)(2,1)S(1)}, u32[]{:S(2)}, u32[]{:S(2)}) %collective-permute-start.12) | collective-permute-done | bytes 786464 | tf_op jit(solution)/shard_map/ppermute | solution.py:36
  60.3 1.4 %collective-permute-start.17 = (bf16[3,128,1024]{2,1,0:T(8,128)(2,1)S(1)}, bf16[3,128,1024]{2,1,0:T(8,128)(2,1)S(1)}, u32[]{:S(2)}, u32[]{:S(2)}) collective-permute-start(bf16[3,128,1024]{2,1,0:T(8,128)(2,1)S(1)} %get-tuple-element.150), channel_id=1, source_target_pairs={{0,16},{1,17},{2,18},{3,19},{4,20},{5,21},{6,22},{7,23},{8,24},{9,... | collective-permute-start | bytes 2359304 | tf_op jit(solution)/shard_map/ppermute | solution.py:36
  61.7 3.0 %collective-permute-start.18 = (bf16[3,128,1024]{2,1,0:T(8,128)(2,1)S(1)}, bf16[3,128,1024]{2,1,0:T(8,128)(2,1)S(1)}, u32[]{:S(2)}, u32[]{:S(2)}) collective-permute-start(bf16[3,128,1024]{2,1,0:T(8,128)(2,1)S(1)} %get-tuple-element.151), channel_id=1, source_target_pairs={{0,96},{1,33},{2,98},{3,35},{4,100},{5,37},{6,102},{7,39},{8,104},... | collective-permute-start | bytes 2359304 | tf_op jit(solution)/shard_map/ppermute | solution.py:36
  64.7 3.8 %forward.7 = (bf16[4,2,128,256]{3,2,1,0:T(8,128)(2,1)S(1)}, bf16[4,2,128,256]{3,2,1,0:T(8,128)(2,1)S(1)}) custom-call(bf16[2048,1024]{1,0:T(8,128)(2,1)S(1)} %get-tuple-element.112.refs_0_.refs_8_, bf16[2048,1024]{1,0:T(8,128)(2,1)S(1)} %get-tuple-element.113.refs_1_.refs_9_, bf16[2048,1024]{1,0:T(8,128)(2,1)S(1)} %get-tuple-element.114.refs_2_.refs_10_, ...), custom_call_target="tpu_custom_call" | custom-call | flops 3221225 | bytes 14680 | tf_op jit(solution)/shard_map/forward/pallas_call | solution.py:172
  68.5 3.7 %forward.6 = (bf16[4,2,128,256]{3,2,1,0:T(8,128)(2,1)S(1)}, bf16[4,2,128,256]{3,2,1,0:T(8,128)(2,1)S(1)}) custom-call(bf16[2048,1024]{1,0:T(8,128)(2,1)S(1)} %get-tuple-element.112.refs_0_.refs_8_, bf16[2048,1024]{1,0:T(8,128)(2,1)S(1)} %get-tuple-element.113.refs_1_.refs_9_, bf16[2048,1024]{1,0:T(8,128)(2,1)S(1)} %get-tuple-element.114.refs_2_.refs_10_, ...), custom_call_target="tpu_custom_call" | custom-call | flops 3221225 | bytes 14680 | tf_op jit(solution)/shard_map/forward/pallas_call | solution.py:172
  74.5 7.5 %backward_own.1 = (bf16[3,128,1024]{2,1,0:T(8,128)(2,1)S(1)}, bf16[3,128,1024]{2,1,0:T(8,128)(2,1)S(1)}, bf16[3,128,1024]{2,1,0:T(8,128)(2,1)S(1)}, bf16[3,128,1024]{2,1,0:T(8,128)(2,1)S(1)}) custom-call(bf16[2,1024,128]{2,1,0:T(8,128)(2,1)S(1)} %pad_maximum_fusion.refs_0_, bf16[2,1024,128]{2,1,0:T(8,128)(2,1)S(1)} %collective-permute-done.2.refs_1_, ...), custom_call_target="tpu_custom_call" | custom-call | flops 6442450 | bytes 20971 | tf_op jit(solution)/shard_map/backward_own/pallas_call | solution.py:216
  83.0 3.3 %collective-permute-start.29 = (bf16[3,128,1024]{2,1,0:T(8,128)(2,1)S(1)}, bf16[3,128,1024]{2,1,0:T(8,128)(2,1)S(1)}, u32[]{:S(2)}, u32[]{:S(2)}) collective-permute-start(bf16[3,128,1024]{2,1,0:T(8,128)(2,1)S(1)} %add_convert_fusion.1), channel_id=1, source_target_pairs={{0,96},{1,33},{2,98},{3,35},{4,100},{5,37},{6,102},{7,39},{8,104},... | collective-permute-start | bytes 2359304 | tf_op jit(solution)/shard_map/ppermute | solution.py:36
  86.6 2.1 %collective-permute-start.24 = (bf16[2,128,512]{2,1,0:T(8,128)(2,1)S(1)}, bf16[2,128,512]{2,1,0:T(8,128)(2,1)S(1)}, u32[]{:S(2)}, u32[]{:S(2)}) collective-permute-start(bf16[2,128,512]{2,1,0:T(8,128)(2,1)S(1)} %get-tuple-element.168), channel_id=1, source_target_pairs={{0,12},{1,5},{2,14},{3,7},{4,0},{5,9},{6,2},{7,11},{8,4},{9,13},{1... | collective-permute-start | bytes 786440 | tf_op jit(solution)/shard_map/ppermute | solution.py:36
  89.8 4.2 %collective-permute-done.24.tb = bf16[2,128,512]{2,1,0:T(8,128)(2,1)S(1)} collective-permute-done((bf16[2,128,512]{2,1,0:T(8,128)(2,1)S(1)}, bf16[2,128,512]{2,1,0:T(8,128)(2,1)S(1)}, u32[]{:S(2)}, u32[]{:S(2)}) %collective-permute-start.24) | collective-permute-done | bytes 262176 | tf_op jit(solution)/shard_map/ppermute | solution.py:36
  94.0 2.3 %collective-permute-done.25.c1 = bf16[2,128,512]{2,1,0:T(8,128)(2,1)S(1)} collective-permute-done((bf16[2,128,512]{2,1,0:T(8,128)(2,1)S(1)}, bf16[2,128,512]{2,1,0:T(8,128)(2,1)S(1)}, u32[]{:S(2)}, u32[]{:S(2)}) %collective-permute-start.25) | collective-permute-done | bytes 262176 | tf_op jit(solution)/shard_map/ppermute | solution.py:36
  96.4 1.5 %collective-permute-start.26 = (bf16[2,2,128,512]{3,2,1,0:T(8,128)(2,1)S(1)}, bf16[2,2,128,512]{3,2,1,0:T(8,128)(2,1)S(1)}, u32[]{:S(2)}, u32[]{:S(2)}) collective-permute-start(bf16[2,2,128,512]{3,2,1,0:T(8,128)(2,1)S(1)} %pass_on.1), channel_id=1, source_target_pairs={{0,12},{1,5},{2,14},{3,7},{4,0},{5,9},{6,2},{7,11},{8,4},{9,13},{1... | collective-permute-start | bytes 1572872 | tf_op jit(solution)/shard_map/ppermute | solution.py:36
  98.2 3.2 %collective-permute-start.30 = (bf16[3,128,1024]{2,1,0:T(8,128)(2,1)S(1)}, bf16[3,128,1024]{2,1,0:T(8,128)(2,1)S(1)}, u32[]{:S(2)}, u32[]{:S(2)}) collective-permute-start(bf16[3,128,1024]{2,1,0:T(8,128)(2,1)S(1)} %add_convert_fusion), channel_id=1, source_target_pairs={{0,96},{1,33},{2,98},{3,35},{4,100},{5,37},{6,102},{7,39},{8,104},... | collective-permute-start | bytes 2359304 | tf_op jit(solution)/shard_map/ppermute | solution.py:36
  101.4 4.3 %collective-permute-done.26.b = bf16[2,2,128,512]{3,2,1,0:T(8,128)(2,1)S(1)} collective-permute-done((bf16[2,2,128,512]{3,2,1,0:T(8,128)(2,1)S(1)}, bf16[2,2,128,512]{3,2,1,0:T(8,128)(2,1)S(1)}, u32[]{:S(2)}, u32[]{:S(2)}) %collective-permute-start.26) | collective-permute-done | bytes 524320 | tf_op jit(solution)/shard_map/ppermute | solution.py:36
  105.9 2.4 %collective-permute-start.27 = (bf16[128,1024]{1,0:T(8,128)(2,1)S(1)}, bf16[128,1024]{1,0:T(8,128)(2,1)S(1)}, u32[]{:S(2)}, u32[]{:S(2)}) collective-permute-start(bf16[128,1024]{1,0:T(8,128)(2,1)S(1)} %get-tuple-element.176), channel_id=1, source_target_pairs={{0,2},{1,3},{2,0},{3,1},{4,6},{5,7},{6,4},{7,5},{8,10},{9,11},{10,... | collective-permute-start | bytes 786440 | tf_op jit(solution)/shard_map/ppermute | solution.py:36
  108.2 1.5 %collective-permute-done.28.b = bf16[3,128,1024]{2,1,0:T(8,128)(2,1)S(1)} collective-permute-done((bf16[3,128,1024]{2,1,0:T(8,128)(2,1)S(1)}, bf16[3,128,1024]{2,1,0:T(8,128)(2,1)S(1)}, u32[]{:S(2)}, u32[]{:S(2)}) %collective-permute-start.28) | collective-permute-done | bytes 786464 | tf_op jit(solution)/shard_map/ppermute | solution.py:36
  109.7 6.4 %collective-permute-done.30.c = bf16[3,128,1024]{2,1,0:T(8,128)(2,1)S(1)} collective-permute-done((bf16[3,128,1024]{2,1,0:T(8,128)(2,1)S(1)}, bf16[3,128,1024]{2,1,0:T(8,128)(2,1)S(1)}, u32[]{:S(2)}, u32[]{:S(2)}) %collective-permute-start.30) | collective-permute-done | bytes 786464 | tf_op jit(solution)/shard_map/ppermute | solution.py:36
  (55 shorter events, 16.0 us)
Async XLA Ops:
  2.7 20.5 %collective-permute-start.4 = (bf16[3072,128]{1,0:T(8,128)(2,1)}, bf16[3072,128]{1,0:T(8,128)(2,1)S(1)}, u32[]{:S(2)}, u32[]{:S(2)}) collective-permute-start(bf16[3072,128]{1,0:T(8,128)(2,1)} %collect.1.refs_3_), channel_id=1, source_target_pairs={{0,32},{1,97},{2,34},{3,99},{4,36},{5,101},{6,38},{7,103},{8,40},{... | collective-permute-start | bytes 2359304 | tf_op jit(solution)/shard_map/ppermute | solution.py:36
  4.4 18.8 %collective-permute-start.5 = (bf16[3072,128]{1,0:T(8,128)(2,1)}, bf16[3072,128]{1,0:T(8,128)(2,1)S(1)}, u32[]{:S(2)}, u32[]{:S(2)}) collective-permute-start(bf16[3072,128]{1,0:T(8,128)(2,1)} %collect.1.refs_3_), channel_id=1, source_target_pairs={{0,96},{1,33},{2,98},{3,35},{4,100},{5,37},{6,102},{7,39},{8,104},... | collective-permute-start | bytes 2359304 | tf_op jit(solution)/shard_map/ppermute | solution.py:36
  7.8 11.0 %collective-permute-start.1 = (bf16[1024,128]{1,0:T(8,128)(2,1)}, bf16[1024,128]{1,0:T(8,128)(2,1)S(1)}, u32[]{:S(2)}, u32[]{:S(2)}) collective-permute-start(bf16[1024,128]{1,0:T(8,128)(2,1)} %masked.1), channel_id=1, source_target_pairs={{0,2},{1,3},{2,0},{3,1},{4,6},{5,7},{6,4},{7,5},{8,10},{9,11},{10,... | collective-permute-start | bytes 786440 | tf_op jit(solution)/shard_map/ppermute | solution.py:36
  11.0 23.6 %collective-permute-start = (bf16[3072,128]{1,0:T(8,128)(2,1)}, bf16[3072,128]{1,0:T(8,128)(2,1)S(1)}, u32[]{:S(2)}, u32[]{:S(2)}) collective-permute-start(bf16[3072,128]{1,0:T(8,128)(2,1)} %collect.1.refs_3_), channel_id=1, source_target_pairs={{0,16},{1,17},{2,18},{3,19},{4,20},{5,21},{6,22},{7,23},{8,24},{9,... | collective-permute-start | bytes 2359304 | tf_op jit(solution)/shard_map/ppermute | solution.py:36
  18.9 15.7 %collective-permute-start.2 = (bf16[2,1024,128]{2,1,0:T(8,128)(2,1)S(1)}, bf16[2,1024,128]{2,1,0:T(8,128)(2,1)S(1)}, u32[]{:S(2)}, u32[]{:S(2)}) collective-permute-start(bf16[2,1024,128]{2,1,0:T(8,128)(2,1)S(1)} %pad_maximum_fusion.refs_0_), channel_id=1, source_target_pairs={{0,4},{1,13},{2,6},{3,15},{4,8},{5,1},{6,10},{7,3},{8,12},{9,5},{1... | collective-permute-start | bytes 1572872 | tf_op jit(solution)/shard_map/ppermute | solution.py:36
  21.0 13.6 %collective-permute-start.3 = (bf16[2,1024,128]{2,1,0:T(8,128)(2,1)S(1)}, bf16[2,1024,128]{2,1,0:T(8,128)(2,1)S(1)}, u32[]{:S(2)}, u32[]{:S(2)}) collective-permute-start(bf16[2,1024,128]{2,1,0:T(8,128)(2,1)S(1)} %pad_maximum_fusion.refs_0_), channel_id=1, source_target_pairs={{0,12},{1,5},{2,14},{3,7},{4,0},{5,9},{6,2},{7,11},{8,4},{9,13},{1... | collective-permute-start | bytes 1572872 | tf_op jit(solution)/shard_map/ppermute | solution.py:36
  23.2 11.4 %collective-permute-start.6 = (bf16[2,1024,128]{2,1,0:T(8,128)(2,1)S(1)}, bf16[2,1024,128]{2,1,0:T(8,128)(2,1)S(1)}, u32[]{:S(2)}, u32[]{:S(2)}) collective-permute-start(bf16[2,1024,128]{2,1,0:T(8,128)(2,1)S(1)} %pad_maximum_fusion.refs_0_), channel_id=1, source_target_pairs={{0,1},{1,0},{2,3},{3,2},{4,5},{5,4},{6,7},{7,6},{8,9},{9,8},{10,11... | collective-permute-start | bytes 1572872 | tf_op jit(solution)/shard_map/ppermute | solution.py:36
  24.4 16.2 %collective-permute-start.11 = (bf16[3072,128]{1,0:T(8,128)(2,1)S(1)}, bf16[3072,128]{1,0:T(8,128)(2,1)S(1)}, u32[]{:S(2)}, u32[]{:S(2)}) collective-permute-start(bf16[3072,128]{1,0:T(8,128)(2,1)S(1)} %collective-permute-done.4.refs_3_), channel_id=1, source_target_pairs={{0,32},{1,97},{2,34},{3,99},{4,36},{5,101},{6,38},{7,103},{8,40},{... | collective-permute-start | bytes 2359304 | tf_op jit(solution)/shard_map/ppermute | solution.py:36
  34.6 11.1 %collective-permute-start.7 = (bf16[2,1024,128]{2,1,0:T(8,128)(2,1)S(1)}, bf16[2,1024,128]{2,1,0:T(8,128)(2,1)S(1)}, u32[]{:S(2)}, u32[]{:S(2)}) collective-permute-start(bf16[2,1024,128]{2,1,0:T(8,128)(2,1)S(1)} %collective-permute-done.2.refs_1_), channel_id=1, source_target_pairs={{0,4},{1,13},{2,6},{3,15},{4,8},{5,1},{6,10},{7,3},{8,12},{9,5},{1... | collective-permute-start | bytes 1572872 | tf_op jit(solution)/shard_map/ppermute | solution.py:36
  36.1 9.6 %collective-permute-start.8 = (bf16[2,1024,128]{2,1,0:T(8,128)(2,1)S(1)}, bf16[2,1024,128]{2,1,0:T(8,128)(2,1)S(1)}, u32[]{:S(2)}, u32[]{:S(2)}) collective-permute-start(bf16[2,1024,128]{2,1,0:T(8,128)(2,1)S(1)} %collective-permute-done.2.refs_1_), channel_id=1, source_target_pairs={{0,1},{1,0},{2,3},{3,2},{4,5},{5,4},{6,7},{7,6},{8,9},{9,8},{10,11... | collective-permute-start | bytes 1572872 | tf_op jit(solution)/shard_map/ppermute | solution.py:36
  36.4 20.6 %collective-permute-start.9 = (bf16[3072,128]{1,0:T(8,128)(2,1)S(1)}, bf16[3072,128]{1,0:T(8,128)(2,1)S(1)}, u32[]{:S(2)}, u32[]{:S(2)}) collective-permute-start(bf16[3072,128]{1,0:T(8,128)(2,1)S(1)} %collective-permute-done.refs_4_), channel_id=1, source_target_pairs={{0,32},{1,97},{2,34},{3,99},{4,36},{5,101},{6,38},{7,103},{8,40},{... | collective-permute-start | bytes 2359304 | tf_op jit(solution)/shard_map/ppermute | solution.py:36
  36.6 21.0 %collective-permute-start.10 = (bf16[3072,128]{1,0:T(8,128)(2,1)S(1)}, bf16[3072,128]{1,0:T(8,128)(2,1)S(1)}, u32[]{:S(2)}, u32[]{:S(2)}) collective-permute-start(bf16[3072,128]{1,0:T(8,128)(2,1)S(1)} %collective-permute-done.refs_4_), channel_id=1, source_target_pairs={{0,96},{1,33},{2,98},{3,35},{4,100},{5,37},{6,102},{7,39},{8,104},... | collective-permute-start | bytes 2359304 | tf_op jit(solution)/shard_map/ppermute | solution.py:36
  40.6 19.2 %collective-permute-start.12 = (bf16[3072,128]{1,0:T(8,128)(2,1)S(1)}, bf16[3072,128]{1,0:T(8,128)(2,1)S(1)}, u32[]{:S(2)}, u32[]{:S(2)}) collective-permute-start(bf16[3072,128]{1,0:T(8,128)(2,1)S(1)} %collective-permute-done.11.refs_3_), channel_id=1, source_target_pairs={{0,16},{1,17},{2,18},{3,19},{4,20},{5,21},{6,22},{7,23},{8,24},{9,... | collective-permute-start | bytes 2359304 | tf_op jit(solution)/shard_map/ppermute | solution.py:36
  45.8 2.0 %collective-permute-start.13 = (bf16[2,1024,128]{2,1,0:T(8,128)(2,1)S(1)}, bf16[2,1024,128]{2,1,0:T(8,128)(2,1)S(1)}, u32[]{:S(2)}, u32[]{:S(2)}) collective-permute-start(bf16[2,1024,128]{2,1,0:T(8,128)(2,1)S(1)} %collective-permute-done.3.refs_2_), channel_id=1, source_target_pairs={{0,1},{1,0},{2,3},{3,2},{4,5},{5,4},{6,7},{7,6},{8,9},{9,8},{10,11... | collective-permute-start | bytes 1572872 | tf_op jit(solution)/shard_map/ppermute | solution.py:36
  45.9 2.6 %collective-permute-start.14 = (bf16[2,1024,128]{2,1,0:T(8,128)(2,1)S(1)}, bf16[2,1024,128]{2,1,0:T(8,128)(2,1)S(1)}, u32[]{:S(2)}, u32[]{:S(2)}) collective-permute-start(bf16[2,1024,128]{2,1,0:T(8,128)(2,1)S(1)} %collective-permute-done.7.refs_3_), channel_id=1, source_target_pairs={{0,1},{1,0},{2,3},{3,2},{4,5},{5,4},{6,7},{7,6},{8,9},{9,8},{10,11... | collective-permute-start | bytes 1572872 | tf_op jit(solution)/shard_map/ppermute | solution.py:36
  59.8 12.4 %collective-permute-start.15 = (bf16[4,2,128,256]{3,2,1,0:T(8,128)(2,1)S(1)}, bf16[4,2,128,256]{3,2,1,0:T(8,128)(2,1)S(1)}, u32[]{:S(2)}, u32[]{:S(2)}) collective-permute-start(bf16[4,2,128,256]{3,2,1,0:T(8,128)(2,1)S(1)} %get-tuple-element.137), channel_id=1, source_target_pairs={{0,1},{1,0},{2,3},{3,2},{4,5},{5,4},{6,7},{7,6},{8,9},{9,8},{10,11... | collective-permute-start | bytes 1572872 | tf_op jit(solution)/shard_map/ppermute | solution.py:36
  59.8 12.4 %collective-permute-start.16 = (bf16[4,2,128,256]{3,2,1,0:T(8,128)(2,1)S(1)}, bf16[4,2,128,256]{3,2,1,0:T(8,128)(2,1)S(1)}, u32[]{:S(2)}, u32[]{:S(2)}) collective-permute-start(bf16[4,2,128,256]{3,2,1,0:T(8,128)(2,1)S(1)} %get-tuple-element.138), channel_id=1, source_target_pairs={{0,1},{1,0},{2,3},{3,2},{4,5},{5,4},{6,7},{7,6},{8,9},{9,8},{10,11... | collective-permute-start | bytes 1572872 | tf_op jit(solution)/shard_map/ppermute | solution.py:36
  60.3 21.8 %collective-permute-start.17 = (bf16[3,128,1024]{2,1,0:T(8,128)(2,1)S(1)}, bf16[3,128,1024]{2,1,0:T(8,128)(2,1)S(1)}, u32[]{:S(2)}, u32[]{:S(2)}) collective-permute-start(bf16[3,128,1024]{2,1,0:T(8,128)(2,1)S(1)} %get-tuple-element.150), channel_id=1, source_target_pairs={{0,16},{1,17},{2,18},{3,19},{4,20},{5,21},{6,22},{7,23},{8,24},{9,... | collective-permute-start | bytes 2359304 | tf_op jit(solution)/shard_map/ppermute | solution.py:36
  61.7 20.3 %collective-permute-start.18 = (bf16[3,128,1024]{2,1,0:T(8,128)(2,1)S(1)}, bf16[3,128,1024]{2,1,0:T(8,128)(2,1)S(1)}, u32[]{:S(2)}, u32[]{:S(2)}) collective-permute-start(bf16[3,128,1024]{2,1,0:T(8,128)(2,1)S(1)} %get-tuple-element.151), channel_id=1, source_target_pairs={{0,96},{1,33},{2,98},{3,35},{4,100},{5,37},{6,102},{7,39},{8,104},... | collective-permute-start | bytes 2359304 | tf_op jit(solution)/shard_map/ppermute | solution.py:36
  64.7 17.4 %collective-permute-start.19 = (bf16[3,128,1024]{2,1,0:T(8,128)(2,1)S(1)}, bf16[3,128,1024]{2,1,0:T(8,128)(2,1)S(1)}, u32[]{:S(2)}, u32[]{:S(2)}) collective-permute-start(bf16[3,128,1024]{2,1,0:T(8,128)(2,1)S(1)} %get-tuple-element.152), channel_id=1, source_target_pairs={{0,32},{1,97},{2,34},{3,99},{4,36},{5,101},{6,38},{7,103},{8,40},{... | collective-permute-start | bytes 2359304 | tf_op jit(solution)/shard_map/ppermute | solution.py:36
  72.4 9.7 %collective-permute-start.20 = (bf16[2,128,512]{2,1,0:T(8,128)(2,1)S(1)}, bf16[2,128,512]{2,1,0:T(8,128)(2,1)S(1)}, u32[]{:S(2)}, u32[]{:S(2)}) collective-permute-start(bf16[2,128,512]{2,1,0:T(8,128)(2,1)S(1)} %get-tuple-element.153), channel_id=1, source_target_pairs={{0,12},{1,5},{2,14},{3,7},{4,0},{5,9},{6,2},{7,11},{8,4},{9,13},{1... | collective-permute-start | bytes 786440 | tf_op jit(solution)/shard_map/ppermute | solution.py:36
  73.4 8.7 %collective-permute-start.21 = (bf16[2,128,512]{2,1,0:T(8,128)(2,1)S(1)}, bf16[2,128,512]{2,1,0:T(8,128)(2,1)S(1)}, u32[]{:S(2)}, u32[]{:S(2)}) collective-permute-start(bf16[2,128,512]{2,1,0:T(8,128)(2,1)S(1)} %get-tuple-element.154), channel_id=1, source_target_pairs={{0,4},{1,13},{2,6},{3,15},{4,8},{5,1},{6,10},{7,3},{8,12},{9,5},{1... | collective-permute-start | bytes 786440 | tf_op jit(solution)/shard_map/ppermute | solution.py:36
  82.1 4.2 %collective-permute-start.22 = (bf16[4,2,128,256]{3,2,1,0:T(8,128)(2,1)S(1)}, bf16[4,2,128,256]{3,2,1,0:T(8,128)(2,1)S(1)}, u32[]{:S(2)}, u32[]{:S(2)}) collective-permute-start(bf16[4,2,128,256]{3,2,1,0:T(8,128)(2,1)S(1)} %get-tuple-element.162), channel_id=1, source_target_pairs={{0,1},{1,0},{2,3},{3,2},{4,5},{5,4},{6,7},{7,6},{8,9},{9,8},{10,11... | collective-permute-start | bytes 1572872 | tf_op jit(solution)/shard_map/ppermute | solution.py:36
  82.3 4.0 %collective-permute-start.23 = (bf16[4,2,128,256]{3,2,1,0:T(8,128)(2,1)S(1)}, bf16[4,2,128,256]{3,2,1,0:T(8,128)(2,1)S(1)}, u32[]{:S(2)}, u32[]{:S(2)}) collective-permute-start(bf16[4,2,128,256]{3,2,1,0:T(8,128)(2,1)S(1)} %get-tuple-element.163), channel_id=1, source_target_pairs={{0,1},{1,0},{2,3},{3,2},{4,5},{5,4},{6,7},{7,6},{8,9},{9,8},{10,11... | collective-permute-start | bytes 1572872 | tf_op jit(solution)/shard_map/ppermute | solution.py:36
  83.0 14.9 %collective-permute-start.29 = (bf16[3,128,1024]{2,1,0:T(8,128)(2,1)S(1)}, bf16[3,128,1024]{2,1,0:T(8,128)(2,1)S(1)}, u32[]{:S(2)}, u32[]{:S(2)}) collective-permute-start(bf16[3,128,1024]{2,1,0:T(8,128)(2,1)S(1)} %add_convert_fusion.1), channel_id=1, source_target_pairs={{0,96},{1,33},{2,98},{3,35},{4,100},{5,37},{6,102},{7,39},{8,104},... | collective-permute-start | bytes 2359304 | tf_op jit(solution)/shard_map/ppermute | solution.py:36
  86.6 7.5 %collective-permute-start.24 = (bf16[2,128,512]{2,1,0:T(8,128)(2,1)S(1)}, bf16[2,128,512]{2,1,0:T(8,128)(2,1)S(1)}, u32[]{:S(2)}, u32[]{:S(2)}) collective-permute-start(bf16[2,128,512]{2,1,0:T(8,128)(2,1)S(1)} %get-tuple-element.168), channel_id=1, source_target_pairs={{0,12},{1,5},{2,14},{3,7},{4,0},{5,9},{6,2},{7,11},{8,4},{9,13},{1... | collective-permute-start | bytes 786440 | tf_op jit(solution)/shard_map/ppermute | solution.py:36
  88.7 7.6 %collective-permute-start.25 = (bf16[2,128,512]{2,1,0:T(8,128)(2,1)S(1)}, bf16[2,128,512]{2,1,0:T(8,128)(2,1)S(1)}, u32[]{:S(2)}, u32[]{:S(2)}) collective-permute-start(bf16[2,128,512]{2,1,0:T(8,128)(2,1)S(1)} %get-tuple-element.169), channel_id=1, source_target_pairs={{0,4},{1,13},{2,6},{3,15},{4,8},{5,1},{6,10},{7,3},{8,12},{9,5},{1... | collective-permute-start | bytes 786440 | tf_op jit(solution)/shard_map/ppermute | solution.py:36
  89.2 20.6 %collective-permute-start.28 = (bf16[3,128,1024]{2,1,0:T(8,128)(2,1)S(1)}, bf16[3,128,1024]{2,1,0:T(8,128)(2,1)S(1)}, u32[]{:S(2)}, u32[]{:S(2)}) collective-permute-start(bf16[3,128,1024]{2,1,0:T(8,128)(2,1)S(1)} %add_convert_fusion.2), channel_id=1, source_target_pairs={{0,16},{1,17},{2,18},{3,19},{4,20},{5,21},{6,22},{7,23},{8,24},{9,... | collective-permute-start | bytes 2359304 | tf_op jit(solution)/shard_map/ppermute | solution.py:36
  96.4 9.3 %collective-permute-start.26 = (bf16[2,2,128,512]{3,2,1,0:T(8,128)(2,1)S(1)}, bf16[2,2,128,512]{3,2,1,0:T(8,128)(2,1)S(1)}, u32[]{:S(2)}, u32[]{:S(2)}) collective-permute-start(bf16[2,2,128,512]{3,2,1,0:T(8,128)(2,1)S(1)} %pass_on.1), channel_id=1, source_target_pairs={{0,12},{1,5},{2,14},{3,7},{4,0},{5,9},{6,2},{7,11},{8,4},{9,13},{1... | collective-permute-start | bytes 1572872 | tf_op jit(solution)/shard_map/ppermute | solution.py:36
  98.2 17.9 %collective-permute-start.30 = (bf16[3,128,1024]{2,1,0:T(8,128)(2,1)S(1)}, bf16[3,128,1024]{2,1,0:T(8,128)(2,1)S(1)}, u32[]{:S(2)}, u32[]{:S(2)}) collective-permute-start(bf16[3,128,1024]{2,1,0:T(8,128)(2,1)S(1)} %add_convert_fusion), channel_id=1, source_target_pairs={{0,96},{1,33},{2,98},{3,35},{4,100},{5,37},{6,102},{7,39},{8,104},... | collective-permute-start | bytes 2359304 | tf_op jit(solution)/shard_map/ppermute | solution.py:36
  101.4 15.5 %collective-permute-start.31 = (bf16[3,128,1024]{2,1,0:T(8,128)(2,1)S(1)}, bf16[3,128,1024]{2,1,0:T(8,128)(2,1)S(1)}, u32[]{:S(2)}, u32[]{:S(2)}) collective-permute-start(bf16[3,128,1024]{2,1,0:T(8,128)(2,1)S(1)} %get-tuple-element.184), channel_id=1, source_target_pairs={{0,32},{1,97},{2,34},{3,99},{4,36},{5,101},{6,38},{7,103},{8,40},{... | collective-permute-start | bytes 2359304 | tf_op jit(solution)/shard_map/ppermute | solution.py:36
  105.9 12.3 %collective-permute-start.27 = (bf16[128,1024]{1,0:T(8,128)(2,1)S(1)}, bf16[128,1024]{1,0:T(8,128)(2,1)S(1)}, u32[]{:S(2)}, u32[]{:S(2)}) collective-permute-start(bf16[128,1024]{1,0:T(8,128)(2,1)S(1)} %get-tuple-element.176), channel_id=1, source_target_pairs={{0,2},{1,3},{2,0},{3,1},{4,6},{5,7},{6,4},{7,5},{8,10},{9,11},{10,... | collective-permute-start | bytes 786440 | tf_op jit(solution)/shard_map/ppermute | solution.py:36
  (2 other events, 34.2 us)

commit v3 on v2

--- a/solution.py
+++ b/solution.py
@@ -65,59 +65,40 @@
 VMEM = pl.BlockSpec(memory_space=pltpu.VMEM)
 
 
-def collect_kernel(w0, w1, w2, w_ref, sems):
+def prepare_kernel(w0, w1, w2, grad_ref, mask_ref, w_ref, turned_ref, grad, mask, sems):
     depth = w0.shape[0]
-    moves = []
-    for i, w in enumerate((w0, w1, w2)):
-        moves.append(pltpu.make_async_copy(w, w_ref.at[pl.ds(i * depth, depth), :], sems.at[i]))
-    for move in moves:
-        move.start()
-    for move in moves:
-        move.wait()
-
-
-def collect(weights):
-    depth, width = weights[0].shape
-    return pl.pallas_call(
-        collect_kernel,
-        in_specs=[pl.BlockSpec(memory_space=pl.ANY)] * 3,
-        out_specs=VMEM,
-        out_shape=jax.ShapeDtypeStruct((3 * depth, width), BF),
-        scratch_shapes=[pltpu.SemaphoreType.DMA((3,))],
-        compiler_params=params(60),
-        cost_estimate=cost(0, 12 * depth * width),
-        name="collect",
-    )(*weights)
-
-
-def mask_kernel(grad_ref, mask_ref, turned_ref, grad, mask, sems):
     moves = [
         pltpu.make_async_copy(mask_ref, mask, sems.at[0]),
         pltpu.make_async_copy(grad_ref, grad, sems.at[1]),
     ]
+    for i, w in enumerate((w0, w1, w2)):
+        moves.append(pltpu.make_async_copy(w, w_ref.at[pl.ds(i * depth, depth), :], sems.at[2 + i]))
     for move in moves:
         move.start()
-    for move in moves:
+    moves[0].wait()
+    moves[1].wait()
+    turned_ref[...] = (grad[...].astype(F32).T * mask[...].astype(F32)).astype(BF)
+    for move in moves[2:]:
         move.wait()
-    turned_ref[...] = (grad[...].astype(F32).T * mask[...].astype(F32)).astype(BF)
-
-
-def masked_turned(kv_grad, loss_mask):
+
+
+def prepare(weights, kv_grad, loss_mask):
     rows, cols = kv_grad.shape
-    return pl.pallas_call(
-        mask_kernel,
-        in_specs=[pl.BlockSpec(memory_space=pl.ANY)] * 2,
-        out_specs=VMEM,
-        out_shape=jax.ShapeDtypeStruct((cols, rows), BF),
+    depth, width = weights[0].shape
+    return pl.pallas_call(
+        prepare_kernel,
+        in_specs=[pl.BlockSpec(memory_space=pl.ANY)] * 5,
+        out_specs=[VMEM] * 2,
+        out_shape=[jax.ShapeDtypeStruct((3 * depth, width), BF), jax.ShapeDtypeStruct((cols, rows), BF)],
         scratch_shapes=[
             pltpu.VMEM((rows, cols), BF),
             pltpu.VMEM((1, rows), jnp.int32),
-            pltpu.SemaphoreType.DMA((2,)),
+            pltpu.SemaphoreType.DMA((5,)),
         ],
         compiler_params=params(60),
-        cost_estimate=cost(rows * cols, 4 * rows * cols),
-        name="masked",
-    )(kv_grad, loss_mask.reshape(1, rows))
+        cost_estimate=cost(rows * cols, 4 * rows * cols + 12 * depth * width),
+        name="prepare",
+    )(*weights, kv_grad, loss_mask.reshape(1, rows))
 
 
 def load_kernel(*refs):
@@ -181,20 +162,21 @@
     )(*states, *blocks)
 
 
-def backward_kernel(other, refs):
-    mine, theirs, (s0, s1, s2) = refs[:4], refs[4:8], refs[8:11]
-    p2, pm, pp, p0, turned = refs[11:]
+def backward_kernel(other, dests, refs):
+    near, far, near_o, far_o, s0, s1, s2 = refs[:7]
+    outs, turned = refs[7:-1], refs[-1]
     y, xl, z, xh, c, d = place()
     half = (xl + 1) % 2 if other else xl
-    for pairs, core in ((mine, c), (theirs, 1 - c)):
+    spots = {"far": y + 2, "back": y - d, "ahead": y + d, "here": y}
+    for ref, core, first in ((near, c, 0), (far, c, 2), (near_o, 1 - c, 0), (far_o, 1 - c, 2)):
         way = 1 - 2 * core
-        for ref, zz in zip(pairs, (z, z - way, z + way, z + 2)):
-            for j in range(2):
-                token = (zz + 4) % 4 * 4 + (xh + j) % 2 * 2 + core
-                lanes = pl.ds(pl.multiple_of(token * 128, 128), 128)
-                for r, yy in enumerate((y + 2, y - d, y + d, y)):
-                    rows = pl.ds(pl.multiple_of(((yy + 4) % 4 * 2 + half) * 128, 128), 128)
-                    turned[r * 128:(r + 1) * 128, lanes] = ref[j, rows, :]
+        for j in range(4):
+            zz = (z, z - way, z + way, z + 2)[first + j // 2]
+            token = (zz + 4) % 4 * 4 + (xh + j % 2) % 2 * 2 + core
+            lanes = pl.ds(pl.multiple_of(token * 128, 128), 128)
+            for r, dest in enumerate(dests):
+                rows = pl.ds(pl.multiple_of(((spots[dest] + 4) % 4 * 2 + half) * 128, 128), 128)
+                turned[r * 128:(r + 1) * 128, lanes] = ref[j, rows, :]
 
     @pl.loop(0, s0.shape[1] // 512)
     def _(i):
@@ -202,26 +184,27 @@
         for s, state in enumerate((s0, s1, s2)):
             product = jnp.dot(turned[...], state[:, cols], preferred_element_type=F32) * (16384 ** -0.5)
             product = product.astype(BF)
-            for r, out in enumerate((p2, pm, pp, p0)):
+            for r, out in enumerate(outs):
                 out[s, :, cols] = product[r * 128:(r + 1) * 128]
 
 
-def backward(states, masked, other):
+def backward(states, masked, other, dests):
     tokens, depth = states[0].shape
+    count = len(dests)
     out = jax.ShapeDtypeStruct((3, 128, depth), BF)
 
     def kernel(*refs):
-        backward_kernel(other, refs)
+        backward_kernel(other, dests, refs)
 
     return pl.pallas_call(
         kernel,
-        in_specs=[VMEM] * 11,
-        out_specs=[VMEM] * 4,
-        out_shape=[out] * 4,
-        scratch_shapes=[pltpu.VMEM((512, tokens), BF)],
+        in_specs=[VMEM] * 7,
+        out_specs=[VMEM] * count,
+        out_shape=[out] * count,
+        scratch_shapes=[pltpu.VMEM((128 * count, tokens), BF)],
         compiler_params=params(16),
-        cost_estimate=cost(6 * tokens * depth * 512, 6 * tokens * depth + 16 * tokens * 256),
-        name="backward_other" if other else "backward_own",
+        cost_estimate=cost(6 * tokens * depth * 128 * count, 6 * tokens * depth + 16 * tokens * 256),
+        name="backward",
     )(*masked, *states)
 
 
@@ -247,38 +230,23 @@
     )(*mine, *theirs)
 
 
-def split_kernel(a0, a1, b, c0, c1, mine, theirs):
+def split_kernel(a0, a1, b0, b1, c0, c1, mine, theirs):
     h = lax.axis_index("tp") // 2 % 2
     for out, k in ((mine, h), (theirs, (h + 1) % 2)):
-        for i, (a, c) in enumerate(((a0, c0), (a1, c1))):
-            total = a[k].astype(F32) + b[i, k].astype(F32) + c[k].astype(F32)
+        for i, (a, b, c) in enumerate(((a0, b0, c0), (a1, b1, c1))):
+            total = a[k].astype(F32) + b[k].astype(F32) + c[k].astype(F32)
             out[:, i * 512:(i + 1) * 512] = total.astype(BF)
 
 
-def split(a0, a1, b, c0, c1):
+def split(a0, a1, b0, b1, c0, c1):
     out = jax.ShapeDtypeStruct((128, 1024), BF)
     return pl.pallas_call(
         split_kernel,
         out_shape=[out] * 2,
         compiler_params=params(),
-        cost_estimate=cost(2 * b.size, 8 * b.size),
+        cost_estimate=cost(4 * b0.size, 16 * b0.size),
         name="split",
-    )(a0, a1, b, c0, c1)
-
-
-def pass_kernel(qa, ta, qb, tb, out):
-    for i, (q, t) in enumerate(((qa, ta), (qb, tb))):
-        out[i] = (q[...].astype(F32) + t[...].astype(F32)).astype(BF)
-
-
-def pass_on(qa, ta, qb, tb):
-    return pl.pallas_call(
-        pass_kernel,
-        out_shape=jax.ShapeDtypeStruct((2, *qa.shape), BF),
-        compiler_params=params(),
-        cost_estimate=cost(2 * qa.size, 12 * qa.size),
-        name="pass_on",
-    )(qa, ta, qb, tb)
+    )(a0, a1, b0, b1, c0, c1)
 
 
 def join_kernel(a, b, out):
@@ -322,62 +290,61 @@
 
 def body(low_state, mid_state, high_state, w_low, w_mid, w_high, kv_grad, loss_mask):
     states = (low_state, mid_state, high_state)
-    w = collect((w_low, w_mid, w_high))
+    w, mt = prepare((w_low, w_mid, w_high), kv_grad, loss_mask)
     a1 = send(w, Y1)
     a2 = send(w, Y2)
-    x1 = send(w, XL)
-
-    w, kv_grad = fence(w, kv_grad)
-    mt = masked_turned(kv_grad, loss_mask)
     m_h = send(mt, XH)
+    m_1 = send(mt, Z1)
     mt, *states = fence(mt, *states)
     states = load(*states)
 
-    mt, m_h, *states = fence(mt, m_h, *states)
+    mt, m_h, m_1, w, *states = fence(mt, m_h, m_1, w, *states)
+    x1 = send(w, XL)
+    h_1 = send(m_h, Z1)
     pair = jnp.stack((mt, m_h))
-    z1 = send(pair, Z1)
     z2 = send(pair, Z2)
 
-    a1, a2, pair, *states = fence(a1, a2, pair, *states)
+    a1, a2, h_1, *states = fence(a1, a2, h_1, *states)
     a3 = send(a1, Y1)
-    pair_o = send(pair, CORE)
+    z1 = jnp.stack((m_1, h_1))
+    z3 = send(z1, Z1)
     mine_a, theirs_a = forward(states, (a1, a2), True)
 
-    x1, z1, z2, pair_o, mine_a, theirs_a = fence(x1, z1, z2, pair_o, mine_a, theirs_a)
-    z3 = send(z1, Z1)
-    z1_o = send(z1, CORE)
+    x1, z2, z3, mine_a, theirs_a = fence(x1, z2, z3, mine_a, theirs_a)
+    near = jnp.concatenate((pair, z1))
+    far = jnp.concatenate((z2, z3))
+    near_o = send(near, CORE)
+    far_o = send(far, CORE)
     b1 = send(x1, Y1)
     b2 = send(x1, Y2)
     b3 = send(a3, XL)
     mine_b, theirs_b = forward(states, (w, x1), False)
-
-    z3, z1_o, z2, mine_b, theirs_b = fence(z3, z1_o, z2, mine_b, theirs_b)
-    z2_o = send(z2, CORE)
-    z3_o = send(z3, CORE)
-    masked = [pair, z1, z2, z3, pair_o, z1_o, z2_o, z3_o]
-    p2x, pmx, ppx, p0x = backward(states, masked, True)
-
-    b1, b2, b3, p2x, pmx, ppx, p0x, pair, theirs_a, theirs_b = fence(
-        b1, b2, b3, p2x, pmx, ppx, p0x, pair, theirs_a, theirs_b
+    near_o, far_o, mine_b = fence(near_o, far_o, mine_b)
+    p2x, pmx, ppx, p0x = backward(states, (near, far, near_o, far_o), True, ("far", "back", "ahead", "here"))
+    p0x, near = fence(p0x, near)
+    p2, pp = backward(states, (near, far, near_o, far_o), False, ("far", "ahead"))
+
+    b1, b2, p2, pp, p2x, pmx, ppx, p0x, near, theirs_a, theirs_b = fence(
+        b1, b2, p2, pp, p2x, pmx, ppx, p0x, near, theirs_a, theirs_b
     )
-    e1 = send(p2x, XL)
     e2 = send(pmx, Y2)
     e3 = send(ppx, Y1)
+    e1 = send(p2x, XL)
     got_a = send(theirs_a, CORE)
     got_b = send(theirs_b, CORE)
     mine_c, theirs_c = forward(states, (a3, b3), False)
     mine_d, theirs_d = forward(states, (b1, b2), True)
-    got_a, got_b, theirs_c, theirs_d, pair = fence(got_a, got_b, theirs_c, theirs_d, pair)
+    got_a, got_b, theirs_c, theirs_d, near = fence(got_a, got_b, theirs_c, theirs_d, near)
     q2a, qma, qpa, q0a = pick((mine_a, mine_b), (got_a, got_b))
     t3a = send(q2a, Z2)
     t2a = send(qpa, Z1)
-    masked = [pair, *masked[1:]]
-    p2, pm, pp, p0 = backward(states, masked, False)
+    pm, p0 = backward(states, (near, far, near_o, far_o), False, ("back", "here"))
 
     e1, e2, e3, t3a, t2a, theirs_c, theirs_d, p2, pm, pp, p0 = fence(
         e1, e2, e3, t3a, t2a, theirs_c, theirs_d, p2, pm, pp, p0
     )
     f3 = send(add(p2, e1), Y2)
+    f2 = send(pp, Y1)
     fx = send(add(p0x, e2, e3), XL)
     got_c = send(theirs_c, CORE)
     got_d = send(theirs_d, CORE)
@@ -385,13 +352,13 @@
     t3b = send(q2b, Z2)
     t2b = send(qpb, Z1)
 
-    t3b, t2b, pm, pp = fence(t3b, t2b, pm, pp)
-    t1 = send(pass_on(qma, t3a, qmb, t3b), Z2)
+    t3b, t2b, qma, qmb = fence(t3b, t2b, qma, qmb)
+    t1a = send(add(qma, t3a), Z2)
+    t1b = send(add(qmb, t3b), Z2)
     f1 = send(add(pm, f3), Y2)
-    f2 = send(pp, Y1)
-    kept, given = split(q0a, q0b, t1, t2a, t2b)
-    got, *grads = fence(send(given, XH), *finish(p0, fx, f1, f2))
-    return (join(kept, got), *grads)
+    kept, given = split(q0a, q0b, t1a, t1b, t2a, t2b)
+    keys_values = join(kept, send(given, XH))
+    return (keys_values, *finish(p0, fx, f1, f2))
 
 
 def solution(mesh):

time: 119 us -> 125 us (1.050); the launches traced: 119 us -> 123 us
  waiting for transfers between devices: 33.6 us -> 37.6 us
  starting transfers between devices: 42 us -> 43.4 us
  Pallas kernels: 41.4 us -> 40.1 us
    ppermute x32, waiting for transfers between devices: 33.6 us -> 37.6 us  [send(): return lax.ppermute(array, FULL, pairs)]
    ppermute x32, starting transfers between devices: 42 us -> 43.4 us  [send(): return lax.ppermute(array, FULL, pairs)]
    pallas_call x5 -> x4, Pallas kernels: 19 us -> 17.7 us  [the longest x3 15.5 us: backward(): pl.pallas_call(kernel, in_specs=[VMEM] * 7, out_specs=[VMEM] * count, out...]
  transfers between devices with their start and end apart: 32 -> 32, of which waited for: 13 -> 15; matrix products, arithmetic and copies ran while one was open for 1% -> 1% of each run, Pallas kernels for 32% -> 30%
where the time goes in v3:
time: 125 us; the launch traced here: 123 us
  starting transfers between devices  43.4 us (35%)
  Pallas kernels  40.1 us (32%)
  waiting for transfers between devices  37.6 us (30%)
  other arithmetic  1.42 us (1%)
    ppermute x32, starting transfers between devices, send(): return lax.ppermute(array, FULL, pairs)  43.4 us
    ppermute x32, waiting for transfers between devices, send(): return lax.ppermute(array, FULL, pairs)  37.6 us
    pallas_call x3, Pallas kernels, backward(): pl.pallas_call(kernel, in_specs=[VMEM] * 7, out_specs=[VMEM] * count, out...  15.5 us
    pallas_call x4, Pallas kernels, forward(): pl.pallas_call(kernel, in_specs=[VMEM] * 5, out_specs=[VMEM] * 2, out_sha...  14.9 us
    pallas_call x1, Pallas kernels, load(): pl.pallas_call(load_kernel, in_specs=[pl.BlockSpec(memory_space=pl.ANY)]...  4.68 us
  transfers between devices with their start and end apart: 32, of which 15 were waited for; matrix products, arithmetic and copies ran while one was open for 1% of the time, Pallas kernels for 30%

profile of v3, /device:TPU:0, one launch (start us, length us, event | category | flops | bytes accessed | tf_op | source)
XLA Modules:
  0.0 123.5 jit_solution(2100536745116832495)
XLA Ops:
  0.6 2.2 %prepare.1 = (bf16[3072,128]{1,0:T(8,128)(2,1)}, bf16[1024,128]{1,0:T(8,128)(2,1)}) custom-call(bf16[1024,128]{1,0:T(8,128)(2,1)} %w0.1, bf16[1024,128]{1,0:T(8,128)(2,1)} %w1.1, bf16[1024,128]{1,0:T(8,128)(2,1)} %w2.1, bf16[128,1024]{1,0:T(8,128)(2,1)} %grad_ref.1, s32[1,128]{1,0:T(1,128)} %bitcast.13), custom_call_target="tpu_custom_call" | custom-call | flops 131 | bytes 2097 | tf_op jit(solution)/shard_map/prepare/pallas_call | solution.py:88
  2.8 3.2 %collective-permute-start.5 = (bf16[3072,128]{1,0:T(8,128)(2,1)}, bf16[3072,128]{1,0:T(8,128)(2,1)S(1)}, u32[]{:S(2)}, u32[]{:S(2)}) collective-permute-start(bf16[3072,128]{1,0:T(8,128)(2,1)} %get-tuple-element.105.refs_3_), channel_id=1, source_target_pairs={{0,96},{1,33},{2,98},{3,35},{4,100},{5,37},{6,102},{7,39},{8,104},... | collective-permute-start | bytes 2359304 | tf_op jit(solution)/shard_map/ppermute | solution.py:36
  6.0 1.9 %collective-permute-start.1 = (bf16[1024,128]{1,0:T(8,128)(2,1)}, bf16[1024,128]{1,0:T(8,128)(2,1)S(1)}, u32[]{:S(2)}, u32[]{:S(2)}) collective-permute-start(bf16[1024,128]{1,0:T(8,128)(2,1)} %get-tuple-element.106), channel_id=1, source_target_pairs={{0,4},{1,13},{2,6},{3,15},{4,8},{5,1},{6,10},{7,3},{8,12},{9,5},{1... | collective-permute-start | bytes 786440 | tf_op jit(solution)/shard_map/ppermute | solution.py:36
  7.9 3.0 %collective-permute-start = (bf16[1024,128]{1,0:T(8,128)(2,1)}, bf16[1024,128]{1,0:T(8,128)(2,1)S(1)}, u32[]{:S(2)}, u32[]{:S(2)}) collective-permute-start(bf16[1024,128]{1,0:T(8,128)(2,1)} %get-tuple-element.106), channel_id=1, source_target_pairs={{0,2},{1,3},{2,0},{3,1},{4,6},{5,7},{6,4},{7,5},{8,10},{9,11},{10,... | collective-permute-start | bytes 786440 | tf_op jit(solution)/shard_map/ppermute | solution.py:36
  11.0 4.7 %load.1 = (bf16[2048,1024]{1,0:T(8,128)(2,1)S(1)}, bf16[2048,1024]{1,0:T(8,128)(2,1)S(1)}, bf16[2048,1024]{1,0:T(8,128)(2,1)S(1)}) custom-call(bf16[2048,1024]{1,0:T(8,128)(2,1)} %refs_0_, bf16[2048,1024]{1,0:T(8,128)(2,1)} %refs_1_, bf16[2048,1024]{1,0:T(8,128)(2,1)} %refs_2_), custom_call_target="tpu_custom_call" | custom-call | bytes 25165 | tf_op jit(solution)/shard_map/load/pallas_call | solution.py:116
  15.7 2.7 %collective-permute-done = bf16[1024,128]{1,0:T(8,128)(2,1)S(1)} collective-permute-done((bf16[1024,128]{1,0:T(8,128)(2,1)}, bf16[1024,128]{1,0:T(8,128)(2,1)S(1)}, u32[]{:S(2)}, u32[]{:S(2)}) %collective-permute-start) | collective-permute-done | bytes 262176 | tf_op jit(solution)/shard_map/ppermute | solution.py:36
  20.0 3.3 %collective-permute-start.3 = (bf16[2,1024,128]{2,1,0:T(8,128)(2,1)S(1)}, bf16[2,1024,128]{2,1,0:T(8,128)(2,1)S(1)}, u32[]{:S(2)}, u32[]{:S(2)}) collective-permute-start(bf16[2,1024,128]{2,1,0:T(8,128)(2,1)S(1)} %pad_maximum_fusion.1), channel_id=1, source_target_pairs={{0,12},{1,5},{2,14},{3,7},{4,0},{5,9},{6,2},{7,11},{8,4},{9,13},{1... | collective-permute-start | bytes 1572872 | tf_op jit(solution)/shard_map/ppermute | solution.py:36
  23.3 4.6 %collective-permute-done.6 = bf16[1024,128]{1,0:T(8,128)(2,1)S(1)} collective-permute-done((bf16[1024,128]{1,0:T(8,128)(2,1)S(1)}, bf16[1024,128]{1,0:T(8,128)(2,1)S(1)}, u32[]{:S(2)}, u32[]{:S(2)}) %collective-permute-start.6) | collective-permute-done | bytes 262176 | tf_op jit(solution)/shard_map/ppermute | solution.py:36
  29.7 3.8 %forward.4 = (bf16[4,2,128,256]{3,2,1,0:T(8,128)(2,1)S(1)}, bf16[4,2,128,256]{3,2,1,0:T(8,128)(2,1)S(1)}) custom-call(bf16[2048,1024]{1,0:T(8,128)(2,1)S(1)} %get-tuple-element.113.refs_0_.refs_4_, bf16[2048,1024]{1,0:T(8,128)(2,1)S(1)} %get-tuple-element.114.refs_1_.refs_5_, bf16[2048,1024]{1,0:T(8,128)(2,1)S(1)} %get-tuple-element.115.refs_2_.refs_6_, ...), custom_call_target="tpu_custom_call" | custom-call | flops 3221225 | bytes 14680 | tf_op jit(solution)/shard_map/forward/pallas_call | solution.py:153
  33.5 4.7 %collective-permute-done.2.refs_4_ = bf16[3072,128]{1,0:T(8,128)(2,1)S(1)} collective-permute-done((bf16[3072,128]{1,0:T(8,128)(2,1)S(1)}, bf16[3072,128]{1,0:T(8,128)(2,1)S(1)}, u32[]{:S(2)}, u32[]{:S(2)}) %collective-permute-start.2) | collective-permute-done | bytes 786464 | tf_op jit(solution)/shard_map/ppermute | solution.py:36
  38.6 3.5 %collective-permute-start.11 = (bf16[3072,128]{1,0:T(8,128)(2,1)S(1)}, bf16[3072,128]{1,0:T(8,128)(2,1)S(1)}, u32[]{:S(2)}, u32[]{:S(2)}) collective-permute-start(bf16[3072,128]{1,0:T(8,128)(2,1)S(1)} %collective-permute-done.2.refs_4_), channel_id=1, source_target_pairs={{0,96},{1,33},{2,98},{3,35},{4,100},{5,37},{6,102},{7,39},{8,104},... | collective-permute-start | bytes 2359304 | tf_op jit(solution)/shard_map/ppermute | solution.py:36
  43.8 3.7 %forward.5 = (bf16[4,2,128,256]{3,2,1,0:T(8,128)(2,1)S(1)}, bf16[4,2,128,256]{3,2,1,0:T(8,128)(2,1)S(1)}) custom-call(bf16[2048,1024]{1,0:T(8,128)(2,1)S(1)} %get-tuple-element.113.refs_0_.refs_4_, bf16[2048,1024]{1,0:T(8,128)(2,1)S(1)} %get-tuple-element.114.refs_1_.refs_5_, bf16[2048,1024]{1,0:T(8,128)(2,1)S(1)} %get-tuple-element.115.refs_2_.refs_6_, ...), custom_call_target="tpu_custom_call" | custom-call | flops 3221225 | bytes 14680 | tf_op jit(solution)/shard_map/forward/pallas_call | solution.py:153
  47.5 7.6 %backward.3 = (bf16[3,128,1024]{2,1,0:T(8,128)(2,1)S(1)}, bf16[3,128,1024]{2,1,0:T(8,128)(2,1)S(1)}, bf16[3,128,1024]{2,1,0:T(8,128)(2,1)S(1)}, bf16[3,128,1024]{2,1,0:T(8,128)(2,1)S(1)}) custom-call(bf16[4,1024,128]{2,1,0:T(8,128)(2,1)S(1)} %pad_maximum_fusion.refs_0_, bf16[4,1024,128]{2,1,0:T(8,128)(2,1)S(1)} %constant_dynamic-update-slice_fusion.refs_1_, ...), custom_call_target="tpu_custom_call" | custom-call | flops 6442450 | bytes 20971 | tf_op jit(solution)/shard_map/backward/pallas_call | solution.py:199
  55.1 4.0 %backward.4 = (bf16[3,128,1024]{2,1,0:T(8,128)(2,1)S(1)}, bf16[3,128,1024]{2,1,0:T(8,128)(2,1)S(1)}) custom-call(bf16[4,1024,128]{2,1,0:T(8,128)(2,1)S(1)} %pad_maximum_fusion.refs_0_, bf16[4,1024,128]{2,1,0:T(8,128)(2,1)S(1)} %constant_dynamic-update-slice_fusion.refs_1_, bf16[4,1024,128]{2,1,0:T(8,128)(2,1)S(1)} %collective-permute-done.8.refs_2_, ...), custom_call_target="tpu_custom_call" | custom-call | flops 3221225 | bytes 20971 | tf_op jit(solution)/shard_map/backward/pallas_call | solution.py:199
  60.8 1.9 %collective-permute-start.16 = (bf16[3,128,1024]{2,1,0:T(8,128)(2,1)S(1)}, bf16[3,128,1024]{2,1,0:T(8,128)(2,1)S(1)}, u32[]{:S(2)}, u32[]{:S(2)}) collective-permute-start(bf16[3,128,1024]{2,1,0:T(8,128)(2,1)S(1)} %get-tuple-element.150), channel_id=1, source_target_pairs={{0,16},{1,17},{2,18},{3,19},{4,20},{5,21},{6,22},{7,23},{8,24},{9,... | collective-permute-start | bytes 2359304 | tf_op jit(solution)/shard_map/ppermute | solution.py:36
  62.7 3.0 %collective-permute-start.17 = (bf16[3,128,1024]{2,1,0:T(8,128)(2,1)S(1)}, bf16[3,128,1024]{2,1,0:T(8,128)(2,1)S(1)}, u32[]{:S(2)}, u32[]{:S(2)}) collective-permute-start(bf16[3,128,1024]{2,1,0:T(8,128)(2,1)S(1)} %get-tuple-element.151), channel_id=1, source_target_pairs={{0,96},{1,33},{2,98},{3,35},{4,100},{5,37},{6,102},{7,39},{8,104},... | collective-permute-start | bytes 2359304 | tf_op jit(solution)/shard_map/ppermute | solution.py:36
  65.6 3.8 %forward.7 = (bf16[4,2,128,256]{3,2,1,0:T(8,128)(2,1)S(1)}, bf16[4,2,128,256]{3,2,1,0:T(8,128)(2,1)S(1)}) custom-call(bf16[2048,1024]{1,0:T(8,128)(2,1)S(1)} %get-tuple-element.113.refs_0_.refs_4_, bf16[2048,1024]{1,0:T(8,128)(2,1)S(1)} %get-tuple-element.114.refs_1_.refs_5_, bf16[2048,1024]{1,0:T(8,128)(2,1)S(1)} %get-tuple-element.115.refs_2_.refs_6_, ...), custom_call_target="tpu_custom_call" | custom-call | flops 3221225 | bytes 14680 | tf_op jit(solution)/shard_map/forward/pallas_call | solution.py:153
  69.4 3.7 %forward.6 = (bf16[4,2,128,256]{3,2,1,0:T(8,128)(2,1)S(1)}, bf16[4,2,128,256]{3,2,1,0:T(8,128)(2,1)S(1)}) custom-call(bf16[2048,1024]{1,0:T(8,128)(2,1)S(1)} %get-tuple-element.113.refs_0_.refs_4_, bf16[2048,1024]{1,0:T(8,128)(2,1)S(1)} %get-tuple-element.114.refs_1_.refs_5_, bf16[2048,1024]{1,0:T(8,128)(2,1)S(1)} %get-tuple-element.115.refs_2_.refs_6_, ...), custom_call_target="tpu_custom_call" | custom-call | flops 3221225 | bytes 14680 | tf_op jit(solution)/shard_map/forward/pallas_call | solution.py:153
  75.5 3.9 %backward.5 = (bf16[3,128,1024]{2,1,0:T(8,128)(2,1)S(1)}, bf16[3,128,1024]{2,1,0:T(8,128)(2,1)S(1)}) custom-call(bf16[4,1024,128]{2,1,0:T(8,128)(2,1)S(1)} %pad_maximum_fusion.refs_0_, bf16[4,1024,128]{2,1,0:T(8,128)(2,1)S(1)} %constant_dynamic-update-slice_fusion.refs_1_, bf16[4,1024,128]{2,1,0:T(8,128)(2,1)S(1)} %collective-permute-done.8.refs_2_, ...), custom_call_target="tpu_custom_call" | custom-call | flops 3221225 | bytes 20971 | tf_op jit(solution)/shard_map/backward/pallas_call | solution.py:199
  80.4 2.0 %collective-permute-done.17 = bf16[3,128,1024]{2,1,0:T(8,128)(2,1)S(1)} collective-permute-done((bf16[3,128,1024]{2,1,0:T(8,128)(2,1)S(1)}, bf16[3,128,1024]{2,1,0:T(8,128)(2,1)S(1)}, u32[]{:S(2)}, u32[]{:S(2)}) %collective-permute-start.17) | collective-permute-done | bytes 786464 | tf_op jit(solution)/shard_map/ppermute | solution.py:36
  83.9 3.1 %collective-permute-start.29 = (bf16[3,128,1024]{2,1,0:T(8,128)(2,1)S(1)}, bf16[3,128,1024]{2,1,0:T(8,128)(2,1)S(1)}, u32[]{:S(2)}, u32[]{:S(2)}) collective-permute-start(bf16[3,128,1024]{2,1,0:T(8,128)(2,1)S(1)} %add_convert_fusion.1), channel_id=1, source_target_pairs={{0,96},{1,33},{2,98},{3,35},{4,100},{5,37},{6,102},{7,39},{8,104},... | collective-permute-start | bytes 2359304 | tf_op jit(solution)/shard_map/ppermute | solution.py:36
  87.3 2.0 %collective-permute-start.23 = (bf16[2,128,512]{2,1,0:T(8,128)(2,1)S(1)}, bf16[2,128,512]{2,1,0:T(8,128)(2,1)S(1)}, u32[]{:S(2)}, u32[]{:S(2)}) collective-permute-start(bf16[2,128,512]{2,1,0:T(8,128)(2,1)S(1)} %get-tuple-element.165), channel_id=1, source_target_pairs={{0,12},{1,5},{2,14},{3,7},{4,0},{5,9},{6,2},{7,11},{8,4},{9,13},{1... | collective-permute-start | bytes 786440 | tf_op jit(solution)/shard_map/ppermute | solution.py:36
  89.8 1.8 %collective-permute-start.28 = (bf16[3,128,1024]{2,1,0:T(8,128)(2,1)S(1)}, bf16[3,128,1024]{2,1,0:T(8,128)(2,1)S(1)}, u32[]{:S(2)}, u32[]{:S(2)}) collective-permute-start(bf16[3,128,1024]{2,1,0:T(8,128)(2,1)S(1)} %add_convert_fusion.2), channel_id=1, source_target_pairs={{0,16},{1,17},{2,18},{3,19},{4,20},{5,21},{6,22},{7,23},{8,24},{9,... | collective-permute-start | bytes 2359304 | tf_op jit(solution)/shard_map/ppermute | solution.py:36
  91.6 3.3 %collective-permute-done.23 = bf16[2,128,512]{2,1,0:T(8,128)(2,1)S(1)} collective-permute-done((bf16[2,128,512]{2,1,0:T(8,128)(2,1)S(1)}, bf16[2,128,512]{2,1,0:T(8,128)(2,1)S(1)}, u32[]{:S(2)}, u32[]{:S(2)}) %collective-permute-start.23) | collective-permute-done | bytes 262176 | tf_op jit(solution)/shard_map/ppermute | solution.py:36
  94.9 2.0 %collective-permute-done.24.c1 = bf16[2,128,512]{2,1,0:T(8,128)(2,1)S(1)} collective-permute-done((bf16[2,128,512]{2,1,0:T(8,128)(2,1)S(1)}, bf16[2,128,512]{2,1,0:T(8,128)(2,1)S(1)}, u32[]{:S(2)}, u32[]{:S(2)}) %collective-permute-start.24) | collective-permute-done | bytes 262176 | tf_op jit(solution)/shard_map/ppermute | solution.py:36
  96.8 3.0 %collective-permute-done.29 = bf16[3,128,1024]{2,1,0:T(8,128)(2,1)S(1)} collective-permute-done((bf16[3,128,1024]{2,1,0:T(8,128)(2,1)S(1)}, bf16[3,128,1024]{2,1,0:T(8,128)(2,1)S(1)}, u32[]{:S(2)}, u32[]{:S(2)}) %collective-permute-start.29) | collective-permute-done | bytes 786464 | tf_op jit(solution)/shard_map/ppermute | solution.py:36
  100.1 3.8 %collective-permute-start.30 = (bf16[3,128,1024]{2,1,0:T(8,128)(2,1)S(1)}, bf16[3,128,1024]{2,1,0:T(8,128)(2,1)S(1)}, u32[]{:S(2)}, u32[]{:S(2)}) collective-permute-start(bf16[3,128,1024]{2,1,0:T(8,128)(2,1)S(1)} %add_convert_fusion), channel_id=1, source_target_pairs={{0,96},{1,33},{2,98},{3,35},{4,100},{5,37},{6,102},{7,39},{8,104},... | collective-permute-start | bytes 2359304 | tf_op jit(solution)/shard_map/ppermute | solution.py:36
  103.9 2.3 %collective-permute-start.26 = (bf16[2,128,512]{2,1,0:T(8,128)(2,1)S(1)}, bf16[2,128,512]{2,1,0:T(8,128)(2,1)S(1)}, u32[]{:S(2)}, u32[]{:S(2)}) collective-permute-start(bf16[2,128,512]{2,1,0:T(8,128)(2,1)S(1)} %add_convert_fusion.3), channel_id=1, source_target_pairs={{0,12},{1,5},{2,14},{3,7},{4,0},{5,9},{6,2},{7,11},{8,4},{9,13},{1... | collective-permute-start | bytes 786440 | tf_op jit(solution)/shard_map/ppermute | solution.py:36
  106.4 4.0 %collective-permute-done.26.b1 = bf16[2,128,512]{2,1,0:T(8,128)(2,1)S(1)} collective-permute-done((bf16[2,128,512]{2,1,0:T(8,128)(2,1)S(1)}, bf16[2,128,512]{2,1,0:T(8,128)(2,1)S(1)}, u32[]{:S(2)}, u32[]{:S(2)}) %collective-permute-start.26) | collective-permute-done | bytes 262176 | tf_op jit(solution)/shard_map/ppermute | solution.py:36
  110.4 2.8 %collective-permute-done.25.b0 = bf16[2,128,512]{2,1,0:T(8,128)(2,1)S(1)} collective-permute-done((bf16[2,128,512]{2,1,0:T(8,128)(2,1)S(1)}, bf16[2,128,512]{2,1,0:T(8,128)(2,1)S(1)}, u32[]{:S(2)}, u32[]{:S(2)}) %collective-permute-start.25) | collective-permute-done | bytes 262176 | tf_op jit(solution)/shard_map/ppermute | solution.py:36
  113.4 2.6 %collective-permute-start.27 = (bf16[128,1024]{1,0:T(8,128)(2,1)S(1)}, bf16[128,1024]{1,0:T(8,128)(2,1)S(1)}, u32[]{:S(2)}, u32[]{:S(2)}) collective-permute-start(bf16[128,1024]{1,0:T(8,128)(2,1)S(1)} %get-tuple-element.176), channel_id=1, source_target_pairs={{0,2},{1,3},{2,0},{3,1},{4,6},{5,7},{6,4},{7,5},{8,10},{9,11},{10,... | collective-permute-start | bytes 786440 | tf_op jit(solution)/shard_map/ppermute | solution.py:36
  116.0 5.4 %collective-permute-done.27.b = bf16[128,1024]{1,0:T(8,128)(2,1)S(1)} collective-permute-done((bf16[128,1024]{1,0:T(8,128)(2,1)S(1)}, bf16[128,1024]{1,0:T(8,128)(2,1)S(1)}, u32[]{:S(2)}, u32[]{:S(2)}) %collective-permute-start.27) | collective-permute-done | bytes 262176 | tf_op jit(solution)/shard_map/ppermute | solution.py:36
  (60 shorter events, 15.6 us)
Async XLA Ops:
  2.8 25.0 %collective-permute-start.5 = (bf16[3072,128]{1,0:T(8,128)(2,1)}, bf16[3072,128]{1,0:T(8,128)(2,1)S(1)}, u32[]{:S(2)}, u32[]{:S(2)}) collective-permute-start(bf16[3072,128]{1,0:T(8,128)(2,1)} %get-tuple-element.105.refs_3_), channel_id=1, source_target_pairs={{0,96},{1,33},{2,98},{3,35},{4,100},{5,37},{6,102},{7,39},{8,104},... | collective-permute-start | bytes 2359304 | tf_op jit(solution)/shard_map/ppermute | solution.py:36
  6.0 21.9 %collective-permute-start.4 = (bf16[3072,128]{1,0:T(8,128)(2,1)}, bf16[3072,128]{1,0:T(8,128)(2,1)S(1)}, u32[]{:S(2)}, u32[]{:S(2)}) collective-permute-start(bf16[3072,128]{1,0:T(8,128)(2,1)} %get-tuple-element.105.refs_3_), channel_id=1, source_target_pairs={{0,32},{1,97},{2,34},{3,99},{4,36},{5,101},{6,38},{7,103},{8,40},{... | collective-permute-start | bytes 2359304 | tf_op jit(solution)/shard_map/ppermute | solution.py:36
  6.0 9.6 %collective-permute-start.1 = (bf16[1024,128]{1,0:T(8,128)(2,1)}, bf16[1024,128]{1,0:T(8,128)(2,1)S(1)}, u32[]{:S(2)}, u32[]{:S(2)}) collective-permute-start(bf16[1024,128]{1,0:T(8,128)(2,1)} %get-tuple-element.106), channel_id=1, source_target_pairs={{0,4},{1,13},{2,6},{3,15},{4,8},{5,1},{6,10},{7,3},{8,12},{9,5},{1... | collective-permute-start | bytes 786440 | tf_op jit(solution)/shard_map/ppermute | solution.py:36
  7.9 10.5 %collective-permute-start = (bf16[1024,128]{1,0:T(8,128)(2,1)}, bf16[1024,128]{1,0:T(8,128)(2,1)S(1)}, u32[]{:S(2)}, u32[]{:S(2)}) collective-permute-start(bf16[1024,128]{1,0:T(8,128)(2,1)} %get-tuple-element.106), channel_id=1, source_target_pairs={{0,2},{1,3},{2,0},{3,1},{4,6},{5,7},{6,4},{7,5},{8,10},{9,11},{10,... | collective-permute-start | bytes 786440 | tf_op jit(solution)/shard_map/ppermute | solution.py:36
  18.4 9.5 %collective-permute-start.6 = (bf16[1024,128]{1,0:T(8,128)(2,1)S(1)}, bf16[1024,128]{1,0:T(8,128)(2,1)S(1)}, u32[]{:S(2)}, u32[]{:S(2)}) collective-permute-start(bf16[1024,128]{1,0:T(8,128)(2,1)S(1)} %collective-permute-done), channel_id=1, source_target_pairs={{0,4},{1,13},{2,6},{3,15},{4,8},{5,1},{6,10},{7,3},{8,12},{9,5},{1... | collective-permute-start | bytes 786440 | tf_op jit(solution)/shard_map/ppermute | solution.py:36
  18.4 19.7 %collective-permute-start.2 = (bf16[3072,128]{1,0:T(8,128)(2,1)S(1)}, bf16[3072,128]{1,0:T(8,128)(2,1)S(1)}, u32[]{:S(2)}, u32[]{:S(2)}) collective-permute-start(bf16[3072,128]{1,0:T(8,128)(2,1)S(1)} %copy-done), channel_id=1, source_target_pairs={{0,16},{1,17},{2,18},{3,19},{4,20},{5,21},{6,22},{7,23},{8,24},{9,... | collective-permute-start | bytes 2359304 | tf_op jit(solution)/shard_map/ppermute | solution.py:36
  20.0 13.5 %collective-permute-start.3 = (bf16[2,1024,128]{2,1,0:T(8,128)(2,1)S(1)}, bf16[2,1024,128]{2,1,0:T(8,128)(2,1)S(1)}, u32[]{:S(2)}, u32[]{:S(2)}) collective-permute-start(bf16[2,1024,128]{2,1,0:T(8,128)(2,1)S(1)} %pad_maximum_fusion.1), channel_id=1, source_target_pairs={{0,12},{1,5},{2,14},{3,7},{4,0},{5,9},{6,2},{7,11},{8,4},{9,13},{1... | collective-permute-start | bytes 1572872 | tf_op jit(solution)/shard_map/ppermute | solution.py:36
  27.9 10.5 %collective-permute-start.7 = (bf16[2,1024,128]{2,1,0:T(8,128)(2,1)S(1)}, bf16[2,1024,128]{2,1,0:T(8,128)(2,1)S(1)}, u32[]{:S(2)}, u32[]{:S(2)}) collective-permute-start(bf16[2,1024,128]{2,1,0:T(8,128)(2,1)S(1)} %pad_maximum_fusion.2), channel_id=1, source_target_pairs={{0,4},{1,13},{2,6},{3,15},{4,8},{5,1},{6,10},{7,3},{8,12},{9,5},{1... | collective-permute-start | bytes 1572872 | tf_op jit(solution)/shard_map/ppermute | solution.py:36
  28.0 14.1 %collective-permute-start.14 = (bf16[3072,128]{1,0:T(8,128)(2,1)S(1)}, bf16[3072,128]{1,0:T(8,128)(2,1)S(1)}, u32[]{:S(2)}, u32[]{:S(2)}) collective-permute-start(bf16[3072,128]{1,0:T(8,128)(2,1)S(1)} %collective-permute-done.4.refs_3_), channel_id=1, source_target_pairs={{0,32},{1,97},{2,34},{3,99},{4,36},{5,101},{6,38},{7,103},{8,40},{... | collective-permute-start | bytes 2359304 | tf_op jit(solution)/shard_map/ppermute | solution.py:36
  29.6 17.9 %collective-permute-start.8 = (bf16[4,1024,128]{2,1,0:T(8,128)(2,1)S(1)}, bf16[4,1024,128]{2,1,0:T(8,128)(2,1)S(1)}, u32[]{:S(2)}, u32[]{:S(2)}) collective-permute-start(bf16[4,1024,128]{2,1,0:T(8,128)(2,1)S(1)} %pad_maximum_fusion.refs_0_), channel_id=1, source_target_pairs={{0,1},{1,0},{2,3},{3,2},{4,5},{5,4},{6,7},{7,6},{8,9},{9,8},{10,11... | collective-permute-start | bytes 3145736 | tf_op jit(solution)/shard_map/ppermute | solution.py:36
  38.5 8.9 %collective-permute-start.9 = (bf16[4,1024,128]{2,1,0:T(8,128)(2,1)S(1)}, bf16[4,1024,128]{2,1,0:T(8,128)(2,1)S(1)}, u32[]{:S(2)}, u32[]{:S(2)}) collective-permute-start(bf16[4,1024,128]{2,1,0:T(8,128)(2,1)S(1)} %constant_dynamic-update-slice_fusion.refs_1_), channel_id=1, source_target_pairs={{0,1},{1,0},{2,3},{3,2},{4,5},{5,4},{6,7},{7,6},{8,9},{9,8},{10,11... | collective-permute-start | bytes 3145736 | tf_op jit(solution)/shard_map/ppermute | solution.py:36
  38.6 21.0 %collective-permute-start.11 = (bf16[3072,128]{1,0:T(8,128)(2,1)S(1)}, bf16[3072,128]{1,0:T(8,128)(2,1)S(1)}, u32[]{:S(2)}, u32[]{:S(2)}) collective-permute-start(bf16[3072,128]{1,0:T(8,128)(2,1)S(1)} %collective-permute-done.2.refs_4_), channel_id=1, source_target_pairs={{0,96},{1,33},{2,98},{3,35},{4,100},{5,37},{6,102},{7,39},{8,104},... | collective-permute-start | bytes 2359304 | tf_op jit(solution)/shard_map/ppermute | solution.py:36
  42.2 18.1 %collective-permute-start.10 = (bf16[3072,128]{1,0:T(8,128)(2,1)S(1)}, bf16[3072,128]{1,0:T(8,128)(2,1)S(1)}, u32[]{:S(2)}, u32[]{:S(2)}) collective-permute-start(bf16[3072,128]{1,0:T(8,128)(2,1)S(1)} %collective-permute-done.2.refs_4_), channel_id=1, source_target_pairs={{0,32},{1,97},{2,34},{3,99},{4,36},{5,101},{6,38},{7,103},{8,40},{... | collective-permute-start | bytes 2359304 | tf_op jit(solution)/shard_map/ppermute | solution.py:36
  42.2 23.5 %collective-permute-start.15 = (bf16[3072,128]{1,0:T(8,128)(2,1)S(1)}, bf16[3072,128]{1,0:T(8,128)(2,1)S(1)}, u32[]{:S(2)}, u32[]{:S(2)}) collective-permute-start(bf16[3072,128]{1,0:T(8,128)(2,1)S(1)} %collective-permute-done.14.refs_3_), channel_id=1, source_target_pairs={{0,16},{1,17},{2,18},{3,19},{4,20},{5,21},{6,22},{7,23},{8,24},{9,... | collective-permute-start | bytes 2359304 | tf_op jit(solution)/shard_map/ppermute | solution.py:36
  60.3 12.8 %collective-permute-start.12 = (bf16[4,2,128,256]{3,2,1,0:T(8,128)(2,1)S(1)}, bf16[4,2,128,256]{3,2,1,0:T(8,128)(2,1)S(1)}, u32[]{:S(2)}, u32[]{:S(2)}) collective-permute-start(bf16[4,2,128,256]{3,2,1,0:T(8,128)(2,1)S(1)} %get-tuple-element.138), channel_id=1, source_target_pairs={{0,1},{1,0},{2,3},{3,2},{4,5},{5,4},{6,7},{7,6},{8,9},{9,8},{10,11... | collective-permute-start | bytes 1572872 | tf_op jit(solution)/shard_map/ppermute | solution.py:36
  60.3 12.8 %collective-permute-start.13 = (bf16[4,2,128,256]{3,2,1,0:T(8,128)(2,1)S(1)}, bf16[4,2,128,256]{3,2,1,0:T(8,128)(2,1)S(1)}, u32[]{:S(2)}, u32[]{:S(2)}) collective-permute-start(bf16[4,2,128,256]{3,2,1,0:T(8,128)(2,1)S(1)} %get-tuple-element.139), channel_id=1, source_target_pairs={{0,1},{1,0},{2,3},{3,2},{4,5},{5,4},{6,7},{7,6},{8,9},{9,8},{10,11... | collective-permute-start | bytes 1572872 | tf_op jit(solution)/shard_map/ppermute | solution.py:36
  60.8 19.6 %collective-permute-start.16 = (bf16[3,128,1024]{2,1,0:T(8,128)(2,1)S(1)}, bf16[3,128,1024]{2,1,0:T(8,128)(2,1)S(1)}, u32[]{:S(2)}, u32[]{:S(2)}) collective-permute-start(bf16[3,128,1024]{2,1,0:T(8,128)(2,1)S(1)} %get-tuple-element.150), channel_id=1, source_target_pairs={{0,16},{1,17},{2,18},{3,19},{4,20},{5,21},{6,22},{7,23},{8,24},{9,... | collective-permute-start | bytes 2359304 | tf_op jit(solution)/shard_map/ppermute | solution.py:36
  62.7 19.7 %collective-permute-start.17 = (bf16[3,128,1024]{2,1,0:T(8,128)(2,1)S(1)}, bf16[3,128,1024]{2,1,0:T(8,128)(2,1)S(1)}, u32[]{:S(2)}, u32[]{:S(2)}) collective-permute-start(bf16[3,128,1024]{2,1,0:T(8,128)(2,1)S(1)} %get-tuple-element.151), channel_id=1, source_target_pairs={{0,96},{1,33},{2,98},{3,35},{4,100},{5,37},{6,102},{7,39},{8,104},... | collective-permute-start | bytes 2359304 | tf_op jit(solution)/shard_map/ppermute | solution.py:36
  65.6 17.4 %collective-permute-start.18 = (bf16[3,128,1024]{2,1,0:T(8,128)(2,1)S(1)}, bf16[3,128,1024]{2,1,0:T(8,128)(2,1)S(1)}, u32[]{:S(2)}, u32[]{:S(2)}) collective-permute-start(bf16[3,128,1024]{2,1,0:T(8,128)(2,1)S(1)} %get-tuple-element.152), channel_id=1, source_target_pairs={{0,32},{1,97},{2,34},{3,99},{4,36},{5,101},{6,38},{7,103},{8,40},{... | collective-permute-start | bytes 2359304 | tf_op jit(solution)/shard_map/ppermute | solution.py:36
  73.4 9.7 %collective-permute-start.19 = (bf16[2,128,512]{2,1,0:T(8,128)(2,1)S(1)}, bf16[2,128,512]{2,1,0:T(8,128)(2,1)S(1)}, u32[]{:S(2)}, u32[]{:S(2)}) collective-permute-start(bf16[2,128,512]{2,1,0:T(8,128)(2,1)S(1)} %get-tuple-element.153), channel_id=1, source_target_pairs={{0,12},{1,5},{2,14},{3,7},{4,0},{5,9},{6,2},{7,11},{8,4},{9,13},{1... | collective-permute-start | bytes 786440 | tf_op jit(solution)/shard_map/ppermute | solution.py:36
  74.5 8.5 %collective-permute-start.20 = (bf16[2,128,512]{2,1,0:T(8,128)(2,1)S(1)}, bf16[2,128,512]{2,1,0:T(8,128)(2,1)S(1)}, u32[]{:S(2)}, u32[]{:S(2)}) collective-permute-start(bf16[2,128,512]{2,1,0:T(8,128)(2,1)S(1)} %get-tuple-element.154), channel_id=1, source_target_pairs={{0,4},{1,13},{2,6},{3,15},{4,8},{5,1},{6,10},{7,3},{8,12},{9,5},{1... | collective-permute-start | bytes 786440 | tf_op jit(solution)/shard_map/ppermute | solution.py:36
  83.1 3.9 %collective-permute-start.21 = (bf16[4,2,128,256]{3,2,1,0:T(8,128)(2,1)S(1)}, bf16[4,2,128,256]{3,2,1,0:T(8,128)(2,1)S(1)}, u32[]{:S(2)}, u32[]{:S(2)}) collective-permute-start(bf16[4,2,128,256]{3,2,1,0:T(8,128)(2,1)S(1)} %get-tuple-element.162), channel_id=1, source_target_pairs={{0,1},{1,0},{2,3},{3,2},{4,5},{5,4},{6,7},{7,6},{8,9},{9,8},{10,11... | collective-permute-start | bytes 1572872 | tf_op jit(solution)/shard_map/ppermute | solution.py:36
  83.1 3.9 %collective-permute-start.22 = (bf16[4,2,128,256]{3,2,1,0:T(8,128)(2,1)S(1)}, bf16[4,2,128,256]{3,2,1,0:T(8,128)(2,1)S(1)}, u32[]{:S(2)}, u32[]{:S(2)}) collective-permute-start(bf16[4,2,128,256]{3,2,1,0:T(8,128)(2,1)S(1)} %get-tuple-element.163), channel_id=1, source_target_pairs={{0,1},{1,0},{2,3},{3,2},{4,5},{5,4},{6,7},{7,6},{8,9},{9,8},{10,11... | collective-permute-start | bytes 1572872 | tf_op jit(solution)/shard_map/ppermute | solution.py:36
  83.9 15.9 %collective-permute-start.29 = (bf16[3,128,1024]{2,1,0:T(8,128)(2,1)S(1)}, bf16[3,128,1024]{2,1,0:T(8,128)(2,1)S(1)}, u32[]{:S(2)}, u32[]{:S(2)}) collective-permute-start(bf16[3,128,1024]{2,1,0:T(8,128)(2,1)S(1)} %add_convert_fusion.1), channel_id=1, source_target_pairs={{0,96},{1,33},{2,98},{3,35},{4,100},{5,37},{6,102},{7,39},{8,104},... | collective-permute-start | bytes 2359304 | tf_op jit(solution)/shard_map/ppermute | solution.py:36
  87.3 7.6 %collective-permute-start.23 = (bf16[2,128,512]{2,1,0:T(8,128)(2,1)S(1)}, bf16[2,128,512]{2,1,0:T(8,128)(2,1)S(1)}, u32[]{:S(2)}, u32[]{:S(2)}) collective-permute-start(bf16[2,128,512]{2,1,0:T(8,128)(2,1)S(1)} %get-tuple-element.165), channel_id=1, source_target_pairs={{0,12},{1,5},{2,14},{3,7},{4,0},{5,9},{6,2},{7,11},{8,4},{9,13},{1... | collective-permute-start | bytes 786440 | tf_op jit(solution)/shard_map/ppermute | solution.py:36
  89.3 7.6 %collective-permute-start.24 = (bf16[2,128,512]{2,1,0:T(8,128)(2,1)S(1)}, bf16[2,128,512]{2,1,0:T(8,128)(2,1)S(1)}, u32[]{:S(2)}, u32[]{:S(2)}) collective-permute-start(bf16[2,128,512]{2,1,0:T(8,128)(2,1)S(1)} %get-tuple-element.166), channel_id=1, source_target_pairs={{0,4},{1,13},{2,6},{3,15},{4,8},{5,1},{6,10},{7,3},{8,12},{9,5},{1... | collective-permute-start | bytes 786440 | tf_op jit(solution)/shard_map/ppermute | solution.py:36
  89.8 32.4 %collective-permute-start.28 = (bf16[3,128,1024]{2,1,0:T(8,128)(2,1)S(1)}, bf16[3,128,1024]{2,1,0:T(8,128)(2,1)S(1)}, u32[]{:S(2)}, u32[]{:S(2)}) collective-permute-start(bf16[3,128,1024]{2,1,0:T(8,128)(2,1)S(1)} %add_convert_fusion.2), channel_id=1, source_target_pairs={{0,16},{1,17},{2,18},{3,19},{4,20},{5,21},{6,22},{7,23},{8,24},{9,... | collective-permute-start | bytes 2359304 | tf_op jit(solution)/shard_map/ppermute | solution.py:36
  91.6 30.6 %collective-permute-start.31 = (bf16[3,128,1024]{2,1,0:T(8,128)(2,1)S(1)}, bf16[3,128,1024]{2,1,0:T(8,128)(2,1)S(1)}, u32[]{:S(2)}, u32[]{:S(2)}) collective-permute-start(bf16[3,128,1024]{2,1,0:T(8,128)(2,1)S(1)} %get-tuple-element.184), channel_id=1, source_target_pairs={{0,32},{1,97},{2,34},{3,99},{4,36},{5,101},{6,38},{7,103},{8,40},{... | collective-permute-start | bytes 2359304 | tf_op jit(solution)/shard_map/ppermute | solution.py:36
  100.1 22.1 %collective-permute-start.30 = (bf16[3,128,1024]{2,1,0:T(8,128)(2,1)S(1)}, bf16[3,128,1024]{2,1,0:T(8,128)(2,1)S(1)}, u32[]{:S(2)}, u32[]{:S(2)}) collective-permute-start(bf16[3,128,1024]{2,1,0:T(8,128)(2,1)S(1)} %add_convert_fusion), channel_id=1, source_target_pairs={{0,96},{1,33},{2,98},{3,35},{4,100},{5,37},{6,102},{7,39},{8,104},... | collective-permute-start | bytes 2359304 | tf_op jit(solution)/shard_map/ppermute | solution.py:36
  103.9 6.4 %collective-permute-start.26 = (bf16[2,128,512]{2,1,0:T(8,128)(2,1)S(1)}, bf16[2,128,512]{2,1,0:T(8,128)(2,1)S(1)}, u32[]{:S(2)}, u32[]{:S(2)}) collective-permute-start(bf16[2,128,512]{2,1,0:T(8,128)(2,1)S(1)} %add_convert_fusion.3), channel_id=1, source_target_pairs={{0,12},{1,5},{2,14},{3,7},{4,0},{5,9},{6,2},{7,11},{8,4},{9,13},{1... | collective-permute-start | bytes 786440 | tf_op jit(solution)/shard_map/ppermute | solution.py:36
  106.3 6.9 %collective-permute-start.25 = (bf16[2,128,512]{2,1,0:T(8,128)(2,1)S(1)}, bf16[2,128,512]{2,1,0:T(8,128)(2,1)S(1)}, u32[]{:S(2)}, u32[]{:S(2)}) collective-permute-start(bf16[2,128,512]{2,1,0:T(8,128)(2,1)S(1)} %add_convert_fusion.4), channel_id=1, source_target_pairs={{0,12},{1,5},{2,14},{3,7},{4,0},{5,9},{6,2},{7,11},{8,4},{9,13},{1... | collective-permute-start | bytes 786440 | tf_op jit(solution)/shard_map/ppermute | solution.py:36
  113.4 8.0 %collective-permute-start.27 = (bf16[128,1024]{1,0:T(8,128)(2,1)S(1)}, bf16[128,1024]{1,0:T(8,128)(2,1)S(1)}, u32[]{:S(2)}, u32[]{:S(2)}) collective-permute-start(bf16[128,1024]{1,0:T(8,128)(2,1)S(1)} %get-tuple-element.176), channel_id=1, source_target_pairs={{0,2},{1,3},{2,0},{3,1},{4,6},{5,7},{6,4},{7,5},{8,10},{9,11},{10,... | collective-permute-start | bytes 786440 | tf_op jit(solution)/shard_map/ppermute | solution.py:36
  (2 other events, 26.3 us)

commit v4 on v3

--- a/solution.py
+++ b/solution.py
@@ -125,10 +125,10 @@
     )(*arrays)
 
 
-def forward_kernel(swap, s0, s1, s2, wa, wb, mine_ref, theirs_ref, w_all):
+def forward_kernel(s0, s1, s2, wa, wb, mine_ref, theirs_ref, w_all):
     c = lax.axis_index("tp") % 2
-    for i, w in ((c, wa), (1 - c, wb)) if swap else ((0, wa), (1, wb)):
-        w_all[:, pl.ds(pl.multiple_of(i * 128, 128), 128)] = w[...]
+    w_all[:, 0:128] = wa[...]
+    w_all[:, 128:256] = wb[...]
     depth = s0.shape[1]
     total = jnp.dot(s0[...], w_all[0:depth, :], preferred_element_type=F32)
     total += jnp.dot(s1[...], w_all[depth:2 * depth, :], preferred_element_type=F32)
@@ -143,15 +143,12 @@
             theirs_ref[z, h] = jnp.where(c == 0, second, first)
 
 
-def forward(states, blocks, swap):
+def forward(states, blocks):
     tokens, depth = states[0].shape
     out = jax.ShapeDtypeStruct((4, 2, 128, 256), BF)
 
-    def kernel(*refs):
-        forward_kernel(swap, *refs)
-
-    return pl.pallas_call(
-        kernel,
+    return pl.pallas_call(
+        forward_kernel,
         in_specs=[VMEM] * 5,
         out_specs=[VMEM] * 2,
         out_shape=[out, out],
@@ -163,16 +160,20 @@
 
 
 def backward_kernel(other, dests, refs):
-    near, far, near_o, far_o, s0, s1, s2 = refs[:7]
-    outs, turned = refs[7:-1], refs[-1]
+    mine, theirs, (s0, s1, s2) = refs[:3], refs[3:6], refs[6:9]
+    outs, turned = refs[9:-1], refs[-1]
     y, xl, z, xh, c, d = place()
     half = (xl + 1) % 2 if other else xl
     spots = {"far": y + 2, "back": y - d, "ahead": y + d, "here": y}
-    for ref, core, first in ((near, c, 0), (far, c, 2), (near_o, 1 - c, 0), (far_o, 1 - c, 2)):
+    for pieces, core in ((mine, c), (theirs, 1 - c)):
         way = 1 - 2 * core
-        for j in range(4):
-            zz = (z, z - way, z + way, z + 2)[first + j // 2]
-            token = (zz + 4) % 4 * 4 + (xh + j % 2) % 2 * 2 + core
+        beside = ((z - way, xh), (z + way, xh))
+        middle = ((z, xh), (z, xh + 1), (z - way, xh + 1), (z + way, xh + 1))
+        across = ((z + 2, xh), (z + 2, xh + 1))
+        for ref, j, (zz, hh) in (
+            (ref, j, at) for ref, ats in zip(pieces, (beside, middle, across)) for j, at in enumerate(ats)
+        ):
+            token = (zz + 4) % 4 * 4 + hh % 2 * 2 + core
             lanes = pl.ds(pl.multiple_of(token * 128, 128), 128)
             for r, dest in enumerate(dests):
                 rows = pl.ds(pl.multiple_of(((spots[dest] + 4) % 4 * 2 + half) * 128, 128), 128)
@@ -198,7 +199,7 @@
 
     return pl.pallas_call(
         kernel,
-        in_specs=[VMEM] * 7,
+        in_specs=[VMEM] * 9,
         out_specs=[VMEM] * count,
         out_shape=[out] * count,
         scratch_shapes=[pltpu.VMEM((128 * count, tokens), BF)],
@@ -208,21 +209,28 @@
     )(*masked, *states)
 
 
-def pick_kernel(*refs):
+def pick_kernel(sums, refs):
     _, _, z, _, _, d = place()
     count = (len(refs) - 4) // 2
+    mine, theirs = refs[:count], refs[count:2 * count]
     for out, zz in zip(refs[2 * count:], (z + 2, z - d, z + d, z)):
         k = (zz + 4) % 4
-        for i in range(count):
-            total = refs[i][k].astype(F32) + refs[count + i][k].astype(F32)
-            out[:, :, i * 256:(i + 1) * 256] = total.astype(BF)
-
-
-def pick(mine, theirs):
+        for i, (m, m_half, t, t_half) in enumerate(sums):
+            m_cut = slice(m_half * 128, m_half * 128 + 128)
+            t_cut = slice(t_half * 128, t_half * 128 + 128)
+            total = mine[m][k, :, :, m_cut].astype(F32) + theirs[t][k, :, :, t_cut].astype(F32)
+            out[:, :, i * 128:(i + 1) * 128] = total.astype(BF)
+
+
+def pick(sums, mine, theirs):
     size = sum(a.size for a in mine)
-    out = jax.ShapeDtypeStruct((2, 128, 256 * len(mine)), BF)
-    return pl.pallas_call(
-        pick_kernel,
+    out = jax.ShapeDtypeStruct((2, 128, 128 * len(sums)), BF)
+
+    def kernel(*refs):
+        pick_kernel(sums, refs)
+
+    return pl.pallas_call(
+        kernel,
         out_shape=[out] * 4,
         compiler_params=params(),
         cost_estimate=cost(size, 6 * size),
@@ -230,30 +238,50 @@
     )(*mine, *theirs)
 
 
-def split_kernel(a0, a1, b0, b1, c0, c1, mine, theirs):
+def split_kernel(a0, a1, b, c0, c1, mine, theirs):
     h = lax.axis_index("tp") // 2 % 2
     for out, k in ((mine, h), (theirs, (h + 1) % 2)):
-        for i, (a, b, c) in enumerate(((a0, b0, c0), (a1, b1, c1))):
-            total = a[k].astype(F32) + b[k].astype(F32) + c[k].astype(F32)
-            out[:, i * 512:(i + 1) * 512] = total.astype(BF)
-
-
-def split(a0, a1, b0, b1, c0, c1):
-    out = jax.ShapeDtypeStruct((128, 1024), BF)
+        at = 0
+        for a, c in ((a0, c0), (a1, c1)):
+            cut = slice(at, at + a.shape[2])
+            at += a.shape[2]
+            out[:, cut] = (a[k].astype(F32) + b[k, :, cut].astype(F32) + c[k].astype(F32)).astype(BF)
+
+
+def split(a0, a1, b, c0, c1):
+    out = jax.ShapeDtypeStruct(b.shape[1:], BF)
     return pl.pallas_call(
         split_kernel,
         out_shape=[out] * 2,
         compiler_params=params(),
-        cost_estimate=cost(4 * b0.size, 16 * b0.size),
+        cost_estimate=cost(2 * b.size, 8 * b.size),
         name="split",
-    )(a0, a1, b0, b1, c0, c1)
+    )(a0, a1, b, c0, c1)
+
+
+def pass_kernel(qa, ta, qb, tb, out):
+    at = 0
+    for q, t in ((qa, ta), (qb, tb)):
+        out[:, :, at:at + q.shape[2]] = (q[...].astype(F32) + t[...].astype(F32)).astype(BF)
+        at += q.shape[2]
+
+
+def pass_on(qa, ta, qb, tb):
+    cols = qa.shape[2] + qb.shape[2]
+    return pl.pallas_call(
+        pass_kernel,
+        out_shape=jax.ShapeDtypeStruct((*qa.shape[:2], cols), BF),
+        compiler_params=params(),
+        cost_estimate=cost(256 * cols, 1536 * cols),
+        name="pass_on",
+    )(qa, ta, qb, tb)
 
 
 def join_kernel(a, b, out):
-    y, xl, _, _, _, _ = place()
+    y, xl, _, _, _, d = place()
     spots = (
-        (y - 1, xl), (y + 1, xl), (y, xl), (y, xl + 1),
-        (y + 2, xl), (y + 2, xl + 1), (y - 1, xl + 1), (y + 1, xl + 1),
+        (y, xl), (y, xl + 1), (y + 2, xl),
+        (y - d, xl), (y + d, xl), (y - d, xl + 1), (y + 2, xl + 1), (y + d, xl + 1),
     )
     for j, (yy, hh) in enumerate(spots):
         lanes = pl.ds(pl.multiple_of(((yy + 4) % 4 * 2 + hh % 2) * 128, 128), 128)
@@ -292,73 +320,73 @@
     states = (low_state, mid_state, high_state)
     w, mt = prepare((w_low, w_mid, w_high), kv_grad, loss_mask)
     a1 = send(w, Y1)
-    a2 = send(w, Y2)
+    x1 = send(w, XL)
     m_h = send(mt, XH)
     m_1 = send(mt, Z1)
+    m_2 = send(mt, Z2)
     mt, *states = fence(mt, *states)
     states = load(*states)
 
-    mt, m_h, m_1, w, *states = fence(mt, m_h, m_1, w, *states)
-    x1 = send(w, XL)
+    a1, mt, m_h, m_1, m_2, w, *states = fence(a1, mt, m_h, m_1, m_2, w, *states)
+    a3 = send(a1, Y1)
     h_1 = send(m_h, Z1)
-    pair = jnp.stack((mt, m_h))
-    z2 = send(pair, Z2)
-
-    a1, a2, h_1, *states = fence(a1, a2, h_1, *states)
-    a3 = send(a1, Y1)
-    z1 = jnp.stack((m_1, h_1))
-    z3 = send(z1, Z1)
-    mine_a, theirs_a = forward(states, (a1, a2), True)
-
-    x1, z2, z3, mine_a, theirs_a = fence(x1, z2, z3, mine_a, theirs_a)
-    near = jnp.concatenate((pair, z1))
-    far = jnp.concatenate((z2, z3))
-    near_o = send(near, CORE)
-    far_o = send(far, CORE)
+    h_2 = send(m_h, Z2)
+    beside = jnp.stack((m_1, m_2))
+    beside_o = send(beside, CORE)
+
+    mine_a, theirs_a = forward(states, (w, a1))
+
+    a3, x1, h_1, h_2, beside_o, w, theirs_a, *states = fence(a3, x1, h_1, h_2, beside_o, w, theirs_a, *states)
+    a2 = send(w, Y2)
     b1 = send(x1, Y1)
+    b3 = send(a3, XL)
+    across = send(jnp.stack((m_1, h_1)), Z1)
+    middle = jnp.stack((mt, m_h, h_1, h_2))
+    middle_o = send(middle, CORE)
+    mine_b, theirs_b = forward(states, (x1, a3))
+
+    across, middle_o, x1, theirs_b = fence(across, middle_o, x1, theirs_b)
+    across_o = send(across, CORE)
     b2 = send(x1, Y2)
-    b3 = send(a3, XL)
-    mine_b, theirs_b = forward(states, (w, x1), False)
-    near_o, far_o, mine_b = fence(near_o, far_o, mine_b)
-    p2x, pmx, ppx, p0x = backward(states, (near, far, near_o, far_o), True, ("far", "back", "ahead", "here"))
-    p0x, near = fence(p0x, near)
-    p2, pp = backward(states, (near, far, near_o, far_o), False, ("far", "ahead"))
-
-    b1, b2, p2, pp, p2x, pmx, ppx, p0x, near, theirs_a, theirs_b = fence(
-        b1, b2, p2, pp, p2x, pmx, ppx, p0x, near, theirs_a, theirs_b
-    )
+    masked = (beside, middle, across, beside_o, middle_o, across_o)
+    p2x, pmx, ppx, p0x = backward(states, masked, True, ("far", "back", "ahead", "here"))
+
+    a2, b1, b3, p2x, pmx, ppx, p0x, beside = fence(a2, b1, b3, p2x, pmx, ppx, p0x, beside)
     e2 = send(pmx, Y2)
     e3 = send(ppx, Y1)
     e1 = send(p2x, XL)
     got_a = send(theirs_a, CORE)
     got_b = send(theirs_b, CORE)
-    mine_c, theirs_c = forward(states, (a3, b3), False)
-    mine_d, theirs_d = forward(states, (b1, b2), True)
-    got_a, got_b, theirs_c, theirs_d, near = fence(got_a, got_b, theirs_c, theirs_d, near)
-    q2a, qma, qpa, q0a = pick((mine_a, mine_b), (got_a, got_b))
+    p2, pm, pp, p0 = backward(states, masked, False, ("far", "back", "ahead", "here"))
+
+    got_a, got_b, p0, b1, a3 = fence(got_a, got_b, p0, b1, a3)
+    sums = ((0, 0, 0, 0), (1, 0, 1, 0), (1, 1, 1, 1))
+    q2a, qma, qpa, q0a = pick(sums, (mine_a, mine_b), (got_a, got_b))
     t3a = send(q2a, Z2)
     t2a = send(qpa, Z1)
-    pm, p0 = backward(states, (near, far, near_o, far_o), False, ("back", "here"))
+    qma, b1, b3 = fence(qma, b1, b3)
+    mine_c, theirs_c = forward(states, (a2, b1))
+    mine_d, theirs_d = forward(states, (b3, b2))
 
     e1, e2, e3, t3a, t2a, theirs_c, theirs_d, p2, pm, pp, p0 = fence(
         e1, e2, e3, t3a, t2a, theirs_c, theirs_d, p2, pm, pp, p0
     )
+    got_c = send(theirs_c, CORE)
+    got_d = send(theirs_d, CORE)
     f3 = send(add(p2, e1), Y2)
     f2 = send(pp, Y1)
     fx = send(add(p0x, e2, e3), XL)
-    got_c = send(theirs_c, CORE)
-    got_d = send(theirs_d, CORE)
-    q2b, qmb, qpb, q0b = pick((mine_c, mine_d), (got_c, got_d))
+    sums = ((0, 1, 1, 0), (1, 0, 0, 1), (1, 1, 2, 1), (2, 0, 2, 0), (2, 1, 1, 1))
+    q2b, qmb, qpb, q0b = pick(sums, (mine_a, mine_c, mine_d), (got_a, got_c, got_d))
     t3b = send(q2b, Z2)
     t2b = send(qpb, Z1)
 
     t3b, t2b, qma, qmb = fence(t3b, t2b, qma, qmb)
-    t1a = send(add(qma, t3a), Z2)
-    t1b = send(add(qmb, t3b), Z2)
+    t1 = send(pass_on(qma, t3a, qmb, t3b), Z2)
     f1 = send(add(pm, f3), Y2)
-    kept, given = split(q0a, q0b, t1a, t1b, t2a, t2b)
-    keys_values = join(kept, send(given, XH))
-    return (keys_values, *finish(p0, fx, f1, f2))
+    kept, given = split(q0a, q0b, t1, t2a, t2b)
+    got, *grads = fence(send(given, XH), *finish(p0, fx, f1, f2))
+    return (join(kept, got), *grads)
 
 
 def solution(mesh):

time: 125 us -> 119 us (0.952)
  starting transfers between devices: 43.4 us -> 36.9 us
  waiting for transfers between devices: 37.6 us -> 39.6 us
    ppermute x32 -> x33, starting transfers between devices: 43.4 us -> 36.9 us  [send(): return lax.ppermute(array, FULL, pairs)]
    ppermute x32 -> x33, waiting for transfers between devices: 37.6 us -> 39.6 us  [send(): return lax.ppermute(array, FULL, pairs)]
  transfers between devices with their start and end apart: 32 -> 33, of which waited for: 15 -> 15; matrix products, arithmetic and copies ran while one was open for 1% -> 1% of each run, Pallas kernels for 30% -> 31%
where the time goes in v4:
time: 119 us; the launch traced here: 118 us
  Pallas kernels  39.6 us (33%)
  waiting for transfers between devices  39.6 us (33%)
  starting transfers between devices  36.9 us (31%)
  other arithmetic  1.29 us (1%)
    ppermute x33, waiting for transfers between devices, send(): return lax.ppermute(array, FULL, pairs)  39.6 us
    ppermute x33, starting transfers between devices, send(): return lax.ppermute(array, FULL, pairs)  36.9 us
    pallas_call x2, Pallas kernels, backward(): pl.pallas_call(kernel, in_specs=[VMEM] * 9, out_specs=[VMEM] * count, out...  15 us
    pallas_call x4, Pallas kernels, forward(): pl.pallas_call(forward_kernel, in_specs=[VMEM] * 5, out_specs=[VMEM] * 2,...  14.7 us
    pallas_call x1, Pallas kernels, load(): pl.pallas_call(load_kernel, in_specs=[pl.BlockSpec(memory_space=pl.ANY)]...  4.68 us
  transfers between devices with their start and end apart: 33, of which 15 were waited for; matrix products, arithmetic and copies ran while one was open for 1% of the time, Pallas kernels for 31%

profile of v4, /device:TPU:0, one launch (start us, length us, event | category | flops | bytes accessed | tf_op | source)
XLA Modules:
  0.0 118.3 jit_solution(14150055321437732732)
XLA Ops:
  0.6 2.2 %prepare.1 = (bf16[3072,128]{1,0:T(8,128)(2,1)}, bf16[1024,128]{1,0:T(8,128)(2,1)}) custom-call(bf16[1024,128]{1,0:T(8,128)(2,1)} %w0.1, bf16[1024,128]{1,0:T(8,128)(2,1)} %w1.1, bf16[1024,128]{1,0:T(8,128)(2,1)} %w2.1, bf16[128,1024]{1,0:T(8,128)(2,1)} %grad_ref.1, s32[1,128]{1,0:T(1,128)} %bitcast.15), custom_call_target="tpu_custom_call" | custom-call | flops 131 | bytes 2097 | tf_op jit(solution)/shard_map/prepare/pallas_call | solution.py:88
  2.8 1.7 %collective-permute-start = (bf16[3072,128]{1,0:T(8,128)(2,1)}, bf16[3072,128]{1,0:T(8,128)(2,1)S(1)}, u32[]{:S(2)}, u32[]{:S(2)}) collective-permute-start(bf16[3072,128]{1,0:T(8,128)(2,1)} %get-tuple-element.133.wa), channel_id=1, source_target_pairs={{0,32},{1,97},{2,34},{3,99},{4,36},{5,101},{6,38},{7,103},{8,40},{... | collective-permute-start | bytes 2359304 | tf_op jit(solution)/shard_map/ppermute | solution.py:36
  4.6 4.0 %collective-permute-start.3 = (bf16[1024,128]{1,0:T(8,128)(2,1)}, bf16[1024,128]{1,0:T(8,128)(2,1)S(1)}, u32[]{:S(2)}, u32[]{:S(2)}) collective-permute-start(bf16[1024,128]{1,0:T(8,128)(2,1)} %get-tuple-element.125), channel_id=1, source_target_pairs={{0,12},{1,5},{2,14},{3,7},{4,0},{5,9},{6,2},{7,11},{8,4},{9,13},{1... | collective-permute-start | bytes 786440 | tf_op jit(solution)/shard_map/ppermute | solution.py:36
  8.6 3.0 %collective-permute-start.1 = (bf16[1024,128]{1,0:T(8,128)(2,1)}, bf16[1024,128]{1,0:T(8,128)(2,1)S(1)}, u32[]{:S(2)}, u32[]{:S(2)}) collective-permute-start(bf16[1024,128]{1,0:T(8,128)(2,1)} %get-tuple-element.125), channel_id=1, source_target_pairs={{0,2},{1,3},{2,0},{3,1},{4,6},{5,7},{6,4},{7,5},{8,10},{9,11},{10,... | collective-permute-start | bytes 786440 | tf_op jit(solution)/shard_map/ppermute | solution.py:36
  12.2 4.7 %load.1 = (bf16[2048,1024]{1,0:T(8,128)(2,1)S(1)}, bf16[2048,1024]{1,0:T(8,128)(2,1)S(1)}, bf16[2048,1024]{1,0:T(8,128)(2,1)S(1)}) custom-call(bf16[2048,1024]{1,0:T(8,128)(2,1)} %refs_0_, bf16[2048,1024]{1,0:T(8,128)(2,1)} %refs_1_, bf16[2048,1024]{1,0:T(8,128)(2,1)} %refs_2_), custom_call_target="tpu_custom_call" | custom-call | bytes 25165 | tf_op jit(solution)/shard_map/load/pallas_call | solution.py:116
  17.0 2.6 %collective-permute-done.1 = bf16[1024,128]{1,0:T(8,128)(2,1)S(1)} collective-permute-done((bf16[1024,128]{1,0:T(8,128)(2,1)}, bf16[1024,128]{1,0:T(8,128)(2,1)S(1)}, u32[]{:S(2)}, u32[]{:S(2)}) %collective-permute-start.1) | collective-permute-done | bytes 262176 | tf_op jit(solution)/shard_map/ppermute | solution.py:36
  19.5 1.6 %collective-permute-start.4 = (bf16[3072,128]{1,0:T(8,128)(2,1)S(1)}, bf16[3072,128]{1,0:T(8,128)(2,1)S(1)}, u32[]{:S(2)}, u32[]{:S(2)}) collective-permute-start(bf16[3072,128]{1,0:T(8,128)(2,1)S(1)} %collective-permute-done.wb), channel_id=1, source_target_pairs={{0,32},{1,97},{2,34},{3,99},{4,36},{5,101},{6,38},{7,103},{8,40},{... | collective-permute-start | bytes 2359304 | tf_op jit(solution)/shard_map/ppermute | solution.py:36
  21.3 3.3 %collective-permute-start.7 = (bf16[1024,128]{1,0:T(8,128)(2,1)S(1)}, bf16[1024,128]{1,0:T(8,128)(2,1)S(1)}, u32[]{:S(2)}, u32[]{:S(2)}) collective-permute-start(bf16[1024,128]{1,0:T(8,128)(2,1)S(1)} %collective-permute-done.1), channel_id=1, source_target_pairs={{0,12},{1,5},{2,14},{3,7},{4,0},{5,9},{6,2},{7,11},{8,4},{9,13},{1... | collective-permute-start | bytes 786440 | tf_op jit(solution)/shard_map/ppermute | solution.py:36
  24.6 3.7 %forward.4 = (bf16[4,2,128,256]{3,2,1,0:T(8,128)(2,1)S(1)}, bf16[4,2,128,256]{3,2,1,0:T(8,128)(2,1)S(1)}) custom-call(bf16[2048,1024]{1,0:T(8,128)(2,1)S(1)} %get-tuple-element.117.s0.refs_6_, bf16[2048,1024]{1,0:T(8,128)(2,1)S(1)} %get-tuple-element.118.s1.refs_7_, bf16[2048,1024]{1,0:T(8,128)(2,1)S(1)} %get-tuple-element.119.s2.refs_8_, ...), custom_call_target="tpu_custom_call" | custom-call | flops 3221225 | bytes 14680 | tf_op jit(solution)/shard_map/forward/pallas_call | solution.py:150
  28.3 7.9 %collective-permute-done.5.wa = bf16[3072,128]{1,0:T(8,128)(2,1)S(1)} collective-permute-done((bf16[3072,128]{1,0:T(8,128)(2,1)}, bf16[3072,128]{1,0:T(8,128)(2,1)S(1)}, u32[]{:S(2)}, u32[]{:S(2)}) %collective-permute-start.5) | collective-permute-done | bytes 786464 | tf_op jit(solution)/shard_map/ppermute | solution.py:36
  38.7 1.4 %collective-permute-start.16 = (bf16[3072,128]{1,0:T(8,128)(2,1)S(1)}, bf16[3072,128]{1,0:T(8,128)(2,1)S(1)}, u32[]{:S(2)}, u32[]{:S(2)}) collective-permute-start(bf16[3072,128]{1,0:T(8,128)(2,1)S(1)} %collective-permute-done.4.wb), channel_id=1, source_target_pairs={{0,16},{1,17},{2,18},{3,19},{4,20},{5,21},{6,22},{7,23},{8,24},{9,... | collective-permute-start | bytes 2359304 | tf_op jit(solution)/shard_map/ppermute | solution.py:36
  40.1 3.7 %forward.5 = (bf16[4,2,128,256]{3,2,1,0:T(8,128)(2,1)S(1)}, bf16[4,2,128,256]{3,2,1,0:T(8,128)(2,1)S(1)}) custom-call(bf16[2048,1024]{1,0:T(8,128)(2,1)S(1)} %get-tuple-element.117.s0.refs_6_, bf16[2048,1024]{1,0:T(8,128)(2,1)S(1)} %get-tuple-element.118.s1.refs_7_, bf16[2048,1024]{1,0:T(8,128)(2,1)S(1)} %get-tuple-element.119.s2.refs_8_, ...), custom_call_target="tpu_custom_call" | custom-call | flops 3221225 | bytes 14680 | tf_op jit(solution)/shard_map/forward/pallas_call | solution.py:150
  43.8 3.2 %collective-permute-done.10.refs_2_ = bf16[2,1024,128]{2,1,0:T(8,128)(2,1)S(1)} collective-permute-done((bf16[2,1024,128]{2,1,0:T(8,128)(2,1)S(1)}, bf16[2,1024,128]{2,1,0:T(8,128)(2,1)S(1)}, u32[]{:S(2)}, u32[]{:S(2)}) %collective-permute-start.10) | collective-permute-done | bytes 524320 | tf_op jit(solution)/shard_map/ppermute | solution.py:36
  47.5 1.4 %collective-permute-done.13.refs_5_ = bf16[2,1024,128]{2,1,0:T(8,128)(2,1)S(1)} collective-permute-done((bf16[2,1024,128]{2,1,0:T(8,128)(2,1)S(1)}, bf16[2,1024,128]{2,1,0:T(8,128)(2,1)S(1)}, u32[]{:S(2)}, u32[]{:S(2)}) %collective-permute-start.13) | collective-permute-done | bytes 524320 | tf_op jit(solution)/shard_map/ppermute | solution.py:36
  49.6 7.5 %backward.3 = (bf16[3,128,1024]{2,1,0:T(8,128)(2,1)S(1)}, bf16[3,128,1024]{2,1,0:T(8,128)(2,1)S(1)}, bf16[3,128,1024]{2,1,0:T(8,128)(2,1)S(1)}, bf16[3,128,1024]{2,1,0:T(8,128)(2,1)S(1)}) custom-call(bf16[2,1024,128]{2,1,0:T(8,128)(2,1)S(1)} %pad_maximum_fusion.2.refs_0_, bf16[4,1024,128]{2,1,0:T(8,128)(2,1)S(1)} %pad_maximum_fusion.refs_1_, ...), custom_call_target="tpu_custom_call" | custom-call | flops 6442450 | bytes 20971 | tf_op jit(solution)/shard_map/backward/pallas_call | solution.py:200
  57.1 1.7 %collective-permute-done.15.wb = bf16[3072,128]{1,0:T(8,128)(2,1)S(1)} collective-permute-done((bf16[3072,128]{1,0:T(8,128)(2,1)S(1)}, bf16[3072,128]{1,0:T(8,128)(2,1)S(1)}, u32[]{:S(2)}, u32[]{:S(2)}) %collective-permute-start.15) | collective-permute-done | bytes 786464 | tf_op jit(solution)/shard_map/ppermute | solution.py:36
  58.9 1.4 %collective-permute-start.18 = (bf16[3,128,1024]{2,1,0:T(8,128)(2,1)S(1)}, bf16[3,128,1024]{2,1,0:T(8,128)(2,1)S(1)}, u32[]{:S(2)}, u32[]{:S(2)}) collective-permute-start(bf16[3,128,1024]{2,1,0:T(8,128)(2,1)S(1)} %get-tuple-element.151), channel_id=1, source_target_pairs={{0,16},{1,17},{2,18},{3,19},{4,20},{5,21},{6,22},{7,23},{8,24},{9,... | collective-permute-start | bytes 2359304 | tf_op jit(solution)/shard_map/ppermute | solution.py:36
  60.3 2.1 %collective-permute-start.19 = (bf16[3,128,1024]{2,1,0:T(8,128)(2,1)S(1)}, bf16[3,128,1024]{2,1,0:T(8,128)(2,1)S(1)}, u32[]{:S(2)}, u32[]{:S(2)}) collective-permute-start(bf16[3,128,1024]{2,1,0:T(8,128)(2,1)S(1)} %get-tuple-element.152), channel_id=1, source_target_pairs={{0,96},{1,33},{2,98},{3,35},{4,100},{5,37},{6,102},{7,39},{8,104},... | collective-permute-start | bytes 2359304 | tf_op jit(solution)/shard_map/ppermute | solution.py:36
  63.2 7.5 %backward.2 = (bf16[3,128,1024]{2,1,0:T(8,128)(2,1)S(1)}, bf16[3,128,1024]{2,1,0:T(8,128)(2,1)S(1)}, bf16[3,128,1024]{2,1,0:T(8,128)(2,1)S(1)}, bf16[3,128,1024]{2,1,0:T(8,128)(2,1)S(1)}) custom-call(bf16[2,1024,128]{2,1,0:T(8,128)(2,1)S(1)} %pad_maximum_fusion.2.refs_0_, bf16[4,1024,128]{2,1,0:T(8,128)(2,1)S(1)} %pad_maximum_fusion.refs_1_, ...), custom_call_target="tpu_custom_call" | custom-call | flops 6442450 | bytes 20971 | tf_op jit(solution)/shard_map/backward/pallas_call | solution.py:200
  71.0 2.6 %collective-permute-start.21 = (bf16[2,128,384]{2,1,0:T(8,128)(2,1)S(1)}, bf16[2,128,384]{2,1,0:T(8,128)(2,1)S(1)}, u32[]{:S(2)}, u32[]{:S(2)}) collective-permute-start(bf16[2,128,384]{2,1,0:T(8,128)(2,1)S(1)} %get-tuple-element.154), channel_id=1, source_target_pairs={{0,12},{1,5},{2,14},{3,7},{4,0},{5,9},{6,2},{7,11},{8,4},{9,13},{1... | collective-permute-start | bytes 589832 | tf_op jit(solution)/shard_map/ppermute | solution.py:36
  73.6 3.7 %forward.6 = (bf16[4,2,128,256]{3,2,1,0:T(8,128)(2,1)S(1)}, bf16[4,2,128,256]{3,2,1,0:T(8,128)(2,1)S(1)}) custom-call(bf16[2048,1024]{1,0:T(8,128)(2,1)S(1)} %get-tuple-element.117.s0.refs_6_, bf16[2048,1024]{1,0:T(8,128)(2,1)S(1)} %get-tuple-element.118.s1.refs_7_, bf16[2048,1024]{1,0:T(8,128)(2,1)S(1)} %get-tuple-element.119.s2.refs_8_, ...), custom_call_target="tpu_custom_call" | custom-call | flops 3221225 | bytes 14680 | tf_op jit(solution)/shard_map/forward/pallas_call | solution.py:150
  77.3 3.7 %forward.7 = (bf16[4,2,128,256]{3,2,1,0:T(8,128)(2,1)S(1)}, bf16[4,2,128,256]{3,2,1,0:T(8,128)(2,1)S(1)}) custom-call(bf16[2048,1024]{1,0:T(8,128)(2,1)S(1)} %get-tuple-element.117.s0.refs_6_, bf16[2048,1024]{1,0:T(8,128)(2,1)S(1)} %get-tuple-element.118.s1.refs_7_, bf16[2048,1024]{1,0:T(8,128)(2,1)S(1)} %get-tuple-element.119.s2.refs_8_, ...), custom_call_target="tpu_custom_call" | custom-call | flops 3221225 | bytes 14680 | tf_op jit(solution)/shard_map/forward/pallas_call | solution.py:150
  81.0 1.4 %collective-permute-done.19 = bf16[3,128,1024]{2,1,0:T(8,128)(2,1)S(1)} collective-permute-done((bf16[3,128,1024]{2,1,0:T(8,128)(2,1)S(1)}, bf16[3,128,1024]{2,1,0:T(8,128)(2,1)S(1)}, u32[]{:S(2)}, u32[]{:S(2)}) %collective-permute-start.19) | collective-permute-done | bytes 786464 | tf_op jit(solution)/shard_map/ppermute | solution.py:36
  82.4 1.7 %collective-permute-done.20 = bf16[3,128,1024]{2,1,0:T(8,128)(2,1)S(1)} collective-permute-done((bf16[3,128,1024]{2,1,0:T(8,128)(2,1)S(1)}, bf16[3,128,1024]{2,1,0:T(8,128)(2,1)S(1)}, u32[]{:S(2)}, u32[]{:S(2)}) %collective-permute-start.20) | collective-permute-done | bytes 786464 | tf_op jit(solution)/shard_map/ppermute | solution.py:36
  87.1 1.7 %collective-permute-start.25 = (bf16[2,128,640]{2,1,0:T(8,128)(2,1)S(1)}, bf16[2,128,640]{2,1,0:T(8,128)(2,1)S(1)}, u32[]{:S(2)}, u32[]{:S(2)}) collective-permute-start(bf16[2,128,640]{2,1,0:T(8,128)(2,1)S(1)} %get-tuple-element.165), channel_id=1, source_target_pairs={{0,12},{1,5},{2,14},{3,7},{4,0},{5,9},{6,2},{7,11},{8,4},{9,13},{1... | collective-permute-start | bytes 983048 | tf_op jit(solution)/shard_map/ppermute | solution.py:36
  91.0 6.0 %collective-permute-done.25.tb = bf16[2,128,640]{2,1,0:T(8,128)(2,1)S(1)} collective-permute-done((bf16[2,128,640]{2,1,0:T(8,128)(2,1)S(1)}, bf16[2,128,640]{2,1,0:T(8,128)(2,1)S(1)}, u32[]{:S(2)}, u32[]{:S(2)}) %collective-permute-start.25) | collective-permute-done | bytes 327712 | tf_op jit(solution)/shard_map/ppermute | solution.py:36
  98.3 2.2 %collective-permute-start.27 = (bf16[2,128,1024]{2,1,0:T(8,128)(2,1)S(1)}, bf16[2,128,1024]{2,1,0:T(8,128)(2,1)S(1)}, u32[]{:S(2)}, u32[]{:S(2)}) collective-permute-start(bf16[2,128,1024]{2,1,0:T(8,128)(2,1)S(1)} %pass_on.1), channel_id=1, source_target_pairs={{0,12},{1,5},{2,14},{3,7},{4,0},{5,9},{6,2},{7,11},{8,4},{9,13},{1... | collective-permute-start | bytes 1572872 | tf_op jit(solution)/shard_map/ppermute | solution.py:36
  100.7 2.1 %collective-permute-start.31 = (bf16[3,128,1024]{2,1,0:T(8,128)(2,1)S(1)}, bf16[3,128,1024]{2,1,0:T(8,128)(2,1)S(1)}, u32[]{:S(2)}, u32[]{:S(2)}) collective-permute-start(bf16[3,128,1024]{2,1,0:T(8,128)(2,1)S(1)} %add_convert_fusion), channel_id=1, source_target_pairs={{0,96},{1,33},{2,98},{3,35},{4,100},{5,37},{6,102},{7,39},{8,104},... | collective-permute-start | bytes 2359304 | tf_op jit(solution)/shard_map/ppermute | solution.py:36
  102.9 4.7 %collective-permute-done.27.b = bf16[2,128,1024]{2,1,0:T(8,128)(2,1)S(1)} collective-permute-done((bf16[2,128,1024]{2,1,0:T(8,128)(2,1)S(1)}, bf16[2,128,1024]{2,1,0:T(8,128)(2,1)S(1)}, u32[]{:S(2)}, u32[]{:S(2)}) %collective-permute-start.27) | collective-permute-done | bytes 524320 | tf_op jit(solution)/shard_map/ppermute | solution.py:36
  107.7 2.0 %collective-permute-start.28 = (bf16[128,1024]{1,0:T(8,128)(2,1)S(1)}, bf16[128,1024]{1,0:T(8,128)(2,1)S(1)}, u32[]{:S(2)}, u32[]{:S(2)}) collective-permute-start(bf16[128,1024]{1,0:T(8,128)(2,1)S(1)} %get-tuple-element.176), channel_id=1, source_target_pairs={{0,2},{1,3},{2,0},{3,1},{4,6},{5,7},{6,4},{7,5},{8,10},{9,11},{10,... | collective-permute-start | bytes 786440 | tf_op jit(solution)/shard_map/ppermute | solution.py:36
  109.9 3.9 %collective-permute-done.31.c = bf16[3,128,1024]{2,1,0:T(8,128)(2,1)S(1)} collective-permute-done((bf16[3,128,1024]{2,1,0:T(8,128)(2,1)S(1)}, bf16[3,128,1024]{2,1,0:T(8,128)(2,1)S(1)}, u32[]{:S(2)}, u32[]{:S(2)}) %collective-permute-start.31) | collective-permute-done | bytes 786464 | tf_op jit(solution)/shard_map/ppermute | solution.py:36
  115.1 2.4 %collective-permute-done.28.b = bf16[128,1024]{1,0:T(8,128)(2,1)S(1)} collective-permute-done((bf16[128,1024]{1,0:T(8,128)(2,1)S(1)}, bf16[128,1024]{1,0:T(8,128)(2,1)S(1)}, u32[]{:S(2)}, u32[]{:S(2)}) %collective-permute-start.28) | collective-permute-done | bytes 262176 | tf_op jit(solution)/shard_map/ppermute | solution.py:36
  (58 shorter events, 14.8 us)
Async XLA Ops:
  2.8 16.7 %collective-permute-start = (bf16[3072,128]{1,0:T(8,128)(2,1)}, bf16[3072,128]{1,0:T(8,128)(2,1)S(1)}, u32[]{:S(2)}, u32[]{:S(2)}) collective-permute-start(bf16[3072,128]{1,0:T(8,128)(2,1)} %get-tuple-element.133.wa), channel_id=1, source_target_pairs={{0,32},{1,97},{2,34},{3,99},{4,36},{5,101},{6,38},{7,103},{8,40},{... | collective-permute-start | bytes 2359304 | tf_op jit(solution)/shard_map/ppermute | solution.py:36
  4.6 12.4 %collective-permute-start.3 = (bf16[1024,128]{1,0:T(8,128)(2,1)}, bf16[1024,128]{1,0:T(8,128)(2,1)S(1)}, u32[]{:S(2)}, u32[]{:S(2)}) collective-permute-start(bf16[1024,128]{1,0:T(8,128)(2,1)} %get-tuple-element.125), channel_id=1, source_target_pairs={{0,12},{1,5},{2,14},{3,7},{4,0},{5,9},{6,2},{7,11},{8,4},{9,13},{1... | collective-permute-start | bytes 786440 | tf_op jit(solution)/shard_map/ppermute | solution.py:36
  8.6 8.3 %collective-permute-start.2 = (bf16[1024,128]{1,0:T(8,128)(2,1)}, bf16[1024,128]{1,0:T(8,128)(2,1)S(1)}, u32[]{:S(2)}, u32[]{:S(2)}) collective-permute-start(bf16[1024,128]{1,0:T(8,128)(2,1)} %get-tuple-element.125), channel_id=1, source_target_pairs={{0,4},{1,13},{2,6},{3,15},{4,8},{5,1},{6,10},{7,3},{8,12},{9,5},{1... | collective-permute-start | bytes 786440 | tf_op jit(solution)/shard_map/ppermute | solution.py:36
  8.6 10.9 %collective-permute-start.1 = (bf16[1024,128]{1,0:T(8,128)(2,1)}, bf16[1024,128]{1,0:T(8,128)(2,1)S(1)}, u32[]{:S(2)}, u32[]{:S(2)}) collective-permute-start(bf16[1024,128]{1,0:T(8,128)(2,1)} %get-tuple-element.125), channel_id=1, source_target_pairs={{0,2},{1,3},{2,0},{3,1},{4,6},{5,7},{6,4},{7,5},{8,10},{9,11},{10,... | collective-permute-start | bytes 786440 | tf_op jit(solution)/shard_map/ppermute | solution.py:36
  11.6 24.6 %collective-permute-start.5 = (bf16[3072,128]{1,0:T(8,128)(2,1)}, bf16[3072,128]{1,0:T(8,128)(2,1)S(1)}, u32[]{:S(2)}, u32[]{:S(2)}) collective-permute-start(bf16[3072,128]{1,0:T(8,128)(2,1)} %get-tuple-element.133.wa), channel_id=1, source_target_pairs={{0,16},{1,17},{2,18},{3,19},{4,20},{5,21},{6,22},{7,23},{8,24},{9,... | collective-permute-start | bytes 2359304 | tf_op jit(solution)/shard_map/ppermute | solution.py:36
  19.5 16.7 %collective-permute-start.4 = (bf16[3072,128]{1,0:T(8,128)(2,1)S(1)}, bf16[3072,128]{1,0:T(8,128)(2,1)S(1)}, u32[]{:S(2)}, u32[]{:S(2)}) collective-permute-start(bf16[3072,128]{1,0:T(8,128)(2,1)S(1)} %collective-permute-done.wb), channel_id=1, source_target_pairs={{0,32},{1,97},{2,34},{3,99},{4,36},{5,101},{6,38},{7,103},{8,40},{... | collective-permute-start | bytes 2359304 | tf_op jit(solution)/shard_map/ppermute | solution.py:36
  21.2 15.0 %collective-permute-start.8 = (bf16[2,1024,128]{2,1,0:T(8,128)(2,1)S(1)}, bf16[2,1024,128]{2,1,0:T(8,128)(2,1)S(1)}, u32[]{:S(2)}, u32[]{:S(2)}) collective-permute-start(bf16[2,1024,128]{2,1,0:T(8,128)(2,1)S(1)} %pad_maximum_fusion.2.refs_0_), channel_id=1, source_target_pairs={{0,1},{1,0},{2,3},{3,2},{4,5},{5,4},{6,7},{7,6},{8,9},{9,8},{10,11... | collective-permute-start | bytes 1572872 | tf_op jit(solution)/shard_map/ppermute | solution.py:36
  21.3 14.9 %collective-permute-start.7 = (bf16[1024,128]{1,0:T(8,128)(2,1)S(1)}, bf16[1024,128]{1,0:T(8,128)(2,1)S(1)}, u32[]{:S(2)}, u32[]{:S(2)}) collective-permute-start(bf16[1024,128]{1,0:T(8,128)(2,1)S(1)} %collective-permute-done.1), channel_id=1, source_target_pairs={{0,12},{1,5},{2,14},{3,7},{4,0},{5,9},{6,2},{7,11},{8,4},{9,13},{1... | collective-permute-start | bytes 786440 | tf_op jit(solution)/shard_map/ppermute | solution.py:36
  24.6 11.6 %collective-permute-start.6 = (bf16[1024,128]{1,0:T(8,128)(2,1)S(1)}, bf16[1024,128]{1,0:T(8,128)(2,1)S(1)}, u32[]{:S(2)}, u32[]{:S(2)}) collective-permute-start(bf16[1024,128]{1,0:T(8,128)(2,1)S(1)} %collective-permute-done.1), channel_id=1, source_target_pairs={{0,4},{1,13},{2,6},{3,15},{4,8},{5,1},{6,10},{7,3},{8,12},{9,5},{1... | collective-permute-start | bytes 786440 | tf_op jit(solution)/shard_map/ppermute | solution.py:36
  36.4 10.6 %collective-permute-start.11 = (bf16[4,1024,128]{2,1,0:T(8,128)(2,1)S(1)}, bf16[4,1024,128]{2,1,0:T(8,128)(2,1)S(1)}, u32[]{:S(2)}, u32[]{:S(2)}) collective-permute-start(bf16[4,1024,128]{2,1,0:T(8,128)(2,1)S(1)} %pad_maximum_fusion.refs_1_), channel_id=1, source_target_pairs={{0,1},{1,0},{2,3},{3,2},{4,5},{5,4},{6,7},{7,6},{8,9},{9,8},{10,11... | collective-permute-start | bytes 3145736 | tf_op jit(solution)/shard_map/ppermute | solution.py:36
  36.5 10.5 %collective-permute-start.10 = (bf16[2,1024,128]{2,1,0:T(8,128)(2,1)S(1)}, bf16[2,1024,128]{2,1,0:T(8,128)(2,1)S(1)}, u32[]{:S(2)}, u32[]{:S(2)}) collective-permute-start(bf16[2,1024,128]{2,1,0:T(8,128)(2,1)S(1)} %pad_maximum_fusion.1), channel_id=1, source_target_pairs={{0,4},{1,13},{2,6},{3,15},{4,8},{5,1},{6,10},{7,3},{8,12},{9,5},{1... | collective-permute-start | bytes 1572872 | tf_op jit(solution)/shard_map/ppermute | solution.py:36
  36.6 20.5 %collective-permute-start.14 = (bf16[3072,128]{1,0:T(8,128)(2,1)S(1)}, bf16[3072,128]{1,0:T(8,128)(2,1)S(1)}, u32[]{:S(2)}, u32[]{:S(2)}) collective-permute-start(bf16[3072,128]{1,0:T(8,128)(2,1)S(1)} %copy-done), channel_id=1, source_target_pairs={{0,96},{1,33},{2,98},{3,35},{4,100},{5,37},{6,102},{7,39},{8,104},... | collective-permute-start | bytes 2359304 | tf_op jit(solution)/shard_map/ppermute | solution.py:36
  37.4 21.5 %collective-permute-start.15 = (bf16[3072,128]{1,0:T(8,128)(2,1)S(1)}, bf16[3072,128]{1,0:T(8,128)(2,1)S(1)}, u32[]{:S(2)}, u32[]{:S(2)}) collective-permute-start(bf16[3072,128]{1,0:T(8,128)(2,1)S(1)} %collective-permute-done.5.wa), channel_id=1, source_target_pairs={{0,32},{1,97},{2,34},{3,99},{4,36},{5,101},{6,38},{7,103},{8,40},{... | collective-permute-start | bytes 2359304 | tf_op jit(solution)/shard_map/ppermute | solution.py:36
  38.7 20.2 %collective-permute-start.16 = (bf16[3072,128]{1,0:T(8,128)(2,1)S(1)}, bf16[3072,128]{1,0:T(8,128)(2,1)S(1)}, u32[]{:S(2)}, u32[]{:S(2)}) collective-permute-start(bf16[3072,128]{1,0:T(8,128)(2,1)S(1)} %collective-permute-done.4.wb), channel_id=1, source_target_pairs={{0,16},{1,17},{2,18},{3,19},{4,20},{5,21},{6,22},{7,23},{8,24},{9,... | collective-permute-start | bytes 2359304 | tf_op jit(solution)/shard_map/ppermute | solution.py:36
  47.0 1.9 %collective-permute-start.13 = (bf16[2,1024,128]{2,1,0:T(8,128)(2,1)S(1)}, bf16[2,1024,128]{2,1,0:T(8,128)(2,1)S(1)}, u32[]{:S(2)}, u32[]{:S(2)}) collective-permute-start(bf16[2,1024,128]{2,1,0:T(8,128)(2,1)S(1)} %collective-permute-done.10.refs_2_), channel_id=1, source_target_pairs={{0,1},{1,0},{2,3},{3,2},{4,5},{5,4},{6,7},{7,6},{8,9},{9,8},{10,11... | collective-permute-start | bytes 1572872 | tf_op jit(solution)/shard_map/ppermute | solution.py:36
  47.0 15.4 %collective-permute-start.9 = (bf16[4,2,128,256]{3,2,1,0:T(8,128)(2,1)S(1)}, bf16[4,2,128,256]{3,2,1,0:T(8,128)(2,1)S(1)}, u32[]{:S(2)}, u32[]{:S(2)}) collective-permute-start(bf16[4,2,128,256]{3,2,1,0:T(8,128)(2,1)S(1)} %get-tuple-element.123), channel_id=1, source_target_pairs={{0,1},{1,0},{2,3},{3,2},{4,5},{5,4},{6,7},{7,6},{8,9},{9,8},{10,11... | collective-permute-start | bytes 1572872 | tf_op jit(solution)/shard_map/ppermute | solution.py:36
  48.9 24.7 %collective-permute-start.17 = (bf16[3072,128]{1,0:T(8,128)(2,1)S(1)}, bf16[3072,128]{1,0:T(8,128)(2,1)S(1)}, u32[]{:S(2)}, u32[]{:S(2)}) collective-permute-start(bf16[3072,128]{1,0:T(8,128)(2,1)S(1)} %collective-permute-done.5.wa), channel_id=1, source_target_pairs={{0,96},{1,33},{2,98},{3,35},{4,100},{5,37},{6,102},{7,39},{8,104},... | collective-permute-start | bytes 2359304 | tf_op jit(solution)/shard_map/ppermute | solution.py:36
  58.9 22.1 %collective-permute-start.18 = (bf16[3,128,1024]{2,1,0:T(8,128)(2,1)S(1)}, bf16[3,128,1024]{2,1,0:T(8,128)(2,1)S(1)}, u32[]{:S(2)}, u32[]{:S(2)}) collective-permute-start(bf16[3,128,1024]{2,1,0:T(8,128)(2,1)S(1)} %get-tuple-element.151), channel_id=1, source_target_pairs={{0,16},{1,17},{2,18},{3,19},{4,20},{5,21},{6,22},{7,23},{8,24},{9,... | collective-permute-start | bytes 2359304 | tf_op jit(solution)/shard_map/ppermute | solution.py:36
  60.3 22.0 %collective-permute-start.19 = (bf16[3,128,1024]{2,1,0:T(8,128)(2,1)S(1)}, bf16[3,128,1024]{2,1,0:T(8,128)(2,1)S(1)}, u32[]{:S(2)}, u32[]{:S(2)}) collective-permute-start(bf16[3,128,1024]{2,1,0:T(8,128)(2,1)S(1)} %get-tuple-element.152), channel_id=1, source_target_pairs={{0,96},{1,33},{2,98},{3,35},{4,100},{5,37},{6,102},{7,39},{8,104},... | collective-permute-start | bytes 2359304 | tf_op jit(solution)/shard_map/ppermute | solution.py:36
  62.4 21.7 %collective-permute-start.20 = (bf16[3,128,1024]{2,1,0:T(8,128)(2,1)S(1)}, bf16[3,128,1024]{2,1,0:T(8,128)(2,1)S(1)}, u32[]{:S(2)}, u32[]{:S(2)}) collective-permute-start(bf16[3,128,1024]{2,1,0:T(8,128)(2,1)S(1)} %get-tuple-element.153), channel_id=1, source_target_pairs={{0,32},{1,97},{2,34},{3,99},{4,36},{5,101},{6,38},{7,103},{8,40},{... | collective-permute-start | bytes 2359304 | tf_op jit(solution)/shard_map/ppermute | solution.py:36
  62.4 8.3 %collective-permute-start.12 = (bf16[4,2,128,256]{3,2,1,0:T(8,128)(2,1)S(1)}, bf16[4,2,128,256]{3,2,1,0:T(8,128)(2,1)S(1)}, u32[]{:S(2)}, u32[]{:S(2)}) collective-permute-start(bf16[4,2,128,256]{3,2,1,0:T(8,128)(2,1)S(1)} %get-tuple-element.128), channel_id=1, source_target_pairs={{0,1},{1,0},{2,3},{3,2},{4,5},{5,4},{6,7},{7,6},{8,9},{9,8},{10,11... | collective-permute-start | bytes 1572872 | tf_op jit(solution)/shard_map/ppermute | solution.py:36
  71.0 10.0 %collective-permute-start.21 = (bf16[2,128,384]{2,1,0:T(8,128)(2,1)S(1)}, bf16[2,128,384]{2,1,0:T(8,128)(2,1)S(1)}, u32[]{:S(2)}, u32[]{:S(2)}) collective-permute-start(bf16[2,128,384]{2,1,0:T(8,128)(2,1)S(1)} %get-tuple-element.154), channel_id=1, source_target_pairs={{0,12},{1,5},{2,14},{3,7},{4,0},{5,9},{6,2},{7,11},{8,4},{9,13},{1... | collective-permute-start | bytes 589832 | tf_op jit(solution)/shard_map/ppermute | solution.py:36
  73.6 7.4 %collective-permute-start.22 = (bf16[2,128,384]{2,1,0:T(8,128)(2,1)S(1)}, bf16[2,128,384]{2,1,0:T(8,128)(2,1)S(1)}, u32[]{:S(2)}, u32[]{:S(2)}) collective-permute-start(bf16[2,128,384]{2,1,0:T(8,128)(2,1)S(1)} %get-tuple-element.155), channel_id=1, source_target_pairs={{0,4},{1,13},{2,6},{3,15},{4,8},{5,1},{6,10},{7,3},{8,12},{9,5},{1... | collective-permute-start | bytes 589832 | tf_op jit(solution)/shard_map/ppermute | solution.py:36
  84.2 2.5 %collective-permute-start.24 = (bf16[4,2,128,256]{3,2,1,0:T(8,128)(2,1)S(1)}, bf16[4,2,128,256]{3,2,1,0:T(8,128)(2,1)S(1)}, u32[]{:S(2)}, u32[]{:S(2)}) collective-permute-start(bf16[4,2,128,256]{3,2,1,0:T(8,128)(2,1)S(1)} %get-tuple-element.163), channel_id=1, source_target_pairs={{0,1},{1,0},{2,3},{3,2},{4,5},{5,4},{6,7},{7,6},{8,9},{9,8},{10,11... | collective-permute-start | bytes 1572872 | tf_op jit(solution)/shard_map/ppermute | solution.py:36
  84.9 15.5 %collective-permute-start.30 = (bf16[3,128,1024]{2,1,0:T(8,128)(2,1)S(1)}, bf16[3,128,1024]{2,1,0:T(8,128)(2,1)S(1)}, u32[]{:S(2)}, u32[]{:S(2)}) collective-permute-start(bf16[3,128,1024]{2,1,0:T(8,128)(2,1)S(1)} %add_convert_fusion.1), channel_id=1, source_target_pairs={{0,96},{1,33},{2,98},{3,35},{4,100},{5,37},{6,102},{7,39},{8,104},... | collective-permute-start | bytes 2359304 | tf_op jit(solution)/shard_map/ppermute | solution.py:36
  87.1 9.9 %collective-permute-start.25 = (bf16[2,128,640]{2,1,0:T(8,128)(2,1)S(1)}, bf16[2,128,640]{2,1,0:T(8,128)(2,1)S(1)}, u32[]{:S(2)}, u32[]{:S(2)}) collective-permute-start(bf16[2,128,640]{2,1,0:T(8,128)(2,1)S(1)} %get-tuple-element.165), channel_id=1, source_target_pairs={{0,12},{1,5},{2,14},{3,7},{4,0},{5,9},{6,2},{7,11},{8,4},{9,13},{1... | collective-permute-start | bytes 983048 | tf_op jit(solution)/shard_map/ppermute | solution.py:36
  88.8 9.3 %collective-permute-start.26 = (bf16[2,128,640]{2,1,0:T(8,128)(2,1)S(1)}, bf16[2,128,640]{2,1,0:T(8,128)(2,1)S(1)}, u32[]{:S(2)}, u32[]{:S(2)}) collective-permute-start(bf16[2,128,640]{2,1,0:T(8,128)(2,1)S(1)} %get-tuple-element.166), channel_id=1, source_target_pairs={{0,4},{1,13},{2,6},{3,15},{4,8},{5,1},{6,10},{7,3},{8,12},{9,5},{1... | collective-permute-start | bytes 983048 | tf_op jit(solution)/shard_map/ppermute | solution.py:36
  89.6 20.3 %collective-permute-start.29 = (bf16[3,128,1024]{2,1,0:T(8,128)(2,1)S(1)}, bf16[3,128,1024]{2,1,0:T(8,128)(2,1)S(1)}, u32[]{:S(2)}, u32[]{:S(2)}) collective-permute-start(bf16[3,128,1024]{2,1,0:T(8,128)(2,1)S(1)} %add_convert_fusion.2), channel_id=1, source_target_pairs={{0,16},{1,17},{2,18},{3,19},{4,20},{5,21},{6,22},{7,23},{8,24},{9,... | collective-permute-start | bytes 2359304 | tf_op jit(solution)/shard_map/ppermute | solution.py:36
  90.8 19.1 %collective-permute-start.32 = (bf16[3,128,1024]{2,1,0:T(8,128)(2,1)S(1)}, bf16[3,128,1024]{2,1,0:T(8,128)(2,1)S(1)}, u32[]{:S(2)}, u32[]{:S(2)}) collective-permute-start(bf16[3,128,1024]{2,1,0:T(8,128)(2,1)S(1)} %get-tuple-element.184), channel_id=1, source_target_pairs={{0,32},{1,97},{2,34},{3,99},{4,36},{5,101},{6,38},{7,103},{8,40},{... | collective-permute-start | bytes 2359304 | tf_op jit(solution)/shard_map/ppermute | solution.py:36
  98.3 9.3 %collective-permute-start.27 = (bf16[2,128,1024]{2,1,0:T(8,128)(2,1)S(1)}, bf16[2,128,1024]{2,1,0:T(8,128)(2,1)S(1)}, u32[]{:S(2)}, u32[]{:S(2)}) collective-permute-start(bf16[2,128,1024]{2,1,0:T(8,128)(2,1)S(1)} %pass_on.1), channel_id=1, source_target_pairs={{0,12},{1,5},{2,14},{3,7},{4,0},{5,9},{6,2},{7,11},{8,4},{9,13},{1... | collective-permute-start | bytes 1572872 | tf_op jit(solution)/shard_map/ppermute | solution.py:36
  100.7 13.1 %collective-permute-start.31 = (bf16[3,128,1024]{2,1,0:T(8,128)(2,1)S(1)}, bf16[3,128,1024]{2,1,0:T(8,128)(2,1)S(1)}, u32[]{:S(2)}, u32[]{:S(2)}) collective-permute-start(bf16[3,128,1024]{2,1,0:T(8,128)(2,1)S(1)} %add_convert_fusion), channel_id=1, source_target_pairs={{0,96},{1,33},{2,98},{3,35},{4,100},{5,37},{6,102},{7,39},{8,104},... | collective-permute-start | bytes 2359304 | tf_op jit(solution)/shard_map/ppermute | solution.py:36
  107.7 9.8 %collective-permute-start.28 = (bf16[128,1024]{1,0:T(8,128)(2,1)S(1)}, bf16[128,1024]{1,0:T(8,128)(2,1)S(1)}, u32[]{:S(2)}, u32[]{:S(2)}) collective-permute-start(bf16[128,1024]{1,0:T(8,128)(2,1)S(1)} %get-tuple-element.176), channel_id=1, source_target_pairs={{0,2},{1,3},{2,0},{3,1},{4,6},{5,7},{6,4},{7,5},{8,10},{9,11},{10,... | collective-permute-start | bytes 786440 | tf_op jit(solution)/shard_map/ppermute | solution.py:36
  (3 other events, 24.6 us)

commit v5 on v4

--- a/solution.py
+++ b/solution.py
@@ -160,18 +160,19 @@
 
 
 def backward_kernel(other, dests, refs):
-    mine, theirs, (s0, s1, s2) = refs[:3], refs[3:6], refs[6:9]
-    outs, turned = refs[9:-1], refs[-1]
+    mine, theirs, (s0, s1, s2) = refs[:4], refs[4:8], refs[8:11]
+    outs, turned = refs[11:-1], refs[-1]
     y, xl, z, xh, c, d = place()
     half = (xl + 1) % 2 if other else xl
     spots = {"far": y + 2, "back": y - d, "ahead": y + d, "here": y}
     for pieces, core in ((mine, c), (theirs, 1 - c)):
         way = 1 - 2 * core
-        beside = ((z - way, xh), (z + way, xh))
-        middle = ((z, xh), (z, xh + 1), (z - way, xh + 1), (z + way, xh + 1))
+        pair = ((z, xh), (z, xh + 1))
+        back = ((z - way, xh), (z - way, xh + 1))
+        ahead = ((z + way, xh), (z + way, xh + 1))
         across = ((z + 2, xh), (z + 2, xh + 1))
         for ref, j, (zz, hh) in (
-            (ref, j, at) for ref, ats in zip(pieces, (beside, middle, across)) for j, at in enumerate(ats)
+            (ref, j, at) for ref, ats in zip(pieces, (pair, back, ahead, across)) for j, at in enumerate(ats)
         ):
             token = (zz + 4) % 4 * 4 + hh % 2 * 2 + core
             lanes = pl.ds(pl.multiple_of(token * 128, 128), 128)
@@ -199,7 +200,7 @@
 
     return pl.pallas_call(
         kernel,
-        in_specs=[VMEM] * 9,
+        in_specs=[VMEM] * 11,
         out_specs=[VMEM] * count,
         out_shape=[out] * count,
         scratch_shapes=[pltpu.VMEM((128 * count, tokens), BF)],
@@ -320,38 +321,38 @@
     states = (low_state, mid_state, high_state)
     w, mt = prepare((w_low, w_mid, w_high), kv_grad, loss_mask)
     a1 = send(w, Y1)
+    a2 = send(w, Y2)
     x1 = send(w, XL)
     m_h = send(mt, XH)
-    m_1 = send(mt, Z1)
-    m_2 = send(mt, Z2)
     mt, *states = fence(mt, *states)
     states = load(*states)
 
-    a1, mt, m_h, m_1, m_2, w, *states = fence(a1, mt, m_h, m_1, m_2, w, *states)
+    mt, m_h, *states = fence(mt, m_h, *states)
+    pair = jnp.stack((mt, m_h))
+    z1 = send(pair, Z1)
+    z2 = send(pair, Z2)
+
+    a1, a2, w, pair = fence(a1, a2, w, pair)
     a3 = send(a1, Y1)
-    h_1 = send(m_h, Z1)
-    h_2 = send(m_h, Z2)
-    beside = jnp.stack((m_1, m_2))
-    beside_o = send(beside, CORE)
-
+    pair_o = send(pair, CORE)
     mine_a, theirs_a = forward(states, (w, a1))
 
-    a3, x1, h_1, h_2, beside_o, w, theirs_a, *states = fence(a3, x1, h_1, h_2, beside_o, w, theirs_a, *states)
-    a2 = send(w, Y2)
+    x1, z1, z2, pair_o, theirs_a, *states = fence(x1, z1, z2, pair_o, theirs_a, *states)
     b1 = send(x1, Y1)
     b3 = send(a3, XL)
-    across = send(jnp.stack((m_1, h_1)), Z1)
-    middle = jnp.stack((mt, m_h, h_1, h_2))
-    middle_o = send(middle, CORE)
+    across = send(z1, Z1)
+    z1_o = send(z1, CORE)
+    z2_o = send(z2, CORE)
     mine_b, theirs_b = forward(states, (x1, a3))
 
-    across, middle_o, x1, theirs_b = fence(across, middle_o, x1, theirs_b)
+    across, z1_o, z2_o, x1, theirs_b = fence(across, z1_o, z2_o, x1, theirs_b)
     across_o = send(across, CORE)
     b2 = send(x1, Y2)
-    masked = (beside, middle, across, beside_o, middle_o, across_o)
+    masked = (pair, z1, z2, across, pair_o, z1_o, z2_o, across_o)
     p2x, pmx, ppx, p0x = backward(states, masked, True, ("far", "back", "ahead", "here"))
 
-    a2, b1, b3, p2x, pmx, ppx, p0x, beside = fence(a2, b1, b3, p2x, pmx, ppx, p0x, beside)
+    b1, b3, p2x, pmx, ppx, p0x, pair = fence(b1, b3, p2x, pmx, ppx, p0x, pair)
+    masked = (pair, *masked[1:])
     e2 = send(pmx, Y2)
     e3 = send(ppx, Y1)
     e1 = send(p2x, XL)

time: 119 us -> 114 us (0.958)
  waiting for transfers between devices: 39.6 us -> 31.2 us
  starting transfers between devices: 36.9 us -> 41.4 us
    ppermute x33 -> x32, waiting for transfers between devices: 39.6 us -> 31.2 us  [send(): return lax.ppermute(array, FULL, pairs)]
    ppermute x33 -> x32, starting transfers between devices: 36.9 us -> 41.4 us  [send(): return lax.ppermute(array, FULL, pairs)]
  transfers between devices with their start and end apart: 33 -> 32, of which waited for: 15 -> 14; matrix products, arithmetic and copies ran while one was open for 1% -> 1% of each run, Pallas kernels for 31% -> 32%
where the time goes in v5:
time: 114 us
  starting transfers between devices  41.4 us (36%)
  Pallas kernels  39.6 us (35%)
  waiting for transfers between devices  31.2 us (27%)
    ppermute x32, starting transfers between devices, send(): return lax.ppermute(array, FULL, pairs)  41.4 us
    ppermute x32, waiting for transfers between devices, send(): return lax.ppermute(array, FULL, pairs)  31.2 us
    pallas_call x2, Pallas kernels, backward(): pl.pallas_call(kernel, in_specs=[VMEM] * 11, out_specs=[VMEM] * count, ou...  15 us
    pallas_call x4, Pallas kernels, forward(): pl.pallas_call(forward_kernel, in_specs=[VMEM] * 5, out_specs=[VMEM] * 2,...  14.7 us
    pallas_call x1, Pallas kernels, load(): pl.pallas_call(load_kernel, in_specs=[pl.BlockSpec(memory_space=pl.ANY)]...  4.68 us
  transfers between devices with their start and end apart: 32, of which 14 were waited for; matrix products, arithmetic and copies ran while one was open for 1% of the time, Pallas kernels for 32%

profile of v5, /device:TPU:0, one launch (start us, length us, event | category | flops | bytes accessed | tf_op | source)
XLA Modules:
  0.0 114.1 jit_solution(835361367017068068)
XLA Ops:
  0.6 2.2 %prepare.1 = (bf16[3072,128]{1,0:T(8,128)(2,1)}, bf16[1024,128]{1,0:T(8,128)(2,1)}) custom-call(bf16[1024,128]{1,0:T(8,128)(2,1)} %w0.1, bf16[1024,128]{1,0:T(8,128)(2,1)} %w1.1, bf16[1024,128]{1,0:T(8,128)(2,1)} %w2.1, bf16[128,1024]{1,0:T(8,128)(2,1)} %grad_ref.1, s32[1,128]{1,0:T(1,128)} %bitcast.5), custom_call_target="tpu_custom_call" | custom-call | flops 131 | bytes 2097 | tf_op jit(solution)/shard_map/prepare/pallas_call | solution.py:88
  2.8 3.2 %collective-permute-start.2 = (bf16[3072,128]{1,0:T(8,128)(2,1)}, bf16[3072,128]{1,0:T(8,128)(2,1)S(1)}, u32[]{:S(2)}, u32[]{:S(2)}) collective-permute-start(bf16[3072,128]{1,0:T(8,128)(2,1)} %get-tuple-element.111.wa), channel_id=1, source_target_pairs={{0,96},{1,33},{2,98},{3,35},{4,100},{5,37},{6,102},{7,39},{8,104},... | collective-permute-start | bytes 2359304 | tf_op jit(solution)/shard_map/ppermute | solution.py:36
  6.0 3.0 %collective-permute-start = (bf16[1024,128]{1,0:T(8,128)(2,1)}, bf16[1024,128]{1,0:T(8,128)(2,1)S(1)}, u32[]{:S(2)}, u32[]{:S(2)}) collective-permute-start(bf16[1024,128]{1,0:T(8,128)(2,1)} %get-tuple-element.109), channel_id=1, source_target_pairs={{0,2},{1,3},{2,0},{3,1},{4,6},{5,7},{6,4},{7,5},{8,10},{9,11},{10,... | collective-permute-start | bytes 786440 | tf_op jit(solution)/shard_map/ppermute | solution.py:36
  9.6 4.7 %load.1 = (bf16[2048,1024]{1,0:T(8,128)(2,1)S(1)}, bf16[2048,1024]{1,0:T(8,128)(2,1)S(1)}, bf16[2048,1024]{1,0:T(8,128)(2,1)S(1)}) custom-call(bf16[2048,1024]{1,0:T(8,128)(2,1)} %refs_0_, bf16[2048,1024]{1,0:T(8,128)(2,1)} %refs_1_, bf16[2048,1024]{1,0:T(8,128)(2,1)} %refs_2_), custom_call_target="tpu_custom_call" | custom-call | bytes 25165 | tf_op jit(solution)/shard_map/load/pallas_call | solution.py:116
  14.3 2.6 %collective-permute-done = bf16[1024,128]{1,0:T(8,128)(2,1)S(1)} collective-permute-done((bf16[1024,128]{1,0:T(8,128)(2,1)}, bf16[1024,128]{1,0:T(8,128)(2,1)S(1)}, u32[]{:S(2)}, u32[]{:S(2)}) %collective-permute-start) | collective-permute-done | bytes 262176 | tf_op jit(solution)/shard_map/ppermute | solution.py:36
  17.0 4.1 %collective-permute-start.5 = (bf16[2,1024,128]{2,1,0:T(8,128)(2,1)S(1)}, bf16[2,1024,128]{2,1,0:T(8,128)(2,1)S(1)}, u32[]{:S(2)}, u32[]{:S(2)}) collective-permute-start(bf16[2,1024,128]{2,1,0:T(8,128)(2,1)S(1)} %pad_maximum_fusion.refs_0_), channel_id=1, source_target_pairs={{0,12},{1,5},{2,14},{3,7},{4,0},{5,9},{6,2},{7,11},{8,4},{9,13},{1... | collective-permute-start | bytes 1572872 | tf_op jit(solution)/shard_map/ppermute | solution.py:36
  21.1 2.2 %collective-permute-done.2.wa = bf16[3072,128]{1,0:T(8,128)(2,1)S(1)} collective-permute-done((bf16[3072,128]{1,0:T(8,128)(2,1)}, bf16[3072,128]{1,0:T(8,128)(2,1)S(1)}, u32[]{:S(2)}, u32[]{:S(2)}) %collective-permute-start.2) | collective-permute-done | bytes 786464 | tf_op jit(solution)/shard_map/ppermute | solution.py:36
  23.8 1.6 %collective-permute-start.7 = (bf16[3072,128]{1,0:T(8,128)(2,1)S(1)}, bf16[3072,128]{1,0:T(8,128)(2,1)S(1)}, u32[]{:S(2)}, u32[]{:S(2)}) collective-permute-start(bf16[3072,128]{1,0:T(8,128)(2,1)S(1)} %collective-permute-done.1.wb), channel_id=1, source_target_pairs={{0,32},{1,97},{2,34},{3,99},{4,36},{5,101},{6,38},{7,103},{8,40},{... | collective-permute-start | bytes 2359304 | tf_op jit(solution)/shard_map/ppermute | solution.py:36
  25.3 3.7 %forward.4 = (bf16[4,2,128,256]{3,2,1,0:T(8,128)(2,1)S(1)}, bf16[4,2,128,256]{3,2,1,0:T(8,128)(2,1)S(1)}) custom-call(bf16[2048,1024]{1,0:T(8,128)(2,1)S(1)} %get-tuple-element.116.s0.refs_8_, bf16[2048,1024]{1,0:T(8,128)(2,1)S(1)} %get-tuple-element.117.s1.refs_9_, bf16[2048,1024]{1,0:T(8,128)(2,1)S(1)} %get-tuple-element.118.s2.refs_10_, ...), custom_call_target="tpu_custom_call" | custom-call | flops 3221225 | bytes 14680 | tf_op jit(solution)/shard_map/forward/pallas_call | solution.py:150
  33.0 1.9 %collective-permute-start.9 = (bf16[2,1024,128]{2,1,0:T(8,128)(2,1)S(1)}, bf16[2,1024,128]{2,1,0:T(8,128)(2,1)S(1)}, u32[]{:S(2)}, u32[]{:S(2)}) collective-permute-start(bf16[2,1024,128]{2,1,0:T(8,128)(2,1)S(1)} %collective-permute-done.4.refs_1_), channel_id=1, source_target_pairs={{0,4},{1,13},{2,6},{3,15},{4,8},{5,1},{6,10},{7,3},{8,12},{9,5},{1... | collective-permute-start | bytes 1572872 | tf_op jit(solution)/shard_map/ppermute | solution.py:36
  35.2 1.8 %collective-permute-done.7.wb = bf16[3072,128]{1,0:T(8,128)(2,1)S(1)} collective-permute-done((bf16[3072,128]{1,0:T(8,128)(2,1)S(1)}, bf16[3072,128]{1,0:T(8,128)(2,1)S(1)}, u32[]{:S(2)}, u32[]{:S(2)}) %collective-permute-start.7) | collective-permute-done | bytes 786464 | tf_op jit(solution)/shard_map/ppermute | solution.py:36
  37.0 1.5 %collective-permute-start.14 = (bf16[3072,128]{1,0:T(8,128)(2,1)S(1)}, bf16[3072,128]{1,0:T(8,128)(2,1)S(1)}, u32[]{:S(2)}, u32[]{:S(2)}) collective-permute-start(bf16[3072,128]{1,0:T(8,128)(2,1)S(1)} %collective-permute-done.7.wb), channel_id=1, source_target_pairs={{0,16},{1,17},{2,18},{3,19},{4,20},{5,21},{6,22},{7,23},{8,24},{9,... | collective-permute-start | bytes 2359304 | tf_op jit(solution)/shard_map/ppermute | solution.py:36
  38.5 3.7 %forward.5 = (bf16[4,2,128,256]{3,2,1,0:T(8,128)(2,1)S(1)}, bf16[4,2,128,256]{3,2,1,0:T(8,128)(2,1)S(1)}) custom-call(bf16[2048,1024]{1,0:T(8,128)(2,1)S(1)} %get-tuple-element.116.s0.refs_8_, bf16[2048,1024]{1,0:T(8,128)(2,1)S(1)} %get-tuple-element.117.s1.refs_9_, bf16[2048,1024]{1,0:T(8,128)(2,1)S(1)} %get-tuple-element.118.s2.refs_10_, ...), custom_call_target="tpu_custom_call" | custom-call | flops 3221225 | bytes 14680 | tf_op jit(solution)/shard_map/forward/pallas_call | solution.py:150
  42.2 2.1 %collective-permute-done.9.refs_3_ = bf16[2,1024,128]{2,1,0:T(8,128)(2,1)S(1)} collective-permute-done((bf16[2,1024,128]{2,1,0:T(8,128)(2,1)S(1)}, bf16[2,1024,128]{2,1,0:T(8,128)(2,1)S(1)}, u32[]{:S(2)}, u32[]{:S(2)}) %collective-permute-start.9) | collective-permute-done | bytes 524320 | tf_op jit(solution)/shard_map/ppermute | solution.py:36
  44.7 1.7 %collective-permute-start.16 = (bf16[3072,128]{1,0:T(8,128)(2,1)S(1)}, bf16[3072,128]{1,0:T(8,128)(2,1)S(1)}, u32[]{:S(2)}, u32[]{:S(2)}) collective-permute-start(bf16[3072,128]{1,0:T(8,128)(2,1)S(1)} %collective-permute-done.3.wa), channel_id=1, source_target_pairs={{0,96},{1,33},{2,98},{3,35},{4,100},{5,37},{6,102},{7,39},{8,104},... | collective-permute-start | bytes 2359304 | tf_op jit(solution)/shard_map/ppermute | solution.py:36
  46.4 7.5 %backward.2 = (bf16[3,128,1024]{2,1,0:T(8,128)(2,1)S(1)}, bf16[3,128,1024]{2,1,0:T(8,128)(2,1)S(1)}, bf16[3,128,1024]{2,1,0:T(8,128)(2,1)S(1)}, bf16[3,128,1024]{2,1,0:T(8,128)(2,1)S(1)}) custom-call(bf16[2,1024,128]{2,1,0:T(8,128)(2,1)S(1)} %pad_maximum_fusion.refs_0_, bf16[2,1024,128]{2,1,0:T(8,128)(2,1)S(1)} %collective-permute-done.4.refs_1_, ...), custom_call_target="tpu_custom_call" | custom-call | flops 6442450 | bytes 20971 | tf_op jit(solution)/shard_map/backward/pallas_call | solution.py:201
  53.9 3.2 %collective-permute-done.14.wa = bf16[3072,128]{1,0:T(8,128)(2,1)S(1)} collective-permute-done((bf16[3072,128]{1,0:T(8,128)(2,1)S(1)}, bf16[3072,128]{1,0:T(8,128)(2,1)S(1)}, u32[]{:S(2)}, u32[]{:S(2)}) %collective-permute-start.14) | collective-permute-done | bytes 786464 | tf_op jit(solution)/shard_map/ppermute | solution.py:36
  57.1 1.6 %collective-permute-start.17 = (bf16[3,128,1024]{2,1,0:T(8,128)(2,1)S(1)}, bf16[3,128,1024]{2,1,0:T(8,128)(2,1)S(1)}, u32[]{:S(2)}, u32[]{:S(2)}) collective-permute-start(bf16[3,128,1024]{2,1,0:T(8,128)(2,1)S(1)} %get-tuple-element.149), channel_id=1, source_target_pairs={{0,16},{1,17},{2,18},{3,19},{4,20},{5,21},{6,22},{7,23},{8,24},{9,... | collective-permute-start | bytes 2359304 | tf_op jit(solution)/shard_map/ppermute | solution.py:36
  58.7 1.6 %collective-permute-start.18 = (bf16[3,128,1024]{2,1,0:T(8,128)(2,1)S(1)}, bf16[3,128,1024]{2,1,0:T(8,128)(2,1)S(1)}, u32[]{:S(2)}, u32[]{:S(2)}) collective-permute-start(bf16[3,128,1024]{2,1,0:T(8,128)(2,1)S(1)} %get-tuple-element.150), channel_id=1, source_target_pairs={{0,96},{1,33},{2,98},{3,35},{4,100},{5,37},{6,102},{7,39},{8,104},... | collective-permute-start | bytes 2359304 | tf_op jit(solution)/shard_map/ppermute | solution.py:36
  61.2 7.5 %backward.3 = (bf16[3,128,1024]{2,1,0:T(8,128)(2,1)S(1)}, bf16[3,128,1024]{2,1,0:T(8,128)(2,1)S(1)}, bf16[3,128,1024]{2,1,0:T(8,128)(2,1)S(1)}, bf16[3,128,1024]{2,1,0:T(8,128)(2,1)S(1)}) custom-call(bf16[2,1024,128]{2,1,0:T(8,128)(2,1)S(1)} %pad_maximum_fusion.refs_0_, bf16[2,1024,128]{2,1,0:T(8,128)(2,1)S(1)} %collective-permute-done.4.refs_1_, ...), custom_call_target="tpu_custom_call" | custom-call | flops 6442450 | bytes 20971 | tf_op jit(solution)/shard_map/backward/pallas_call | solution.py:201
  69.0 3.3 %collective-permute-start.20 = (bf16[2,128,384]{2,1,0:T(8,128)(2,1)S(1)}, bf16[2,128,384]{2,1,0:T(8,128)(2,1)S(1)}, u32[]{:S(2)}, u32[]{:S(2)}) collective-permute-start(bf16[2,128,384]{2,1,0:T(8,128)(2,1)S(1)} %get-tuple-element.152), channel_id=1, source_target_pairs={{0,12},{1,5},{2,14},{3,7},{4,0},{5,9},{6,2},{7,11},{8,4},{9,13},{1... | collective-permute-start | bytes 589832 | tf_op jit(solution)/shard_map/ppermute | solution.py:36
  72.3 3.7 %forward.6 = (bf16[4,2,128,256]{3,2,1,0:T(8,128)(2,1)S(1)}, bf16[4,2,128,256]{3,2,1,0:T(8,128)(2,1)S(1)}) custom-call(bf16[2048,1024]{1,0:T(8,128)(2,1)S(1)} %get-tuple-element.116.s0.refs_8_, bf16[2048,1024]{1,0:T(8,128)(2,1)S(1)} %get-tuple-element.117.s1.refs_9_, bf16[2048,1024]{1,0:T(8,128)(2,1)S(1)} %get-tuple-element.118.s2.refs_10_, ...), custom_call_target="tpu_custom_call" | custom-call | flops 3221225 | bytes 14680 | tf_op jit(solution)/shard_map/forward/pallas_call | solution.py:150
  75.9 3.7 %forward.7 = (bf16[4,2,128,256]{3,2,1,0:T(8,128)(2,1)S(1)}, bf16[4,2,128,256]{3,2,1,0:T(8,128)(2,1)S(1)}) custom-call(bf16[2048,1024]{1,0:T(8,128)(2,1)S(1)} %get-tuple-element.116.s0.refs_8_, bf16[2048,1024]{1,0:T(8,128)(2,1)S(1)} %get-tuple-element.117.s1.refs_9_, bf16[2048,1024]{1,0:T(8,128)(2,1)S(1)} %get-tuple-element.118.s2.refs_10_, ...), custom_call_target="tpu_custom_call" | custom-call | flops 3221225 | bytes 14680 | tf_op jit(solution)/shard_map/forward/pallas_call | solution.py:150
  80.6 3.3 %collective-permute-start.29 = (bf16[3,128,1024]{2,1,0:T(8,128)(2,1)S(1)}, bf16[3,128,1024]{2,1,0:T(8,128)(2,1)S(1)}, u32[]{:S(2)}, u32[]{:S(2)}) collective-permute-start(bf16[3,128,1024]{2,1,0:T(8,128)(2,1)S(1)} %add_convert_fusion.1), channel_id=1, source_target_pairs={{0,96},{1,33},{2,98},{3,35},{4,100},{5,37},{6,102},{7,39},{8,104},... | collective-permute-start | bytes 2359304 | tf_op jit(solution)/shard_map/ppermute | solution.py:36
  84.3 3.2 %collective-permute-start.24 = (bf16[2,128,640]{2,1,0:T(8,128)(2,1)S(1)}, bf16[2,128,640]{2,1,0:T(8,128)(2,1)S(1)}, u32[]{:S(2)}, u32[]{:S(2)}) collective-permute-start(bf16[2,128,640]{2,1,0:T(8,128)(2,1)S(1)} %get-tuple-element.163), channel_id=1, source_target_pairs={{0,12},{1,5},{2,14},{3,7},{4,0},{5,9},{6,2},{7,11},{8,4},{9,13},{1... | collective-permute-start | bytes 983048 | tf_op jit(solution)/shard_map/ppermute | solution.py:36
  88.6 4.9 %collective-permute-done.24.tb = bf16[2,128,640]{2,1,0:T(8,128)(2,1)S(1)} collective-permute-done((bf16[2,128,640]{2,1,0:T(8,128)(2,1)S(1)}, bf16[2,128,640]{2,1,0:T(8,128)(2,1)S(1)}, u32[]{:S(2)}, u32[]{:S(2)}) %collective-permute-start.24) | collective-permute-done | bytes 327712 | tf_op jit(solution)/shard_map/ppermute | solution.py:36
  93.4 2.4 %collective-permute-done.25.c1 = bf16[2,128,640]{2,1,0:T(8,128)(2,1)S(1)} collective-permute-done((bf16[2,128,640]{2,1,0:T(8,128)(2,1)S(1)}, bf16[2,128,640]{2,1,0:T(8,128)(2,1)S(1)}, u32[]{:S(2)}, u32[]{:S(2)}) %collective-permute-start.25) | collective-permute-done | bytes 327712 | tf_op jit(solution)/shard_map/ppermute | solution.py:36
  97.6 3.3 %collective-permute-start.30 = (bf16[3,128,1024]{2,1,0:T(8,128)(2,1)S(1)}, bf16[3,128,1024]{2,1,0:T(8,128)(2,1)S(1)}, u32[]{:S(2)}, u32[]{:S(2)}) collective-permute-start(bf16[3,128,1024]{2,1,0:T(8,128)(2,1)S(1)} %add_convert_fusion), channel_id=1, source_target_pairs={{0,96},{1,33},{2,98},{3,35},{4,100},{5,37},{6,102},{7,39},{8,104},... | collective-permute-start | bytes 2359304 | tf_op jit(solution)/shard_map/ppermute | solution.py:36
  100.9 4.2 %collective-permute-done.26.b = bf16[2,128,1024]{2,1,0:T(8,128)(2,1)S(1)} collective-permute-done((bf16[2,128,1024]{2,1,0:T(8,128)(2,1)S(1)}, bf16[2,128,1024]{2,1,0:T(8,128)(2,1)S(1)}, u32[]{:S(2)}, u32[]{:S(2)}) %collective-permute-start.26) | collective-permute-done | bytes 524320 | tf_op jit(solution)/shard_map/ppermute | solution.py:36
  105.4 2.8 %collective-permute-start.27 = (bf16[128,1024]{1,0:T(8,128)(2,1)S(1)}, bf16[128,1024]{1,0:T(8,128)(2,1)S(1)}, u32[]{:S(2)}, u32[]{:S(2)}) collective-permute-start(bf16[128,1024]{1,0:T(8,128)(2,1)S(1)} %get-tuple-element.174), channel_id=1, source_target_pairs={{0,2},{1,3},{2,0},{3,1},{4,6},{5,7},{6,4},{7,5},{8,10},{9,11},{10,... | collective-permute-start | bytes 786440 | tf_op jit(solution)/shard_map/ppermute | solution.py:36
  108.2 2.2 %collective-permute-done.30.c = bf16[3,128,1024]{2,1,0:T(8,128)(2,1)S(1)} collective-permute-done((bf16[3,128,1024]{2,1,0:T(8,128)(2,1)S(1)}, bf16[3,128,1024]{2,1,0:T(8,128)(2,1)S(1)}, u32[]{:S(2)}, u32[]{:S(2)}) %collective-permute-start.30) | collective-permute-done | bytes 786464 | tf_op jit(solution)/shard_map/ppermute | solution.py:36
  111.7 1.6 %collective-permute-done.27.b = bf16[128,1024]{1,0:T(8,128)(2,1)S(1)} collective-permute-done((bf16[128,1024]{1,0:T(8,128)(2,1)S(1)}, bf16[128,1024]{1,0:T(8,128)(2,1)S(1)}, u32[]{:S(2)}, u32[]{:S(2)}) %collective-permute-start.27) | collective-permute-done | bytes 262176 | tf_op jit(solution)/shard_map/ppermute | solution.py:36
  (54 shorter events, 13.5 us)
Async XLA Ops:
  2.8 20.4 %collective-permute-start.2 = (bf16[3072,128]{1,0:T(8,128)(2,1)}, bf16[3072,128]{1,0:T(8,128)(2,1)S(1)}, u32[]{:S(2)}, u32[]{:S(2)}) collective-permute-start(bf16[3072,128]{1,0:T(8,128)(2,1)} %get-tuple-element.111.wa), channel_id=1, source_target_pairs={{0,96},{1,33},{2,98},{3,35},{4,100},{5,37},{6,102},{7,39},{8,104},... | collective-permute-start | bytes 2359304 | tf_op jit(solution)/shard_map/ppermute | solution.py:36
  6.0 17.8 %collective-permute-start.1 = (bf16[3072,128]{1,0:T(8,128)(2,1)}, bf16[3072,128]{1,0:T(8,128)(2,1)S(1)}, u32[]{:S(2)}, u32[]{:S(2)}) collective-permute-start(bf16[3072,128]{1,0:T(8,128)(2,1)} %get-tuple-element.111.wa), channel_id=1, source_target_pairs={{0,32},{1,97},{2,34},{3,99},{4,36},{5,101},{6,38},{7,103},{8,40},{... | collective-permute-start | bytes 2359304 | tf_op jit(solution)/shard_map/ppermute | solution.py:36
  6.0 10.9 %collective-permute-start = (bf16[1024,128]{1,0:T(8,128)(2,1)}, bf16[1024,128]{1,0:T(8,128)(2,1)S(1)}, u32[]{:S(2)}, u32[]{:S(2)}) collective-permute-start(bf16[1024,128]{1,0:T(8,128)(2,1)} %get-tuple-element.109), channel_id=1, source_target_pairs={{0,2},{1,3},{2,0},{3,1},{4,6},{5,7},{6,4},{7,5},{8,10},{9,11},{10,... | collective-permute-start | bytes 786440 | tf_op jit(solution)/shard_map/ppermute | solution.py:36
  9.0 23.5 %collective-permute-start.3 = (bf16[3072,128]{1,0:T(8,128)(2,1)}, bf16[3072,128]{1,0:T(8,128)(2,1)S(1)}, u32[]{:S(2)}, u32[]{:S(2)}) collective-permute-start(bf16[3072,128]{1,0:T(8,128)(2,1)} %get-tuple-element.111.wa), channel_id=1, source_target_pairs={{0,16},{1,17},{2,18},{3,19},{4,20},{5,21},{6,22},{7,23},{8,24},{9,... | collective-permute-start | bytes 2359304 | tf_op jit(solution)/shard_map/ppermute | solution.py:36
  17.0 13.1 %collective-permute-start.5 = (bf16[2,1024,128]{2,1,0:T(8,128)(2,1)S(1)}, bf16[2,1024,128]{2,1,0:T(8,128)(2,1)S(1)}, u32[]{:S(2)}, u32[]{:S(2)}) collective-permute-start(bf16[2,1024,128]{2,1,0:T(8,128)(2,1)S(1)} %pad_maximum_fusion.refs_0_), channel_id=1, source_target_pairs={{0,12},{1,5},{2,14},{3,7},{4,0},{5,9},{6,2},{7,11},{8,4},{9,13},{1... | collective-permute-start | bytes 1572872 | tf_op jit(solution)/shard_map/ppermute | solution.py:36
  21.1 10.4 %collective-permute-start.4 = (bf16[2,1024,128]{2,1,0:T(8,128)(2,1)S(1)}, bf16[2,1024,128]{2,1,0:T(8,128)(2,1)S(1)}, u32[]{:S(2)}, u32[]{:S(2)}) collective-permute-start(bf16[2,1024,128]{2,1,0:T(8,128)(2,1)S(1)} %pad_maximum_fusion.refs_0_), channel_id=1, source_target_pairs={{0,4},{1,13},{2,6},{3,15},{4,8},{5,1},{6,10},{7,3},{8,12},{9,5},{1... | collective-permute-start | bytes 1572872 | tf_op jit(solution)/shard_map/ppermute | solution.py:36
  23.8 8.8 %collective-permute-start.6 = (bf16[2,1024,128]{2,1,0:T(8,128)(2,1)S(1)}, bf16[2,1024,128]{2,1,0:T(8,128)(2,1)S(1)}, u32[]{:S(2)}, u32[]{:S(2)}) collective-permute-start(bf16[2,1024,128]{2,1,0:T(8,128)(2,1)S(1)} %pad_maximum_fusion.refs_0_), channel_id=1, source_target_pairs={{0,1},{1,0},{2,3},{3,2},{4,5},{5,4},{6,7},{7,6},{8,9},{9,8},{10,11... | collective-permute-start | bytes 1572872 | tf_op jit(solution)/shard_map/ppermute | solution.py:36
  23.8 13.2 %collective-permute-start.7 = (bf16[3072,128]{1,0:T(8,128)(2,1)S(1)}, bf16[3072,128]{1,0:T(8,128)(2,1)S(1)}, u32[]{:S(2)}, u32[]{:S(2)}) collective-permute-start(bf16[3072,128]{1,0:T(8,128)(2,1)S(1)} %collective-permute-done.1.wb), channel_id=1, source_target_pairs={{0,32},{1,97},{2,34},{3,99},{4,36},{5,101},{6,38},{7,103},{8,40},{... | collective-permute-start | bytes 2359304 | tf_op jit(solution)/shard_map/ppermute | solution.py:36
  32.5 9.6 %collective-permute-start.11 = (bf16[2,1024,128]{2,1,0:T(8,128)(2,1)S(1)}, bf16[2,1024,128]{2,1,0:T(8,128)(2,1)S(1)}, u32[]{:S(2)}, u32[]{:S(2)}) collective-permute-start(bf16[2,1024,128]{2,1,0:T(8,128)(2,1)S(1)} %collective-permute-done.5.refs_2_), channel_id=1, source_target_pairs={{0,1},{1,0},{2,3},{3,2},{4,5},{5,4},{6,7},{7,6},{8,9},{9,8},{10,11... | collective-permute-start | bytes 1572872 | tf_op jit(solution)/shard_map/ppermute | solution.py:36
  32.5 9.6 %collective-permute-start.10 = (bf16[2,1024,128]{2,1,0:T(8,128)(2,1)S(1)}, bf16[2,1024,128]{2,1,0:T(8,128)(2,1)S(1)}, u32[]{:S(2)}, u32[]{:S(2)}) collective-permute-start(bf16[2,1024,128]{2,1,0:T(8,128)(2,1)S(1)} %collective-permute-done.4.refs_1_), channel_id=1, source_target_pairs={{0,1},{1,0},{2,3},{3,2},{4,5},{5,4},{6,7},{7,6},{8,9},{9,8},{10,11... | collective-permute-start | bytes 1572872 | tf_op jit(solution)/shard_map/ppermute | solution.py:36
  33.0 11.2 %collective-permute-start.9 = (bf16[2,1024,128]{2,1,0:T(8,128)(2,1)S(1)}, bf16[2,1024,128]{2,1,0:T(8,128)(2,1)S(1)}, u32[]{:S(2)}, u32[]{:S(2)}) collective-permute-start(bf16[2,1024,128]{2,1,0:T(8,128)(2,1)S(1)} %collective-permute-done.4.refs_1_), channel_id=1, source_target_pairs={{0,4},{1,13},{2,6},{3,15},{4,8},{5,1},{6,10},{7,3},{8,12},{9,5},{1... | collective-permute-start | bytes 1572872 | tf_op jit(solution)/shard_map/ppermute | solution.py:36
  35.0 19.0 %collective-permute-start.13 = (bf16[3072,128]{1,0:T(8,128)(2,1)S(1)}, bf16[3072,128]{1,0:T(8,128)(2,1)S(1)}, u32[]{:S(2)}, u32[]{:S(2)}) collective-permute-start(bf16[3072,128]{1,0:T(8,128)(2,1)S(1)} %collective-permute-done.3.wa), channel_id=1, source_target_pairs={{0,32},{1,97},{2,34},{3,99},{4,36},{5,101},{6,38},{7,103},{8,40},{... | collective-permute-start | bytes 2359304 | tf_op jit(solution)/shard_map/ppermute | solution.py:36
  37.0 20.2 %collective-permute-start.14 = (bf16[3072,128]{1,0:T(8,128)(2,1)S(1)}, bf16[3072,128]{1,0:T(8,128)(2,1)S(1)}, u32[]{:S(2)}, u32[]{:S(2)}) collective-permute-start(bf16[3072,128]{1,0:T(8,128)(2,1)S(1)} %collective-permute-done.7.wb), channel_id=1, source_target_pairs={{0,16},{1,17},{2,18},{3,19},{4,20},{5,21},{6,22},{7,23},{8,24},{9,... | collective-permute-start | bytes 2359304 | tf_op jit(solution)/shard_map/ppermute | solution.py:36
  44.2 2.2 %collective-permute-start.15 = (bf16[2,1024,128]{2,1,0:T(8,128)(2,1)S(1)}, bf16[2,1024,128]{2,1,0:T(8,128)(2,1)S(1)}, u32[]{:S(2)}, u32[]{:S(2)}) collective-permute-start(bf16[2,1024,128]{2,1,0:T(8,128)(2,1)S(1)} %collective-permute-done.9.refs_3_), channel_id=1, source_target_pairs={{0,1},{1,0},{2,3},{3,2},{4,5},{5,4},{6,7},{7,6},{8,9},{9,8},{10,11... | collective-permute-start | bytes 1572872 | tf_op jit(solution)/shard_map/ppermute | solution.py:36
  44.2 16.5 %collective-permute-start.8 = (bf16[4,2,128,256]{3,2,1,0:T(8,128)(2,1)S(1)}, bf16[4,2,128,256]{3,2,1,0:T(8,128)(2,1)S(1)}, u32[]{:S(2)}, u32[]{:S(2)}) collective-permute-start(bf16[4,2,128,256]{3,2,1,0:T(8,128)(2,1)S(1)} %get-tuple-element.121), channel_id=1, source_target_pairs={{0,1},{1,0},{2,3},{3,2},{4,5},{5,4},{6,7},{7,6},{8,9},{9,8},{10,11... | collective-permute-start | bytes 1572872 | tf_op jit(solution)/shard_map/ppermute | solution.py:36
  44.7 27.5 %collective-permute-start.16 = (bf16[3072,128]{1,0:T(8,128)(2,1)S(1)}, bf16[3072,128]{1,0:T(8,128)(2,1)S(1)}, u32[]{:S(2)}, u32[]{:S(2)}) collective-permute-start(bf16[3072,128]{1,0:T(8,128)(2,1)S(1)} %collective-permute-done.3.wa), channel_id=1, source_target_pairs={{0,96},{1,33},{2,98},{3,35},{4,100},{5,37},{6,102},{7,39},{8,104},... | collective-permute-start | bytes 2359304 | tf_op jit(solution)/shard_map/ppermute | solution.py:36
  57.1 22.5 %collective-permute-start.17 = (bf16[3,128,1024]{2,1,0:T(8,128)(2,1)S(1)}, bf16[3,128,1024]{2,1,0:T(8,128)(2,1)S(1)}, u32[]{:S(2)}, u32[]{:S(2)}) collective-permute-start(bf16[3,128,1024]{2,1,0:T(8,128)(2,1)S(1)} %get-tuple-element.149), channel_id=1, source_target_pairs={{0,16},{1,17},{2,18},{3,19},{4,20},{5,21},{6,22},{7,23},{8,24},{9,... | collective-permute-start | bytes 2359304 | tf_op jit(solution)/shard_map/ppermute | solution.py:36
  58.7 21.0 %collective-permute-start.18 = (bf16[3,128,1024]{2,1,0:T(8,128)(2,1)S(1)}, bf16[3,128,1024]{2,1,0:T(8,128)(2,1)S(1)}, u32[]{:S(2)}, u32[]{:S(2)}) collective-permute-start(bf16[3,128,1024]{2,1,0:T(8,128)(2,1)S(1)} %get-tuple-element.150), channel_id=1, source_target_pairs={{0,96},{1,33},{2,98},{3,35},{4,100},{5,37},{6,102},{7,39},{8,104},... | collective-permute-start | bytes 2359304 | tf_op jit(solution)/shard_map/ppermute | solution.py:36
  60.3 19.4 %collective-permute-start.19 = (bf16[3,128,1024]{2,1,0:T(8,128)(2,1)S(1)}, bf16[3,128,1024]{2,1,0:T(8,128)(2,1)S(1)}, u32[]{:S(2)}, u32[]{:S(2)}) collective-permute-start(bf16[3,128,1024]{2,1,0:T(8,128)(2,1)S(1)} %get-tuple-element.151), channel_id=1, source_target_pairs={{0,32},{1,97},{2,34},{3,99},{4,36},{5,101},{6,38},{7,103},{8,40},{... | collective-permute-start | bytes 2359304 | tf_op jit(solution)/shard_map/ppermute | solution.py:36
  60.7 8.0 %collective-permute-start.12 = (bf16[4,2,128,256]{3,2,1,0:T(8,128)(2,1)S(1)}, bf16[4,2,128,256]{3,2,1,0:T(8,128)(2,1)S(1)}, u32[]{:S(2)}, u32[]{:S(2)}) collective-permute-start(bf16[4,2,128,256]{3,2,1,0:T(8,128)(2,1)S(1)} %get-tuple-element.125), channel_id=1, source_target_pairs={{0,1},{1,0},{2,3},{3,2},{4,5},{5,4},{6,7},{7,6},{8,9},{9,8},{10,11... | collective-permute-start | bytes 1572872 | tf_op jit(solution)/shard_map/ppermute | solution.py:36
  69.0 10.7 %collective-permute-start.20 = (bf16[2,128,384]{2,1,0:T(8,128)(2,1)S(1)}, bf16[2,128,384]{2,1,0:T(8,128)(2,1)S(1)}, u32[]{:S(2)}, u32[]{:S(2)}) collective-permute-start(bf16[2,128,384]{2,1,0:T(8,128)(2,1)S(1)} %get-tuple-element.152), channel_id=1, source_target_pairs={{0,12},{1,5},{2,14},{3,7},{4,0},{5,9},{6,2},{7,11},{8,4},{9,13},{1... | collective-permute-start | bytes 589832 | tf_op jit(solution)/shard_map/ppermute | solution.py:36
  72.3 7.4 %collective-permute-start.21 = (bf16[2,128,384]{2,1,0:T(8,128)(2,1)S(1)}, bf16[2,128,384]{2,1,0:T(8,128)(2,1)S(1)}, u32[]{:S(2)}, u32[]{:S(2)}) collective-permute-start(bf16[2,128,384]{2,1,0:T(8,128)(2,1)S(1)} %get-tuple-element.153), channel_id=1, source_target_pairs={{0,4},{1,13},{2,6},{3,15},{4,8},{5,1},{6,10},{7,3},{8,12},{9,5},{1... | collective-permute-start | bytes 589832 | tf_op jit(solution)/shard_map/ppermute | solution.py:36
  79.7 4.3 %collective-permute-start.22 = (bf16[4,2,128,256]{3,2,1,0:T(8,128)(2,1)S(1)}, bf16[4,2,128,256]{3,2,1,0:T(8,128)(2,1)S(1)}, u32[]{:S(2)}, u32[]{:S(2)}) collective-permute-start(bf16[4,2,128,256]{3,2,1,0:T(8,128)(2,1)S(1)} %get-tuple-element.160), channel_id=1, source_target_pairs={{0,1},{1,0},{2,3},{3,2},{4,5},{5,4},{6,7},{7,6},{8,9},{9,8},{10,11... | collective-permute-start | bytes 1572872 | tf_op jit(solution)/shard_map/ppermute | solution.py:36
  80.2 3.7 %collective-permute-start.23 = (bf16[4,2,128,256]{3,2,1,0:T(8,128)(2,1)S(1)}, bf16[4,2,128,256]{3,2,1,0:T(8,128)(2,1)S(1)}, u32[]{:S(2)}, u32[]{:S(2)}) collective-permute-start(bf16[4,2,128,256]{3,2,1,0:T(8,128)(2,1)S(1)} %get-tuple-element.161), channel_id=1, source_target_pairs={{0,1},{1,0},{2,3},{3,2},{4,5},{5,4},{6,7},{7,6},{8,9},{9,8},{10,11... | collective-permute-start | bytes 1572872 | tf_op jit(solution)/shard_map/ppermute | solution.py:36
  80.6 16.7 %collective-permute-start.29 = (bf16[3,128,1024]{2,1,0:T(8,128)(2,1)S(1)}, bf16[3,128,1024]{2,1,0:T(8,128)(2,1)S(1)}, u32[]{:S(2)}, u32[]{:S(2)}) collective-permute-start(bf16[3,128,1024]{2,1,0:T(8,128)(2,1)S(1)} %add_convert_fusion.1), channel_id=1, source_target_pairs={{0,96},{1,33},{2,98},{3,35},{4,100},{5,37},{6,102},{7,39},{8,104},... | collective-permute-start | bytes 2359304 | tf_op jit(solution)/shard_map/ppermute | solution.py:36
  84.3 9.1 %collective-permute-start.24 = (bf16[2,128,640]{2,1,0:T(8,128)(2,1)S(1)}, bf16[2,128,640]{2,1,0:T(8,128)(2,1)S(1)}, u32[]{:S(2)}, u32[]{:S(2)}) collective-permute-start(bf16[2,128,640]{2,1,0:T(8,128)(2,1)S(1)} %get-tuple-element.163), channel_id=1, source_target_pairs={{0,12},{1,5},{2,14},{3,7},{4,0},{5,9},{6,2},{7,11},{8,4},{9,13},{1... | collective-permute-start | bytes 983048 | tf_op jit(solution)/shard_map/ppermute | solution.py:36
  87.5 8.3 %collective-permute-start.25 = (bf16[2,128,640]{2,1,0:T(8,128)(2,1)S(1)}, bf16[2,128,640]{2,1,0:T(8,128)(2,1)S(1)}, u32[]{:S(2)}, u32[]{:S(2)}) collective-permute-start(bf16[2,128,640]{2,1,0:T(8,128)(2,1)S(1)} %get-tuple-element.164), channel_id=1, source_target_pairs={{0,4},{1,13},{2,6},{3,15},{4,8},{5,1},{6,10},{7,3},{8,12},{9,5},{1... | collective-permute-start | bytes 983048 | tf_op jit(solution)/shard_map/ppermute | solution.py:36
  87.9 20.2 %collective-permute-start.28 = (bf16[3,128,1024]{2,1,0:T(8,128)(2,1)S(1)}, bf16[3,128,1024]{2,1,0:T(8,128)(2,1)S(1)}, u32[]{:S(2)}, u32[]{:S(2)}) collective-permute-start(bf16[3,128,1024]{2,1,0:T(8,128)(2,1)S(1)} %add_convert_fusion.2), channel_id=1, source_target_pairs={{0,16},{1,17},{2,18},{3,19},{4,20},{5,21},{6,22},{7,23},{8,24},{9,... | collective-permute-start | bytes 2359304 | tf_op jit(solution)/shard_map/ppermute | solution.py:36
  88.6 19.6 %collective-permute-start.31 = (bf16[3,128,1024]{2,1,0:T(8,128)(2,1)S(1)}, bf16[3,128,1024]{2,1,0:T(8,128)(2,1)S(1)}, u32[]{:S(2)}, u32[]{:S(2)}) collective-permute-start(bf16[3,128,1024]{2,1,0:T(8,128)(2,1)S(1)} %get-tuple-element.182), channel_id=1, source_target_pairs={{0,32},{1,97},{2,34},{3,99},{4,36},{5,101},{6,38},{7,103},{8,40},{... | collective-permute-start | bytes 2359304 | tf_op jit(solution)/shard_map/ppermute | solution.py:36
  95.9 9.3 %collective-permute-start.26 = (bf16[2,128,1024]{2,1,0:T(8,128)(2,1)S(1)}, bf16[2,128,1024]{2,1,0:T(8,128)(2,1)S(1)}, u32[]{:S(2)}, u32[]{:S(2)}) collective-permute-start(bf16[2,128,1024]{2,1,0:T(8,128)(2,1)S(1)} %pass_on.1), channel_id=1, source_target_pairs={{0,12},{1,5},{2,14},{3,7},{4,0},{5,9},{6,2},{7,11},{8,4},{9,13},{1... | collective-permute-start | bytes 1572872 | tf_op jit(solution)/shard_map/ppermute | solution.py:36
  97.6 12.8 %collective-permute-start.30 = (bf16[3,128,1024]{2,1,0:T(8,128)(2,1)S(1)}, bf16[3,128,1024]{2,1,0:T(8,128)(2,1)S(1)}, u32[]{:S(2)}, u32[]{:S(2)}) collective-permute-start(bf16[3,128,1024]{2,1,0:T(8,128)(2,1)S(1)} %add_convert_fusion), channel_id=1, source_target_pairs={{0,96},{1,33},{2,98},{3,35},{4,100},{5,37},{6,102},{7,39},{8,104},... | collective-permute-start | bytes 2359304 | tf_op jit(solution)/shard_map/ppermute | solution.py:36
  105.4 8.0 %collective-permute-start.27 = (bf16[128,1024]{1,0:T(8,128)(2,1)S(1)}, bf16[128,1024]{1,0:T(8,128)(2,1)S(1)}, u32[]{:S(2)}, u32[]{:S(2)}) collective-permute-start(bf16[128,1024]{1,0:T(8,128)(2,1)S(1)} %get-tuple-element.174), channel_id=1, source_target_pairs={{0,2},{1,3},{2,0},{3,1},{4,6},{5,7},{6,4},{7,5},{8,10},{9,11},{10,... | collective-permute-start | bytes 786440 | tf_op jit(solution)/shard_map/ppermute | solution.py:36
  (2 other events, 21.9 us)

commit v6 on v5

--- a/solution.py
+++ b/solution.py
@@ -351,7 +351,7 @@
     masked = (pair, z1, z2, across, pair_o, z1_o, z2_o, across_o)
     p2x, pmx, ppx, p0x = backward(states, masked, True, ("far", "back", "ahead", "here"))
 
-    b1, b3, p2x, pmx, ppx, p0x, pair = fence(b1, b3, p2x, pmx, ppx, p0x, pair)
+    b1, p2x, pmx, ppx, p0x, pair = fence(b1, p2x, pmx, ppx, p0x, pair)
     masked = (pair, *masked[1:])
     e2 = send(pmx, Y2)
     e3 = send(ppx, Y1)

time: 114 us -> 116 us (1.018)
  transfers between devices with their start and end apart: 32 -> 32, of which waited for: 14 -> 12; matrix products, arithmetic and copies ran while one was open for 1% -> 1% of each run, Pallas kernels for 32% -> 32%
where the time goes in v6:
time: 116 us; the launch traced here: 115 us
  starting transfers between devices  41.5 us (36%)
  Pallas kernels  39.6 us (34%)
  waiting for transfers between devices  32.1 us (28%)
    ppermute x32, starting transfers between devices, send(): return lax.ppermute(array, FULL, pairs)  41.5 us
    ppermute x32, waiting for transfers between devices, send(): return lax.ppermute(array, FULL, pairs)  32.1 us
    pallas_call x2, Pallas kernels, backward(): pl.pallas_call(kernel, in_specs=[VMEM] * 11, out_specs=[VMEM] * count, ou...  15 us
    pallas_call x4, Pallas kernels, forward(): pl.pallas_call(forward_kernel, in_specs=[VMEM] * 5, out_specs=[VMEM] * 2,...  14.7 us
    pallas_call x1, Pallas kernels, load(): pl.pallas_call(load_kernel, in_specs=[pl.BlockSpec(memory_space=pl.ANY)]...  4.68 us
  transfers between devices with their start and end apart: 32, of which 12 were waited for; matrix products, arithmetic and copies ran while one was open for 1% of the time, Pallas kernels for 32%

profile of v6, /device:TPU:0, one launch (start us, length us, event | category | flops | bytes accessed | tf_op | source)
XLA Modules:
  0.0 115.2 jit_solution(1438084266212247805)
XLA Ops:
  0.6 2.2 %prepare.1 = (bf16[3072,128]{1,0:T(8,128)(2,1)}, bf16[1024,128]{1,0:T(8,128)(2,1)}) custom-call(bf16[1024,128]{1,0:T(8,128)(2,1)} %w0.1, bf16[1024,128]{1,0:T(8,128)(2,1)} %w1.1, bf16[1024,128]{1,0:T(8,128)(2,1)} %w2.1, bf16[128,1024]{1,0:T(8,128)(2,1)} %grad_ref.1, s32[1,128]{1,0:T(1,128)} %bitcast.5), custom_call_target="tpu_custom_call" | custom-call | flops 131 | bytes 2097 | tf_op jit(solution)/shard_map/prepare/pallas_call | solution.py:88
  2.8 1.7 %collective-permute-start.1 = (bf16[3072,128]{1,0:T(8,128)(2,1)}, bf16[3072,128]{1,0:T(8,128)(2,1)S(1)}, u32[]{:S(2)}, u32[]{:S(2)}) collective-permute-start(bf16[3072,128]{1,0:T(8,128)(2,1)} %get-tuple-element.110.wa), channel_id=1, source_target_pairs={{0,32},{1,97},{2,34},{3,99},{4,36},{5,101},{6,38},{7,103},{8,40},{... | collective-permute-start | bytes 2359304 | tf_op jit(solution)/shard_map/ppermute | solution.py:36
  4.6 1.6 %collective-permute-start.2 = (bf16[3072,128]{1,0:T(8,128)(2,1)}, bf16[3072,128]{1,0:T(8,128)(2,1)S(1)}, u32[]{:S(2)}, u32[]{:S(2)}) collective-permute-start(bf16[3072,128]{1,0:T(8,128)(2,1)} %get-tuple-element.110.wa), channel_id=1, source_target_pairs={{0,96},{1,33},{2,98},{3,35},{4,100},{5,37},{6,102},{7,39},{8,104},... | collective-permute-start | bytes 2359304 | tf_op jit(solution)/shard_map/ppermute | solution.py:36
  6.2 3.1 %collective-permute-start = (bf16[1024,128]{1,0:T(8,128)(2,1)}, bf16[1024,128]{1,0:T(8,128)(2,1)S(1)}, u32[]{:S(2)}, u32[]{:S(2)}) collective-permute-start(bf16[1024,128]{1,0:T(8,128)(2,1)} %get-tuple-element.108), channel_id=1, source_target_pairs={{0,2},{1,3},{2,0},{3,1},{4,6},{5,7},{6,4},{7,5},{8,10},{9,11},{10,... | collective-permute-start | bytes 786440 | tf_op jit(solution)/shard_map/ppermute | solution.py:36
  9.9 4.7 %load.1 = (bf16[2048,1024]{1,0:T(8,128)(2,1)S(1)}, bf16[2048,1024]{1,0:T(8,128)(2,1)S(1)}, bf16[2048,1024]{1,0:T(8,128)(2,1)S(1)}) custom-call(bf16[2048,1024]{1,0:T(8,128)(2,1)} %refs_0_, bf16[2048,1024]{1,0:T(8,128)(2,1)} %refs_1_, bf16[2048,1024]{1,0:T(8,128)(2,1)} %refs_2_), custom_call_target="tpu_custom_call" | custom-call | bytes 25165 | tf_op jit(solution)/shard_map/load/pallas_call | solution.py:116
  14.6 2.6 %collective-permute-done = bf16[1024,128]{1,0:T(8,128)(2,1)S(1)} collective-permute-done((bf16[1024,128]{1,0:T(8,128)(2,1)}, bf16[1024,128]{1,0:T(8,128)(2,1)S(1)}, u32[]{:S(2)}, u32[]{:S(2)}) %collective-permute-start) | collective-permute-done | bytes 262176 | tf_op jit(solution)/shard_map/ppermute | solution.py:36
  17.2 2.1 %collective-permute-start.4 = (bf16[2,1024,128]{2,1,0:T(8,128)(2,1)S(1)}, bf16[2,1024,128]{2,1,0:T(8,128)(2,1)S(1)}, u32[]{:S(2)}, u32[]{:S(2)}) collective-permute-start(bf16[2,1024,128]{2,1,0:T(8,128)(2,1)S(1)} %pad_maximum_fusion.refs_0_), channel_id=1, source_target_pairs={{0,4},{1,13},{2,6},{3,15},{4,8},{5,1},{6,10},{7,3},{8,12},{9,5},{1... | collective-permute-start | bytes 1572872 | tf_op jit(solution)/shard_map/ppermute | solution.py:36
  19.2 2.2 %collective-permute-start.5 = (bf16[2,1024,128]{2,1,0:T(8,128)(2,1)S(1)}, bf16[2,1024,128]{2,1,0:T(8,128)(2,1)S(1)}, u32[]{:S(2)}, u32[]{:S(2)}) collective-permute-start(bf16[2,1024,128]{2,1,0:T(8,128)(2,1)S(1)} %pad_maximum_fusion.refs_0_), channel_id=1, source_target_pairs={{0,12},{1,5},{2,14},{3,7},{4,0},{5,9},{6,2},{7,11},{8,4},{9,13},{1... | collective-permute-start | bytes 1572872 | tf_op jit(solution)/shard_map/ppermute | solution.py:36
  21.4 1.6 %collective-permute-done.1.wb = bf16[3072,128]{1,0:T(8,128)(2,1)S(1)} collective-permute-done((bf16[3072,128]{1,0:T(8,128)(2,1)}, bf16[3072,128]{1,0:T(8,128)(2,1)S(1)}, u32[]{:S(2)}, u32[]{:S(2)}) %collective-permute-start.1) | collective-permute-done | bytes 786464 | tf_op jit(solution)/shard_map/ppermute | solution.py:36
  23.1 1.7 %collective-permute-start.6 = (bf16[2,1024,128]{2,1,0:T(8,128)(2,1)S(1)}, bf16[2,1024,128]{2,1,0:T(8,128)(2,1)S(1)}, u32[]{:S(2)}, u32[]{:S(2)}) collective-permute-start(bf16[2,1024,128]{2,1,0:T(8,128)(2,1)S(1)} %pad_maximum_fusion.refs_0_), channel_id=1, source_target_pairs={{0,1},{1,0},{2,3},{3,2},{4,5},{5,4},{6,7},{7,6},{8,9},{9,8},{10,11... | collective-permute-start | bytes 1572872 | tf_op jit(solution)/shard_map/ppermute | solution.py:36
  25.3 3.7 %forward.4 = (bf16[4,2,128,256]{3,2,1,0:T(8,128)(2,1)S(1)}, bf16[4,2,128,256]{3,2,1,0:T(8,128)(2,1)S(1)}) custom-call(bf16[2048,1024]{1,0:T(8,128)(2,1)S(1)} %get-tuple-element.115.s0.refs_8_, bf16[2048,1024]{1,0:T(8,128)(2,1)S(1)} %get-tuple-element.116.s1.refs_9_, bf16[2048,1024]{1,0:T(8,128)(2,1)S(1)} %get-tuple-element.117.s2.refs_10_, ...), custom_call_target="tpu_custom_call" | custom-call | flops 3221225 | bytes 14680 | tf_op jit(solution)/shard_map/forward/pallas_call | solution.py:150
  29.0 3.8 %collective-permute-done.4.refs_1_ = bf16[2,1024,128]{2,1,0:T(8,128)(2,1)S(1)} collective-permute-done((bf16[2,1024,128]{2,1,0:T(8,128)(2,1)S(1)}, bf16[2,1024,128]{2,1,0:T(8,128)(2,1)S(1)}, u32[]{:S(2)}, u32[]{:S(2)}) %collective-permute-start.4) | collective-permute-done | bytes 524320 | tf_op jit(solution)/shard_map/ppermute | solution.py:36
  35.2 2.9 %collective-permute-done.7.wb = bf16[3072,128]{1,0:T(8,128)(2,1)S(1)} collective-permute-done((bf16[3072,128]{1,0:T(8,128)(2,1)S(1)}, bf16[3072,128]{1,0:T(8,128)(2,1)S(1)}, u32[]{:S(2)}, u32[]{:S(2)}) %collective-permute-start.7) | collective-permute-done | bytes 786464 | tf_op jit(solution)/shard_map/ppermute | solution.py:36
  38.1 3.7 %forward.5 = (bf16[4,2,128,256]{3,2,1,0:T(8,128)(2,1)S(1)}, bf16[4,2,128,256]{3,2,1,0:T(8,128)(2,1)S(1)}) custom-call(bf16[2048,1024]{1,0:T(8,128)(2,1)S(1)} %get-tuple-element.115.s0.refs_8_, bf16[2048,1024]{1,0:T(8,128)(2,1)S(1)} %get-tuple-element.116.s1.refs_9_, bf16[2048,1024]{1,0:T(8,128)(2,1)S(1)} %get-tuple-element.117.s2.refs_10_, ...), custom_call_target="tpu_custom_call" | custom-call | flops 3221225 | bytes 14680 | tf_op jit(solution)/shard_map/forward/pallas_call | solution.py:150
  41.8 1.9 %collective-permute-done.9.refs_3_ = bf16[2,1024,128]{2,1,0:T(8,128)(2,1)S(1)} collective-permute-done((bf16[2,1024,128]{2,1,0:T(8,128)(2,1)S(1)}, bf16[2,1024,128]{2,1,0:T(8,128)(2,1)S(1)}, u32[]{:S(2)}, u32[]{:S(2)}) %collective-permute-start.9) | collective-permute-done | bytes 524320 | tf_op jit(solution)/shard_map/ppermute | solution.py:36
  45.7 3.0 %collective-permute-start.16 = (bf16[3072,128]{1,0:T(8,128)(2,1)S(1)}, bf16[3072,128]{1,0:T(8,128)(2,1)S(1)}, u32[]{:S(2)}, u32[]{:S(2)}) collective-permute-start(bf16[3072,128]{1,0:T(8,128)(2,1)S(1)} %collective-permute-done.3.wa), channel_id=1, source_target_pairs={{0,96},{1,33},{2,98},{3,35},{4,100},{5,37},{6,102},{7,39},{8,104},... | collective-permute-start | bytes 2359304 | tf_op jit(solution)/shard_map/ppermute | solution.py:36
  48.6 7.5 %backward.2 = (bf16[3,128,1024]{2,1,0:T(8,128)(2,1)S(1)}, bf16[3,128,1024]{2,1,0:T(8,128)(2,1)S(1)}, bf16[3,128,1024]{2,1,0:T(8,128)(2,1)S(1)}, bf16[3,128,1024]{2,1,0:T(8,128)(2,1)S(1)}) custom-call(bf16[2,1024,128]{2,1,0:T(8,128)(2,1)S(1)} %pad_maximum_fusion.refs_0_, bf16[2,1024,128]{2,1,0:T(8,128)(2,1)S(1)} %collective-permute-done.4.refs_1_, ...), custom_call_target="tpu_custom_call" | custom-call | flops 6442450 | bytes 20971 | tf_op jit(solution)/shard_map/backward/pallas_call | solution.py:201
  57.6 2.0 %collective-permute-start.19 = (bf16[3,128,1024]{2,1,0:T(8,128)(2,1)S(1)}, bf16[3,128,1024]{2,1,0:T(8,128)(2,1)S(1)}, u32[]{:S(2)}, u32[]{:S(2)}) collective-permute-start(bf16[3,128,1024]{2,1,0:T(8,128)(2,1)S(1)} %get-tuple-element.149), channel_id=1, source_target_pairs={{0,32},{1,97},{2,34},{3,99},{4,36},{5,101},{6,38},{7,103},{8,40},{... | collective-permute-start | bytes 2359304 | tf_op jit(solution)/shard_map/ppermute | solution.py:36
  59.6 7.5 %backward.3 = (bf16[3,128,1024]{2,1,0:T(8,128)(2,1)S(1)}, bf16[3,128,1024]{2,1,0:T(8,128)(2,1)S(1)}, bf16[3,128,1024]{2,1,0:T(8,128)(2,1)S(1)}, bf16[3,128,1024]{2,1,0:T(8,128)(2,1)S(1)}) custom-call(bf16[2,1024,128]{2,1,0:T(8,128)(2,1)S(1)} %pad_maximum_fusion.refs_0_, bf16[2,1024,128]{2,1,0:T(8,128)(2,1)S(1)} %collective-permute-done.4.refs_1_, ...), custom_call_target="tpu_custom_call" | custom-call | flops 6442450 | bytes 20971 | tf_op jit(solution)/shard_map/backward/pallas_call | solution.py:201
  67.4 2.1 %collective-permute-start.20 = (bf16[2,128,384]{2,1,0:T(8,128)(2,1)S(1)}, bf16[2,128,384]{2,1,0:T(8,128)(2,1)S(1)}, u32[]{:S(2)}, u32[]{:S(2)}) collective-permute-start(bf16[2,128,384]{2,1,0:T(8,128)(2,1)S(1)} %get-tuple-element.150), channel_id=1, source_target_pairs={{0,12},{1,5},{2,14},{3,7},{4,0},{5,9},{6,2},{7,11},{8,4},{9,13},{1... | collective-permute-start | bytes 589832 | tf_op jit(solution)/shard_map/ppermute | solution.py:36
  69.5 3.7 %forward.6 = (bf16[4,2,128,256]{3,2,1,0:T(8,128)(2,1)S(1)}, bf16[4,2,128,256]{3,2,1,0:T(8,128)(2,1)S(1)}) custom-call(bf16[2048,1024]{1,0:T(8,128)(2,1)S(1)} %get-tuple-element.115.s0.refs_8_, bf16[2048,1024]{1,0:T(8,128)(2,1)S(1)} %get-tuple-element.116.s1.refs_9_, bf16[2048,1024]{1,0:T(8,128)(2,1)S(1)} %get-tuple-element.117.s2.refs_10_, ...), custom_call_target="tpu_custom_call" | custom-call | flops 3221225 | bytes 14680 | tf_op jit(solution)/shard_map/forward/pallas_call | solution.py:150
  73.1 3.7 %forward.7 = (bf16[4,2,128,256]{3,2,1,0:T(8,128)(2,1)S(1)}, bf16[4,2,128,256]{3,2,1,0:T(8,128)(2,1)S(1)}) custom-call(bf16[2048,1024]{1,0:T(8,128)(2,1)S(1)} %get-tuple-element.115.s0.refs_8_, bf16[2048,1024]{1,0:T(8,128)(2,1)S(1)} %get-tuple-element.116.s1.refs_9_, bf16[2048,1024]{1,0:T(8,128)(2,1)S(1)} %get-tuple-element.117.s2.refs_10_, ...), custom_call_target="tpu_custom_call" | custom-call | flops 3221225 | bytes 14680 | tf_op jit(solution)/shard_map/forward/pallas_call | solution.py:150
  76.9 4.1 %collective-permute-done.17 = bf16[3,128,1024]{2,1,0:T(8,128)(2,1)S(1)} collective-permute-done((bf16[3,128,1024]{2,1,0:T(8,128)(2,1)S(1)}, bf16[3,128,1024]{2,1,0:T(8,128)(2,1)S(1)}, u32[]{:S(2)}, u32[]{:S(2)}) %collective-permute-start.17) | collective-permute-done | bytes 786464 | tf_op jit(solution)/shard_map/ppermute | solution.py:36
  81.8 3.0 %collective-permute-start.29 = (bf16[3,128,1024]{2,1,0:T(8,128)(2,1)S(1)}, bf16[3,128,1024]{2,1,0:T(8,128)(2,1)S(1)}, u32[]{:S(2)}, u32[]{:S(2)}) collective-permute-start(bf16[3,128,1024]{2,1,0:T(8,128)(2,1)S(1)} %add_convert_fusion.1), channel_id=1, source_target_pairs={{0,96},{1,33},{2,98},{3,35},{4,100},{5,37},{6,102},{7,39},{8,104},... | collective-permute-start | bytes 2359304 | tf_op jit(solution)/shard_map/ppermute | solution.py:36
  85.2 2.1 %collective-permute-start.24 = (bf16[2,128,640]{2,1,0:T(8,128)(2,1)S(1)}, bf16[2,128,640]{2,1,0:T(8,128)(2,1)S(1)}, u32[]{:S(2)}, u32[]{:S(2)}) collective-permute-start(bf16[2,128,640]{2,1,0:T(8,128)(2,1)S(1)} %get-tuple-element.161), channel_id=1, source_target_pairs={{0,12},{1,5},{2,14},{3,7},{4,0},{5,9},{6,2},{7,11},{8,4},{9,13},{1... | collective-permute-start | bytes 983048 | tf_op jit(solution)/shard_map/ppermute | solution.py:36
  89.3 5.0 %collective-permute-done.24.tb = bf16[2,128,640]{2,1,0:T(8,128)(2,1)S(1)} collective-permute-done((bf16[2,128,640]{2,1,0:T(8,128)(2,1)S(1)}, bf16[2,128,640]{2,1,0:T(8,128)(2,1)S(1)}, u32[]{:S(2)}, u32[]{:S(2)}) %collective-permute-start.24) | collective-permute-done | bytes 327712 | tf_op jit(solution)/shard_map/ppermute | solution.py:36
  95.7 2.5 %collective-permute-start.26 = (bf16[2,128,1024]{2,1,0:T(8,128)(2,1)S(1)}, bf16[2,128,1024]{2,1,0:T(8,128)(2,1)S(1)}, u32[]{:S(2)}, u32[]{:S(2)}) collective-permute-start(bf16[2,128,1024]{2,1,0:T(8,128)(2,1)S(1)} %pass_on.1), channel_id=1, source_target_pairs={{0,12},{1,5},{2,14},{3,7},{4,0},{5,9},{6,2},{7,11},{8,4},{9,13},{1... | collective-permute-start | bytes 1572872 | tf_op jit(solution)/shard_map/ppermute | solution.py:36
  98.5 2.8 %collective-permute-start.30 = (bf16[3,128,1024]{2,1,0:T(8,128)(2,1)S(1)}, bf16[3,128,1024]{2,1,0:T(8,128)(2,1)S(1)}, u32[]{:S(2)}, u32[]{:S(2)}) collective-permute-start(bf16[3,128,1024]{2,1,0:T(8,128)(2,1)S(1)} %add_convert_fusion), channel_id=1, source_target_pairs={{0,96},{1,33},{2,98},{3,35},{4,100},{5,37},{6,102},{7,39},{8,104},... | collective-permute-start | bytes 2359304 | tf_op jit(solution)/shard_map/ppermute | solution.py:36
  101.3 3.6 %collective-permute-done.26.b = bf16[2,128,1024]{2,1,0:T(8,128)(2,1)S(1)} collective-permute-done((bf16[2,128,1024]{2,1,0:T(8,128)(2,1)S(1)}, bf16[2,128,1024]{2,1,0:T(8,128)(2,1)S(1)}, u32[]{:S(2)}, u32[]{:S(2)}) %collective-permute-start.26) | collective-permute-done | bytes 524320 | tf_op jit(solution)/shard_map/ppermute | solution.py:36
  105.2 2.7 %collective-permute-start.27 = (bf16[128,1024]{1,0:T(8,128)(2,1)S(1)}, bf16[128,1024]{1,0:T(8,128)(2,1)S(1)}, u32[]{:S(2)}, u32[]{:S(2)}) collective-permute-start(bf16[128,1024]{1,0:T(8,128)(2,1)S(1)} %get-tuple-element.172), channel_id=1, source_target_pairs={{0,2},{1,3},{2,0},{3,1},{4,6},{5,7},{6,4},{7,5},{8,10},{9,11},{10,... | collective-permute-start | bytes 786440 | tf_op jit(solution)/shard_map/ppermute | solution.py:36
  107.9 3.3 %collective-permute-done.30.c = bf16[3,128,1024]{2,1,0:T(8,128)(2,1)S(1)} collective-permute-done((bf16[3,128,1024]{2,1,0:T(8,128)(2,1)S(1)}, bf16[3,128,1024]{2,1,0:T(8,128)(2,1)S(1)}, u32[]{:S(2)}, u32[]{:S(2)}) %collective-permute-start.30) | collective-permute-done | bytes 786464 | tf_op jit(solution)/shard_map/ppermute | solution.py:36
  112.5 1.8 %collective-permute-done.27.b = bf16[128,1024]{1,0:T(8,128)(2,1)S(1)} collective-permute-done((bf16[128,1024]{1,0:T(8,128)(2,1)S(1)}, bf16[128,1024]{1,0:T(8,128)(2,1)S(1)}, u32[]{:S(2)}, u32[]{:S(2)}) %collective-permute-start.27) | collective-permute-done | bytes 262176 | tf_op jit(solution)/shard_map/ppermute | solution.py:36
  (54 shorter events, 14.4 us)
Async XLA Ops:
  2.8 20.2 %collective-permute-start.1 = (bf16[3072,128]{1,0:T(8,128)(2,1)}, bf16[3072,128]{1,0:T(8,128)(2,1)S(1)}, u32[]{:S(2)}, u32[]{:S(2)}) collective-permute-start(bf16[3072,128]{1,0:T(8,128)(2,1)} %get-tuple-element.110.wa), channel_id=1, source_target_pairs={{0,32},{1,97},{2,34},{3,99},{4,36},{5,101},{6,38},{7,103},{8,40},{... | collective-permute-start | bytes 2359304 | tf_op jit(solution)/shard_map/ppermute | solution.py:36
  4.6 18.6 %collective-permute-start.2 = (bf16[3072,128]{1,0:T(8,128)(2,1)}, bf16[3072,128]{1,0:T(8,128)(2,1)S(1)}, u32[]{:S(2)}, u32[]{:S(2)}) collective-permute-start(bf16[3072,128]{1,0:T(8,128)(2,1)} %get-tuple-element.110.wa), channel_id=1, source_target_pairs={{0,96},{1,33},{2,98},{3,35},{4,100},{5,37},{6,102},{7,39},{8,104},... | collective-permute-start | bytes 2359304 | tf_op jit(solution)/shard_map/ppermute | solution.py:36
  6.2 11.0 %collective-permute-start = (bf16[1024,128]{1,0:T(8,128)(2,1)}, bf16[1024,128]{1,0:T(8,128)(2,1)S(1)}, u32[]{:S(2)}, u32[]{:S(2)}) collective-permute-start(bf16[1024,128]{1,0:T(8,128)(2,1)} %get-tuple-element.108), channel_id=1, source_target_pairs={{0,2},{1,3},{2,0},{3,1},{4,6},{5,7},{6,4},{7,5},{8,10},{9,11},{10,... | collective-permute-start | bytes 786440 | tf_op jit(solution)/shard_map/ppermute | solution.py:36
  9.3 23.6 %collective-permute-start.3 = (bf16[3072,128]{1,0:T(8,128)(2,1)}, bf16[3072,128]{1,0:T(8,128)(2,1)S(1)}, u32[]{:S(2)}, u32[]{:S(2)}) collective-permute-start(bf16[3072,128]{1,0:T(8,128)(2,1)} %get-tuple-element.110.wa), channel_id=1, source_target_pairs={{0,16},{1,17},{2,18},{3,19},{4,20},{5,21},{6,22},{7,23},{8,24},{9,... | collective-permute-start | bytes 2359304 | tf_op jit(solution)/shard_map/ppermute | solution.py:36
  17.2 15.7 %collective-permute-start.4 = (bf16[2,1024,128]{2,1,0:T(8,128)(2,1)S(1)}, bf16[2,1024,128]{2,1,0:T(8,128)(2,1)S(1)}, u32[]{:S(2)}, u32[]{:S(2)}) collective-permute-start(bf16[2,1024,128]{2,1,0:T(8,128)(2,1)S(1)} %pad_maximum_fusion.refs_0_), channel_id=1, source_target_pairs={{0,4},{1,13},{2,6},{3,15},{4,8},{5,1},{6,10},{7,3},{8,12},{9,5},{1... | collective-permute-start | bytes 1572872 | tf_op jit(solution)/shard_map/ppermute | solution.py:36
  19.2 13.6 %collective-permute-start.5 = (bf16[2,1024,128]{2,1,0:T(8,128)(2,1)S(1)}, bf16[2,1024,128]{2,1,0:T(8,128)(2,1)S(1)}, u32[]{:S(2)}, u32[]{:S(2)}) collective-permute-start(bf16[2,1024,128]{2,1,0:T(8,128)(2,1)S(1)} %pad_maximum_fusion.refs_0_), channel_id=1, source_target_pairs={{0,12},{1,5},{2,14},{3,7},{4,0},{5,9},{6,2},{7,11},{8,4},{9,13},{1... | collective-permute-start | bytes 1572872 | tf_op jit(solution)/shard_map/ppermute | solution.py:36
  23.1 9.7 %collective-permute-start.6 = (bf16[2,1024,128]{2,1,0:T(8,128)(2,1)S(1)}, bf16[2,1024,128]{2,1,0:T(8,128)(2,1)S(1)}, u32[]{:S(2)}, u32[]{:S(2)}) collective-permute-start(bf16[2,1024,128]{2,1,0:T(8,128)(2,1)S(1)} %pad_maximum_fusion.refs_0_), channel_id=1, source_target_pairs={{0,1},{1,0},{2,3},{3,2},{4,5},{5,4},{6,7},{7,6},{8,9},{9,8},{10,11... | collective-permute-start | bytes 1572872 | tf_op jit(solution)/shard_map/ppermute | solution.py:36
  24.9 13.2 %collective-permute-start.7 = (bf16[3072,128]{1,0:T(8,128)(2,1)S(1)}, bf16[3072,128]{1,0:T(8,128)(2,1)S(1)}, u32[]{:S(2)}, u32[]{:S(2)}) collective-permute-start(bf16[3072,128]{1,0:T(8,128)(2,1)S(1)} %collective-permute-done.1.wb), channel_id=1, source_target_pairs={{0,32},{1,97},{2,34},{3,99},{4,36},{5,101},{6,38},{7,103},{8,40},{... | collective-permute-start | bytes 2359304 | tf_op jit(solution)/shard_map/ppermute | solution.py:36
  32.8 10.8 %collective-permute-start.9 = (bf16[2,1024,128]{2,1,0:T(8,128)(2,1)S(1)}, bf16[2,1024,128]{2,1,0:T(8,128)(2,1)S(1)}, u32[]{:S(2)}, u32[]{:S(2)}) collective-permute-start(bf16[2,1024,128]{2,1,0:T(8,128)(2,1)S(1)} %collective-permute-done.4.refs_1_), channel_id=1, source_target_pairs={{0,4},{1,13},{2,6},{3,15},{4,8},{5,1},{6,10},{7,3},{8,12},{9,5},{1... | collective-permute-start | bytes 1572872 | tf_op jit(solution)/shard_map/ppermute | solution.py:36
  34.4 9.3 %collective-permute-start.10 = (bf16[2,1024,128]{2,1,0:T(8,128)(2,1)S(1)}, bf16[2,1024,128]{2,1,0:T(8,128)(2,1)S(1)}, u32[]{:S(2)}, u32[]{:S(2)}) collective-permute-start(bf16[2,1024,128]{2,1,0:T(8,128)(2,1)S(1)} %collective-permute-done.4.refs_1_), channel_id=1, source_target_pairs={{0,1},{1,0},{2,3},{3,2},{4,5},{5,4},{6,7},{7,6},{8,9},{9,8},{10,11... | collective-permute-start | bytes 1572872 | tf_op jit(solution)/shard_map/ppermute | solution.py:36
  34.6 9.0 %collective-permute-start.11 = (bf16[2,1024,128]{2,1,0:T(8,128)(2,1)S(1)}, bf16[2,1024,128]{2,1,0:T(8,128)(2,1)S(1)}, u32[]{:S(2)}, u32[]{:S(2)}) collective-permute-start(bf16[2,1024,128]{2,1,0:T(8,128)(2,1)S(1)} %collective-permute-done.5.refs_2_), channel_id=1, source_target_pairs={{0,1},{1,0},{2,3},{3,2},{4,5},{5,4},{6,7},{7,6},{8,9},{9,8},{10,11... | collective-permute-start | bytes 1572872 | tf_op jit(solution)/shard_map/ppermute | solution.py:36
  34.9 21.3 %collective-permute-start.13 = (bf16[3072,128]{1,0:T(8,128)(2,1)S(1)}, bf16[3072,128]{1,0:T(8,128)(2,1)S(1)}, u32[]{:S(2)}, u32[]{:S(2)}) collective-permute-start(bf16[3072,128]{1,0:T(8,128)(2,1)S(1)} %collective-permute-done.3.wa), channel_id=1, source_target_pairs={{0,32},{1,97},{2,34},{3,99},{4,36},{5,101},{6,38},{7,103},{8,40},{... | collective-permute-start | bytes 2359304 | tf_op jit(solution)/shard_map/ppermute | solution.py:36
  43.6 2.0 %collective-permute-start.14 = (bf16[2,1024,128]{2,1,0:T(8,128)(2,1)S(1)}, bf16[2,1024,128]{2,1,0:T(8,128)(2,1)S(1)}, u32[]{:S(2)}, u32[]{:S(2)}) collective-permute-start(bf16[2,1024,128]{2,1,0:T(8,128)(2,1)S(1)} %collective-permute-done.9.refs_3_), channel_id=1, source_target_pairs={{0,1},{1,0},{2,3},{3,2},{4,5},{5,4},{6,7},{7,6},{8,9},{9,8},{10,11... | collective-permute-start | bytes 1572872 | tf_op jit(solution)/shard_map/ppermute | solution.py:36
  43.7 13.9 %collective-permute-start.8 = (bf16[4,2,128,256]{3,2,1,0:T(8,128)(2,1)S(1)}, bf16[4,2,128,256]{3,2,1,0:T(8,128)(2,1)S(1)}, u32[]{:S(2)}, u32[]{:S(2)}) collective-permute-start(bf16[4,2,128,256]{3,2,1,0:T(8,128)(2,1)S(1)} %get-tuple-element.120), channel_id=1, source_target_pairs={{0,1},{1,0},{2,3},{3,2},{4,5},{5,4},{6,7},{7,6},{8,9},{9,8},{10,11... | collective-permute-start | bytes 1572872 | tf_op jit(solution)/shard_map/ppermute | solution.py:36
  44.2 13.4 %collective-permute-start.12 = (bf16[4,2,128,256]{3,2,1,0:T(8,128)(2,1)S(1)}, bf16[4,2,128,256]{3,2,1,0:T(8,128)(2,1)S(1)}, u32[]{:S(2)}, u32[]{:S(2)}) collective-permute-start(bf16[4,2,128,256]{3,2,1,0:T(8,128)(2,1)S(1)} %get-tuple-element.124), channel_id=1, source_target_pairs={{0,1},{1,0},{2,3},{3,2},{4,5},{5,4},{6,7},{7,6},{8,9},{9,8},{10,11... | collective-permute-start | bytes 1572872 | tf_op jit(solution)/shard_map/ppermute | solution.py:36
  44.2 23.1 %collective-permute-start.15 = (bf16[3072,128]{1,0:T(8,128)(2,1)S(1)}, bf16[3072,128]{1,0:T(8,128)(2,1)S(1)}, u32[]{:S(2)}, u32[]{:S(2)}) collective-permute-start(bf16[3072,128]{1,0:T(8,128)(2,1)S(1)} %collective-permute-done.7.wb), channel_id=1, source_target_pairs={{0,16},{1,17},{2,18},{3,19},{4,20},{5,21},{6,22},{7,23},{8,24},{9,... | collective-permute-start | bytes 2359304 | tf_op jit(solution)/shard_map/ppermute | solution.py:36
  45.7 23.8 %collective-permute-start.16 = (bf16[3072,128]{1,0:T(8,128)(2,1)S(1)}, bf16[3072,128]{1,0:T(8,128)(2,1)S(1)}, u32[]{:S(2)}, u32[]{:S(2)}) collective-permute-start(bf16[3072,128]{1,0:T(8,128)(2,1)S(1)} %collective-permute-done.3.wa), channel_id=1, source_target_pairs={{0,96},{1,33},{2,98},{3,35},{4,100},{5,37},{6,102},{7,39},{8,104},... | collective-permute-start | bytes 2359304 | tf_op jit(solution)/shard_map/ppermute | solution.py:36
  56.2 24.8 %collective-permute-start.17 = (bf16[3,128,1024]{2,1,0:T(8,128)(2,1)S(1)}, bf16[3,128,1024]{2,1,0:T(8,128)(2,1)S(1)}, u32[]{:S(2)}, u32[]{:S(2)}) collective-permute-start(bf16[3,128,1024]{2,1,0:T(8,128)(2,1)S(1)} %get-tuple-element.147), channel_id=1, source_target_pairs={{0,16},{1,17},{2,18},{3,19},{4,20},{5,21},{6,22},{7,23},{8,24},{9,... | collective-permute-start | bytes 2359304 | tf_op jit(solution)/shard_map/ppermute | solution.py:36
  57.6 23.4 %collective-permute-start.18 = (bf16[3,128,1024]{2,1,0:T(8,128)(2,1)S(1)}, bf16[3,128,1024]{2,1,0:T(8,128)(2,1)S(1)}, u32[]{:S(2)}, u32[]{:S(2)}) collective-permute-start(bf16[3,128,1024]{2,1,0:T(8,128)(2,1)S(1)} %get-tuple-element.148), channel_id=1, source_target_pairs={{0,96},{1,33},{2,98},{3,35},{4,100},{5,37},{6,102},{7,39},{8,104},... | collective-permute-start | bytes 2359304 | tf_op jit(solution)/shard_map/ppermute | solution.py:36
  57.6 23.4 %collective-permute-start.19 = (bf16[3,128,1024]{2,1,0:T(8,128)(2,1)S(1)}, bf16[3,128,1024]{2,1,0:T(8,128)(2,1)S(1)}, u32[]{:S(2)}, u32[]{:S(2)}) collective-permute-start(bf16[3,128,1024]{2,1,0:T(8,128)(2,1)S(1)} %get-tuple-element.149), channel_id=1, source_target_pairs={{0,32},{1,97},{2,34},{3,99},{4,36},{5,101},{6,38},{7,103},{8,40},{... | collective-permute-start | bytes 2359304 | tf_op jit(solution)/shard_map/ppermute | solution.py:36
  67.4 9.5 %collective-permute-start.20 = (bf16[2,128,384]{2,1,0:T(8,128)(2,1)S(1)}, bf16[2,128,384]{2,1,0:T(8,128)(2,1)S(1)}, u32[]{:S(2)}, u32[]{:S(2)}) collective-permute-start(bf16[2,128,384]{2,1,0:T(8,128)(2,1)S(1)} %get-tuple-element.150), channel_id=1, source_target_pairs={{0,12},{1,5},{2,14},{3,7},{4,0},{5,9},{6,2},{7,11},{8,4},{9,13},{1... | collective-permute-start | bytes 589832 | tf_op jit(solution)/shard_map/ppermute | solution.py:36
  69.5 7.4 %collective-permute-start.21 = (bf16[2,128,384]{2,1,0:T(8,128)(2,1)S(1)}, bf16[2,128,384]{2,1,0:T(8,128)(2,1)S(1)}, u32[]{:S(2)}, u32[]{:S(2)}) collective-permute-start(bf16[2,128,384]{2,1,0:T(8,128)(2,1)S(1)} %get-tuple-element.151), channel_id=1, source_target_pairs={{0,4},{1,13},{2,6},{3,15},{4,8},{5,1},{6,10},{7,3},{8,12},{9,5},{1... | collective-permute-start | bytes 589832 | tf_op jit(solution)/shard_map/ppermute | solution.py:36
  81.0 3.9 %collective-permute-start.22 = (bf16[4,2,128,256]{3,2,1,0:T(8,128)(2,1)S(1)}, bf16[4,2,128,256]{3,2,1,0:T(8,128)(2,1)S(1)}, u32[]{:S(2)}, u32[]{:S(2)}) collective-permute-start(bf16[4,2,128,256]{3,2,1,0:T(8,128)(2,1)S(1)} %get-tuple-element.158), channel_id=1, source_target_pairs={{0,1},{1,0},{2,3},{3,2},{4,5},{5,4},{6,7},{7,6},{8,9},{9,8},{10,11... | collective-permute-start | bytes 1572872 | tf_op jit(solution)/shard_map/ppermute | solution.py:36
  81.0 3.9 %collective-permute-start.23 = (bf16[4,2,128,256]{3,2,1,0:T(8,128)(2,1)S(1)}, bf16[4,2,128,256]{3,2,1,0:T(8,128)(2,1)S(1)}, u32[]{:S(2)}, u32[]{:S(2)}) collective-permute-start(bf16[4,2,128,256]{3,2,1,0:T(8,128)(2,1)S(1)} %get-tuple-element.159), channel_id=1, source_target_pairs={{0,1},{1,0},{2,3},{3,2},{4,5},{5,4},{6,7},{7,6},{8,9},{9,8},{10,11... | collective-permute-start | bytes 1572872 | tf_op jit(solution)/shard_map/ppermute | solution.py:36
  81.8 16.4 %collective-permute-start.29 = (bf16[3,128,1024]{2,1,0:T(8,128)(2,1)S(1)}, bf16[3,128,1024]{2,1,0:T(8,128)(2,1)S(1)}, u32[]{:S(2)}, u32[]{:S(2)}) collective-permute-start(bf16[3,128,1024]{2,1,0:T(8,128)(2,1)S(1)} %add_convert_fusion.1), channel_id=1, source_target_pairs={{0,96},{1,33},{2,98},{3,35},{4,100},{5,37},{6,102},{7,39},{8,104},... | collective-permute-start | bytes 2359304 | tf_op jit(solution)/shard_map/ppermute | solution.py:36
  85.2 9.1 %collective-permute-start.24 = (bf16[2,128,640]{2,1,0:T(8,128)(2,1)S(1)}, bf16[2,128,640]{2,1,0:T(8,128)(2,1)S(1)}, u32[]{:S(2)}, u32[]{:S(2)}) collective-permute-start(bf16[2,128,640]{2,1,0:T(8,128)(2,1)S(1)} %get-tuple-element.161), channel_id=1, source_target_pairs={{0,12},{1,5},{2,14},{3,7},{4,0},{5,9},{6,2},{7,11},{8,4},{9,13},{1... | collective-permute-start | bytes 983048 | tf_op jit(solution)/shard_map/ppermute | solution.py:36
  87.3 8.3 %collective-permute-start.25 = (bf16[2,128,640]{2,1,0:T(8,128)(2,1)S(1)}, bf16[2,128,640]{2,1,0:T(8,128)(2,1)S(1)}, u32[]{:S(2)}, u32[]{:S(2)}) collective-permute-start(bf16[2,128,640]{2,1,0:T(8,128)(2,1)S(1)} %get-tuple-element.162), channel_id=1, source_target_pairs={{0,4},{1,13},{2,6},{3,15},{4,8},{5,1},{6,10},{7,3},{8,12},{9,5},{1... | collective-permute-start | bytes 983048 | tf_op jit(solution)/shard_map/ppermute | solution.py:36
  87.7 20.1 %collective-permute-start.28 = (bf16[3,128,1024]{2,1,0:T(8,128)(2,1)S(1)}, bf16[3,128,1024]{2,1,0:T(8,128)(2,1)S(1)}, u32[]{:S(2)}, u32[]{:S(2)}) collective-permute-start(bf16[3,128,1024]{2,1,0:T(8,128)(2,1)S(1)} %add_convert_fusion.2), channel_id=1, source_target_pairs={{0,16},{1,17},{2,18},{3,19},{4,20},{5,21},{6,22},{7,23},{8,24},{9,... | collective-permute-start | bytes 2359304 | tf_op jit(solution)/shard_map/ppermute | solution.py:36
  89.2 18.6 %collective-permute-start.31 = (bf16[3,128,1024]{2,1,0:T(8,128)(2,1)S(1)}, bf16[3,128,1024]{2,1,0:T(8,128)(2,1)S(1)}, u32[]{:S(2)}, u32[]{:S(2)}) collective-permute-start(bf16[3,128,1024]{2,1,0:T(8,128)(2,1)S(1)} %get-tuple-element.180), channel_id=1, source_target_pairs={{0,32},{1,97},{2,34},{3,99},{4,36},{5,101},{6,38},{7,103},{8,40},{... | collective-permute-start | bytes 2359304 | tf_op jit(solution)/shard_map/ppermute | solution.py:36
  95.7 9.3 %collective-permute-start.26 = (bf16[2,128,1024]{2,1,0:T(8,128)(2,1)S(1)}, bf16[2,128,1024]{2,1,0:T(8,128)(2,1)S(1)}, u32[]{:S(2)}, u32[]{:S(2)}) collective-permute-start(bf16[2,128,1024]{2,1,0:T(8,128)(2,1)S(1)} %pass_on.1), channel_id=1, source_target_pairs={{0,12},{1,5},{2,14},{3,7},{4,0},{5,9},{6,2},{7,11},{8,4},{9,13},{1... | collective-permute-start | bytes 1572872 | tf_op jit(solution)/shard_map/ppermute | solution.py:36
  98.5 12.7 %collective-permute-start.30 = (bf16[3,128,1024]{2,1,0:T(8,128)(2,1)S(1)}, bf16[3,128,1024]{2,1,0:T(8,128)(2,1)S(1)}, u32[]{:S(2)}, u32[]{:S(2)}) collective-permute-start(bf16[3,128,1024]{2,1,0:T(8,128)(2,1)S(1)} %add_convert_fusion), channel_id=1, source_target_pairs={{0,96},{1,33},{2,98},{3,35},{4,100},{5,37},{6,102},{7,39},{8,104},... | collective-permute-start | bytes 2359304 | tf_op jit(solution)/shard_map/ppermute | solution.py:36
  105.2 9.2 %collective-permute-start.27 = (bf16[128,1024]{1,0:T(8,128)(2,1)S(1)}, bf16[128,1024]{1,0:T(8,128)(2,1)S(1)}, u32[]{:S(2)}, u32[]{:S(2)}) collective-permute-start(bf16[128,1024]{1,0:T(8,128)(2,1)S(1)} %get-tuple-element.172), channel_id=1, source_target_pairs={{0,2},{1,3},{2,0},{3,1},{4,6},{5,7},{6,4},{7,5},{8,10},{9,11},{10,... | collective-permute-start | bytes 786440 | tf_op jit(solution)/shard_map/ppermute | solution.py:36
  (2 other events, 21.7 us)

commit v7 on v6

--- a/solution.py
+++ b/solution.py
@@ -351,10 +351,10 @@
     masked = (pair, z1, z2, across, pair_o, z1_o, z2_o, across_o)
     p2x, pmx, ppx, p0x = backward(states, masked, True, ("far", "back", "ahead", "here"))
 
-    b1, p2x, pmx, ppx, p0x, pair = fence(b1, p2x, pmx, ppx, p0x, pair)
-    masked = (pair, *masked[1:])
     e2 = send(pmx, Y2)
     e3 = send(ppx, Y1)
+    b1, b3, p2x, p0x, pair = fence(b1, b3, p2x, p0x, pair)
+    masked = (pair, *masked[1:])
     e1 = send(p2x, XL)
     got_a = send(theirs_a, CORE)
     got_b = send(theirs_b, CORE)

time: 116 us -> 114 us (0.983)
  transfers between devices with their start and end apart: 32 -> 32, of which waited for: 12 -> 14; matrix products, arithmetic and copies ran while one was open for 1% -> 1% of each run, Pallas kernels for 32% -> 32%
where the time goes in v7:
time: 114 us
  starting transfers between devices  41.4 us (36%)
  Pallas kernels  39.6 us (35%)
  waiting for transfers between devices  31.2 us (27%)
    ppermute x32, starting transfers between devices, send(): return lax.ppermute(array, FULL, pairs)  41.4 us
    ppermute x32, waiting for transfers between devices, send(): return lax.ppermute(array, FULL, pairs)  31.2 us
    pallas_call x2, Pallas kernels, backward(): pl.pallas_call(kernel, in_specs=[VMEM] * 11, out_specs=[VMEM] * count, ou...  15 us
    pallas_call x4, Pallas kernels, forward(): pl.pallas_call(forward_kernel, in_specs=[VMEM] * 5, out_specs=[VMEM] * 2,...  14.7 us
    pallas_call x1, Pallas kernels, load(): pl.pallas_call(load_kernel, in_specs=[pl.BlockSpec(memory_space=pl.ANY)]...  4.68 us
  transfers between devices with their start and end apart: 32, of which 14 were waited for; matrix products, arithmetic and copies ran while one was open for 1% of the time, Pallas kernels for 32%

profile of v7, /device:TPU:0, one launch (start us, length us, event | category | flops | bytes accessed | tf_op | source)
XLA Modules:
  0.0 114.1 jit_solution(16989893523536718427)
XLA Ops:
  0.6 2.2 %prepare.1 = (bf16[3072,128]{1,0:T(8,128)(2,1)}, bf16[1024,128]{1,0:T(8,128)(2,1)}) custom-call(bf16[1024,128]{1,0:T(8,128)(2,1)} %w0.1, bf16[1024,128]{1,0:T(8,128)(2,1)} %w1.1, bf16[1024,128]{1,0:T(8,128)(2,1)} %w2.1, bf16[128,1024]{1,0:T(8,128)(2,1)} %grad_ref.1, s32[1,128]{1,0:T(1,128)} %bitcast.5), custom_call_target="tpu_custom_call" | custom-call | flops 131 | bytes 2097 | tf_op jit(solution)/shard_map/prepare/pallas_call | solution.py:88
  2.8 3.2 %collective-permute-start.2 = (bf16[3072,128]{1,0:T(8,128)(2,1)}, bf16[3072,128]{1,0:T(8,128)(2,1)S(1)}, u32[]{:S(2)}, u32[]{:S(2)}) collective-permute-start(bf16[3072,128]{1,0:T(8,128)(2,1)} %get-tuple-element.109.wa), channel_id=1, source_target_pairs={{0,96},{1,33},{2,98},{3,35},{4,100},{5,37},{6,102},{7,39},{8,104},... | collective-permute-start | bytes 2359304 | tf_op jit(solution)/shard_map/ppermute | solution.py:36
  6.0 3.0 %collective-permute-start = (bf16[1024,128]{1,0:T(8,128)(2,1)}, bf16[1024,128]{1,0:T(8,128)(2,1)S(1)}, u32[]{:S(2)}, u32[]{:S(2)}) collective-permute-start(bf16[1024,128]{1,0:T(8,128)(2,1)} %get-tuple-element.107), channel_id=1, source_target_pairs={{0,2},{1,3},{2,0},{3,1},{4,6},{5,7},{6,4},{7,5},{8,10},{9,11},{10,... | collective-permute-start | bytes 786440 | tf_op jit(solution)/shard_map/ppermute | solution.py:36
  9.6 4.7 %load.1 = (bf16[2048,1024]{1,0:T(8,128)(2,1)S(1)}, bf16[2048,1024]{1,0:T(8,128)(2,1)S(1)}, bf16[2048,1024]{1,0:T(8,128)(2,1)S(1)}) custom-call(bf16[2048,1024]{1,0:T(8,128)(2,1)} %refs_0_, bf16[2048,1024]{1,0:T(8,128)(2,1)} %refs_1_, bf16[2048,1024]{1,0:T(8,128)(2,1)} %refs_2_), custom_call_target="tpu_custom_call" | custom-call | bytes 25165 | tf_op jit(solution)/shard_map/load/pallas_call | solution.py:116
  14.3 2.6 %collective-permute-done = bf16[1024,128]{1,0:T(8,128)(2,1)S(1)} collective-permute-done((bf16[1024,128]{1,0:T(8,128)(2,1)}, bf16[1024,128]{1,0:T(8,128)(2,1)S(1)}, u32[]{:S(2)}, u32[]{:S(2)}) %collective-permute-start) | collective-permute-done | bytes 262176 | tf_op jit(solution)/shard_map/ppermute | solution.py:36
  17.0 4.1 %collective-permute-start.5 = (bf16[2,1024,128]{2,1,0:T(8,128)(2,1)S(1)}, bf16[2,1024,128]{2,1,0:T(8,128)(2,1)S(1)}, u32[]{:S(2)}, u32[]{:S(2)}) collective-permute-start(bf16[2,1024,128]{2,1,0:T(8,128)(2,1)S(1)} %pad_maximum_fusion.refs_0_), channel_id=1, source_target_pairs={{0,12},{1,5},{2,14},{3,7},{4,0},{5,9},{6,2},{7,11},{8,4},{9,13},{1... | collective-permute-start | bytes 1572872 | tf_op jit(solution)/shard_map/ppermute | solution.py:36
  21.1 2.2 %collective-permute-done.2.wa = bf16[3072,128]{1,0:T(8,128)(2,1)S(1)} collective-permute-done((bf16[3072,128]{1,0:T(8,128)(2,1)}, bf16[3072,128]{1,0:T(8,128)(2,1)S(1)}, u32[]{:S(2)}, u32[]{:S(2)}) %collective-permute-start.2) | collective-permute-done | bytes 786464 | tf_op jit(solution)/shard_map/ppermute | solution.py:36
  23.8 1.6 %collective-permute-start.7 = (bf16[3072,128]{1,0:T(8,128)(2,1)S(1)}, bf16[3072,128]{1,0:T(8,128)(2,1)S(1)}, u32[]{:S(2)}, u32[]{:S(2)}) collective-permute-start(bf16[3072,128]{1,0:T(8,128)(2,1)S(1)} %collective-permute-done.1.wb), channel_id=1, source_target_pairs={{0,32},{1,97},{2,34},{3,99},{4,36},{5,101},{6,38},{7,103},{8,40},{... | collective-permute-start | bytes 2359304 | tf_op jit(solution)/shard_map/ppermute | solution.py:36
  25.3 3.7 %forward.4 = (bf16[4,2,128,256]{3,2,1,0:T(8,128)(2,1)S(1)}, bf16[4,2,128,256]{3,2,1,0:T(8,128)(2,1)S(1)}) custom-call(bf16[2048,1024]{1,0:T(8,128)(2,1)S(1)} %get-tuple-element.114.s0.refs_8_, bf16[2048,1024]{1,0:T(8,128)(2,1)S(1)} %get-tuple-element.115.s1.refs_9_, bf16[2048,1024]{1,0:T(8,128)(2,1)S(1)} %get-tuple-element.116.s2.refs_10_, ...), custom_call_target="tpu_custom_call" | custom-call | flops 3221225 | bytes 14680 | tf_op jit(solution)/shard_map/forward/pallas_call | solution.py:150
  33.0 1.9 %collective-permute-start.9 = (bf16[2,1024,128]{2,1,0:T(8,128)(2,1)S(1)}, bf16[2,1024,128]{2,1,0:T(8,128)(2,1)S(1)}, u32[]{:S(2)}, u32[]{:S(2)}) collective-permute-start(bf16[2,1024,128]{2,1,0:T(8,128)(2,1)S(1)} %collective-permute-done.4.refs_1_), channel_id=1, source_target_pairs={{0,4},{1,13},{2,6},{3,15},{4,8},{5,1},{6,10},{7,3},{8,12},{9,5},{1... | collective-permute-start | bytes 1572872 | tf_op jit(solution)/shard_map/ppermute | solution.py:36
  35.2 1.8 %collective-permute-done.7.wb = bf16[3072,128]{1,0:T(8,128)(2,1)S(1)} collective-permute-done((bf16[3072,128]{1,0:T(8,128)(2,1)S(1)}, bf16[3072,128]{1,0:T(8,128)(2,1)S(1)}, u32[]{:S(2)}, u32[]{:S(2)}) %collective-permute-start.7) | collective-permute-done | bytes 786464 | tf_op jit(solution)/shard_map/ppermute | solution.py:36
  37.0 1.5 %collective-permute-start.14 = (bf16[3072,128]{1,0:T(8,128)(2,1)S(1)}, bf16[3072,128]{1,0:T(8,128)(2,1)S(1)}, u32[]{:S(2)}, u32[]{:S(2)}) collective-permute-start(bf16[3072,128]{1,0:T(8,128)(2,1)S(1)} %collective-permute-done.7.wb), channel_id=1, source_target_pairs={{0,16},{1,17},{2,18},{3,19},{4,20},{5,21},{6,22},{7,23},{8,24},{9,... | collective-permute-start | bytes 2359304 | tf_op jit(solution)/shard_map/ppermute | solution.py:36
  38.5 3.7 %forward.5 = (bf16[4,2,128,256]{3,2,1,0:T(8,128)(2,1)S(1)}, bf16[4,2,128,256]{3,2,1,0:T(8,128)(2,1)S(1)}) custom-call(bf16[2048,1024]{1,0:T(8,128)(2,1)S(1)} %get-tuple-element.114.s0.refs_8_, bf16[2048,1024]{1,0:T(8,128)(2,1)S(1)} %get-tuple-element.115.s1.refs_9_, bf16[2048,1024]{1,0:T(8,128)(2,1)S(1)} %get-tuple-element.116.s2.refs_10_, ...), custom_call_target="tpu_custom_call" | custom-call | flops 3221225 | bytes 14680 | tf_op jit(solution)/shard_map/forward/pallas_call | solution.py:150
  42.2 2.1 %collective-permute-done.9.refs_3_ = bf16[2,1024,128]{2,1,0:T(8,128)(2,1)S(1)} collective-permute-done((bf16[2,1024,128]{2,1,0:T(8,128)(2,1)S(1)}, bf16[2,1024,128]{2,1,0:T(8,128)(2,1)S(1)}, u32[]{:S(2)}, u32[]{:S(2)}) %collective-permute-start.9) | collective-permute-done | bytes 524320 | tf_op jit(solution)/shard_map/ppermute | solution.py:36
  44.7 1.7 %collective-permute-start.16 = (bf16[3072,128]{1,0:T(8,128)(2,1)S(1)}, bf16[3072,128]{1,0:T(8,128)(2,1)S(1)}, u32[]{:S(2)}, u32[]{:S(2)}) collective-permute-start(bf16[3072,128]{1,0:T(8,128)(2,1)S(1)} %collective-permute-done.3.wa), channel_id=1, source_target_pairs={{0,96},{1,33},{2,98},{3,35},{4,100},{5,37},{6,102},{7,39},{8,104},... | collective-permute-start | bytes 2359304 | tf_op jit(solution)/shard_map/ppermute | solution.py:36
  46.4 7.5 %backward.2 = (bf16[3,128,1024]{2,1,0:T(8,128)(2,1)S(1)}, bf16[3,128,1024]{2,1,0:T(8,128)(2,1)S(1)}, bf16[3,128,1024]{2,1,0:T(8,128)(2,1)S(1)}, bf16[3,128,1024]{2,1,0:T(8,128)(2,1)S(1)}) custom-call(bf16[2,1024,128]{2,1,0:T(8,128)(2,1)S(1)} %pad_maximum_fusion.refs_0_, bf16[2,1024,128]{2,1,0:T(8,128)(2,1)S(1)} %collective-permute-done.4.refs_1_, ...), custom_call_target="tpu_custom_call" | custom-call | flops 6442450 | bytes 20971 | tf_op jit(solution)/shard_map/backward/pallas_call | solution.py:201
  53.9 3.2 %collective-permute-done.14.wa = bf16[3072,128]{1,0:T(8,128)(2,1)S(1)} collective-permute-done((bf16[3072,128]{1,0:T(8,128)(2,1)S(1)}, bf16[3072,128]{1,0:T(8,128)(2,1)S(1)}, u32[]{:S(2)}, u32[]{:S(2)}) %collective-permute-start.14) | collective-permute-done | bytes 786464 | tf_op jit(solution)/shard_map/ppermute | solution.py:36
  57.1 1.6 %collective-permute-start.17 = (bf16[3,128,1024]{2,1,0:T(8,128)(2,1)S(1)}, bf16[3,128,1024]{2,1,0:T(8,128)(2,1)S(1)}, u32[]{:S(2)}, u32[]{:S(2)}) collective-permute-start(bf16[3,128,1024]{2,1,0:T(8,128)(2,1)S(1)} %get-tuple-element.145), channel_id=1, source_target_pairs={{0,16},{1,17},{2,18},{3,19},{4,20},{5,21},{6,22},{7,23},{8,24},{9,... | collective-permute-start | bytes 2359304 | tf_op jit(solution)/shard_map/ppermute | solution.py:36
  58.7 1.6 %collective-permute-start.18 = (bf16[3,128,1024]{2,1,0:T(8,128)(2,1)S(1)}, bf16[3,128,1024]{2,1,0:T(8,128)(2,1)S(1)}, u32[]{:S(2)}, u32[]{:S(2)}) collective-permute-start(bf16[3,128,1024]{2,1,0:T(8,128)(2,1)S(1)} %get-tuple-element.146), channel_id=1, source_target_pairs={{0,96},{1,33},{2,98},{3,35},{4,100},{5,37},{6,102},{7,39},{8,104},... | collective-permute-start | bytes 2359304 | tf_op jit(solution)/shard_map/ppermute | solution.py:36
  61.2 7.5 %backward.3 = (bf16[3,128,1024]{2,1,0:T(8,128)(2,1)S(1)}, bf16[3,128,1024]{2,1,0:T(8,128)(2,1)S(1)}, bf16[3,128,1024]{2,1,0:T(8,128)(2,1)S(1)}, bf16[3,128,1024]{2,1,0:T(8,128)(2,1)S(1)}) custom-call(bf16[2,1024,128]{2,1,0:T(8,128)(2,1)S(1)} %pad_maximum_fusion.refs_0_, bf16[2,1024,128]{2,1,0:T(8,128)(2,1)S(1)} %collective-permute-done.4.refs_1_, ...), custom_call_target="tpu_custom_call" | custom-call | flops 6442450 | bytes 20971 | tf_op jit(solution)/shard_map/backward/pallas_call | solution.py:201
  69.0 3.3 %collective-permute-start.20 = (bf16[2,128,384]{2,1,0:T(8,128)(2,1)S(1)}, bf16[2,128,384]{2,1,0:T(8,128)(2,1)S(1)}, u32[]{:S(2)}, u32[]{:S(2)}) collective-permute-start(bf16[2,128,384]{2,1,0:T(8,128)(2,1)S(1)} %get-tuple-element.148), channel_id=1, source_target_pairs={{0,12},{1,5},{2,14},{3,7},{4,0},{5,9},{6,2},{7,11},{8,4},{9,13},{1... | collective-permute-start | bytes 589832 | tf_op jit(solution)/shard_map/ppermute | solution.py:36
  72.3 3.7 %forward.6 = (bf16[4,2,128,256]{3,2,1,0:T(8,128)(2,1)S(1)}, bf16[4,2,128,256]{3,2,1,0:T(8,128)(2,1)S(1)}) custom-call(bf16[2048,1024]{1,0:T(8,128)(2,1)S(1)} %get-tuple-element.114.s0.refs_8_, bf16[2048,1024]{1,0:T(8,128)(2,1)S(1)} %get-tuple-element.115.s1.refs_9_, bf16[2048,1024]{1,0:T(8,128)(2,1)S(1)} %get-tuple-element.116.s2.refs_10_, ...), custom_call_target="tpu_custom_call" | custom-call | flops 3221225 | bytes 14680 | tf_op jit(solution)/shard_map/forward/pallas_call | solution.py:150
  75.9 3.7 %forward.7 = (bf16[4,2,128,256]{3,2,1,0:T(8,128)(2,1)S(1)}, bf16[4,2,128,256]{3,2,1,0:T(8,128)(2,1)S(1)}) custom-call(bf16[2048,1024]{1,0:T(8,128)(2,1)S(1)} %get-tuple-element.114.s0.refs_8_, bf16[2048,1024]{1,0:T(8,128)(2,1)S(1)} %get-tuple-element.115.s1.refs_9_, bf16[2048,1024]{1,0:T(8,128)(2,1)S(1)} %get-tuple-element.116.s2.refs_10_, ...), custom_call_target="tpu_custom_call" | custom-call | flops 3221225 | bytes 14680 | tf_op jit(solution)/shard_map/forward/pallas_call | solution.py:150
  80.6 3.3 %collective-permute-start.29 = (bf16[3,128,1024]{2,1,0:T(8,128)(2,1)S(1)}, bf16[3,128,1024]{2,1,0:T(8,128)(2,1)S(1)}, u32[]{:S(2)}, u32[]{:S(2)}) collective-permute-start(bf16[3,128,1024]{2,1,0:T(8,128)(2,1)S(1)} %add_convert_fusion.1), channel_id=1, source_target_pairs={{0,96},{1,33},{2,98},{3,35},{4,100},{5,37},{6,102},{7,39},{8,104},... | collective-permute-start | bytes 2359304 | tf_op jit(solution)/shard_map/ppermute | solution.py:36
  84.3 3.2 %collective-permute-start.24 = (bf16[2,128,640]{2,1,0:T(8,128)(2,1)S(1)}, bf16[2,128,640]{2,1,0:T(8,128)(2,1)S(1)}, u32[]{:S(2)}, u32[]{:S(2)}) collective-permute-start(bf16[2,128,640]{2,1,0:T(8,128)(2,1)S(1)} %get-tuple-element.159), channel_id=1, source_target_pairs={{0,12},{1,5},{2,14},{3,7},{4,0},{5,9},{6,2},{7,11},{8,4},{9,13},{1... | collective-permute-start | bytes 983048 | tf_op jit(solution)/shard_map/ppermute | solution.py:36
  88.6 4.9 %collective-permute-done.24.tb = bf16[2,128,640]{2,1,0:T(8,128)(2,1)S(1)} collective-permute-done((bf16[2,128,640]{2,1,0:T(8,128)(2,1)S(1)}, bf16[2,128,640]{2,1,0:T(8,128)(2,1)S(1)}, u32[]{:S(2)}, u32[]{:S(2)}) %collective-permute-start.24) | collective-permute-done | bytes 327712 | tf_op jit(solution)/shard_map/ppermute | solution.py:36
  93.4 2.4 %collective-permute-done.25.c1 = bf16[2,128,640]{2,1,0:T(8,128)(2,1)S(1)} collective-permute-done((bf16[2,128,640]{2,1,0:T(8,128)(2,1)S(1)}, bf16[2,128,640]{2,1,0:T(8,128)(2,1)S(1)}, u32[]{:S(2)}, u32[]{:S(2)}) %collective-permute-start.25) | collective-permute-done | bytes 327712 | tf_op jit(solution)/shard_map/ppermute | solution.py:36
  97.6 3.3 %collective-permute-start.30 = (bf16[3,128,1024]{2,1,0:T(8,128)(2,1)S(1)}, bf16[3,128,1024]{2,1,0:T(8,128)(2,1)S(1)}, u32[]{:S(2)}, u32[]{:S(2)}) collective-permute-start(bf16[3,128,1024]{2,1,0:T(8,128)(2,1)S(1)} %add_convert_fusion), channel_id=1, source_target_pairs={{0,96},{1,33},{2,98},{3,35},{4,100},{5,37},{6,102},{7,39},{8,104},... | collective-permute-start | bytes 2359304 | tf_op jit(solution)/shard_map/ppermute | solution.py:36
  100.9 4.2 %collective-permute-done.26.b = bf16[2,128,1024]{2,1,0:T(8,128)(2,1)S(1)} collective-permute-done((bf16[2,128,1024]{2,1,0:T(8,128)(2,1)S(1)}, bf16[2,128,1024]{2,1,0:T(8,128)(2,1)S(1)}, u32[]{:S(2)}, u32[]{:S(2)}) %collective-permute-start.26) | collective-permute-done | bytes 524320 | tf_op jit(solution)/shard_map/ppermute | solution.py:36
  105.4 2.8 %collective-permute-start.27 = (bf16[128,1024]{1,0:T(8,128)(2,1)S(1)}, bf16[128,1024]{1,0:T(8,128)(2,1)S(1)}, u32[]{:S(2)}, u32[]{:S(2)}) collective-permute-start(bf16[128,1024]{1,0:T(8,128)(2,1)S(1)} %get-tuple-element.170), channel_id=1, source_target_pairs={{0,2},{1,3},{2,0},{3,1},{4,6},{5,7},{6,4},{7,5},{8,10},{9,11},{10,... | collective-permute-start | bytes 786440 | tf_op jit(solution)/shard_map/ppermute | solution.py:36
  108.2 2.2 %collective-permute-done.30.c = bf16[3,128,1024]{2,1,0:T(8,128)(2,1)S(1)} collective-permute-done((bf16[3,128,1024]{2,1,0:T(8,128)(2,1)S(1)}, bf16[3,128,1024]{2,1,0:T(8,128)(2,1)S(1)}, u32[]{:S(2)}, u32[]{:S(2)}) %collective-permute-start.30) | collective-permute-done | bytes 786464 | tf_op jit(solution)/shard_map/ppermute | solution.py:36
  111.7 1.6 %collective-permute-done.27.b = bf16[128,1024]{1,0:T(8,128)(2,1)S(1)} collective-permute-done((bf16[128,1024]{1,0:T(8,128)(2,1)S(1)}, bf16[128,1024]{1,0:T(8,128)(2,1)S(1)}, u32[]{:S(2)}, u32[]{:S(2)}) %collective-permute-start.27) | collective-permute-done | bytes 262176 | tf_op jit(solution)/shard_map/ppermute | solution.py:36
  (54 shorter events, 13.5 us)
Async XLA Ops:
  2.8 20.4 %collective-permute-start.2 = (bf16[3072,128]{1,0:T(8,128)(2,1)}, bf16[3072,128]{1,0:T(8,128)(2,1)S(1)}, u32[]{:S(2)}, u32[]{:S(2)}) collective-permute-start(bf16[3072,128]{1,0:T(8,128)(2,1)} %get-tuple-element.109.wa), channel_id=1, source_target_pairs={{0,96},{1,33},{2,98},{3,35},{4,100},{5,37},{6,102},{7,39},{8,104},... | collective-permute-start | bytes 2359304 | tf_op jit(solution)/shard_map/ppermute | solution.py:36
  6.0 17.8 %collective-permute-start.1 = (bf16[3072,128]{1,0:T(8,128)(2,1)}, bf16[3072,128]{1,0:T(8,128)(2,1)S(1)}, u32[]{:S(2)}, u32[]{:S(2)}) collective-permute-start(bf16[3072,128]{1,0:T(8,128)(2,1)} %get-tuple-element.109.wa), channel_id=1, source_target_pairs={{0,32},{1,97},{2,34},{3,99},{4,36},{5,101},{6,38},{7,103},{8,40},{... | collective-permute-start | bytes 2359304 | tf_op jit(solution)/shard_map/ppermute | solution.py:36
  6.0 10.9 %collective-permute-start = (bf16[1024,128]{1,0:T(8,128)(2,1)}, bf16[1024,128]{1,0:T(8,128)(2,1)S(1)}, u32[]{:S(2)}, u32[]{:S(2)}) collective-permute-start(bf16[1024,128]{1,0:T(8,128)(2,1)} %get-tuple-element.107), channel_id=1, source_target_pairs={{0,2},{1,3},{2,0},{3,1},{4,6},{5,7},{6,4},{7,5},{8,10},{9,11},{10,... | collective-permute-start | bytes 786440 | tf_op jit(solution)/shard_map/ppermute | solution.py:36
  9.0 23.5 %collective-permute-start.3 = (bf16[3072,128]{1,0:T(8,128)(2,1)}, bf16[3072,128]{1,0:T(8,128)(2,1)S(1)}, u32[]{:S(2)}, u32[]{:S(2)}) collective-permute-start(bf16[3072,128]{1,0:T(8,128)(2,1)} %get-tuple-element.109.wa), channel_id=1, source_target_pairs={{0,16},{1,17},{2,18},{3,19},{4,20},{5,21},{6,22},{7,23},{8,24},{9,... | collective-permute-start | bytes 2359304 | tf_op jit(solution)/shard_map/ppermute | solution.py:36
  17.0 13.1 %collective-permute-start.5 = (bf16[2,1024,128]{2,1,0:T(8,128)(2,1)S(1)}, bf16[2,1024,128]{2,1,0:T(8,128)(2,1)S(1)}, u32[]{:S(2)}, u32[]{:S(2)}) collective-permute-start(bf16[2,1024,128]{2,1,0:T(8,128)(2,1)S(1)} %pad_maximum_fusion.refs_0_), channel_id=1, source_target_pairs={{0,12},{1,5},{2,14},{3,7},{4,0},{5,9},{6,2},{7,11},{8,4},{9,13},{1... | collective-permute-start | bytes 1572872 | tf_op jit(solution)/shard_map/ppermute | solution.py:36
  21.1 10.4 %collective-permute-start.4 = (bf16[2,1024,128]{2,1,0:T(8,128)(2,1)S(1)}, bf16[2,1024,128]{2,1,0:T(8,128)(2,1)S(1)}, u32[]{:S(2)}, u32[]{:S(2)}) collective-permute-start(bf16[2,1024,128]{2,1,0:T(8,128)(2,1)S(1)} %pad_maximum_fusion.refs_0_), channel_id=1, source_target_pairs={{0,4},{1,13},{2,6},{3,15},{4,8},{5,1},{6,10},{7,3},{8,12},{9,5},{1... | collective-permute-start | bytes 1572872 | tf_op jit(solution)/shard_map/ppermute | solution.py:36
  23.8 8.8 %collective-permute-start.6 = (bf16[2,1024,128]{2,1,0:T(8,128)(2,1)S(1)}, bf16[2,1024,128]{2,1,0:T(8,128)(2,1)S(1)}, u32[]{:S(2)}, u32[]{:S(2)}) collective-permute-start(bf16[2,1024,128]{2,1,0:T(8,128)(2,1)S(1)} %pad_maximum_fusion.refs_0_), channel_id=1, source_target_pairs={{0,1},{1,0},{2,3},{3,2},{4,5},{5,4},{6,7},{7,6},{8,9},{9,8},{10,11... | collective-permute-start | bytes 1572872 | tf_op jit(solution)/shard_map/ppermute | solution.py:36
  23.8 13.2 %collective-permute-start.7 = (bf16[3072,128]{1,0:T(8,128)(2,1)S(1)}, bf16[3072,128]{1,0:T(8,128)(2,1)S(1)}, u32[]{:S(2)}, u32[]{:S(2)}) collective-permute-start(bf16[3072,128]{1,0:T(8,128)(2,1)S(1)} %collective-permute-done.1.wb), channel_id=1, source_target_pairs={{0,32},{1,97},{2,34},{3,99},{4,36},{5,101},{6,38},{7,103},{8,40},{... | collective-permute-start | bytes 2359304 | tf_op jit(solution)/shard_map/ppermute | solution.py:36
  32.5 9.6 %collective-permute-start.11 = (bf16[2,1024,128]{2,1,0:T(8,128)(2,1)S(1)}, bf16[2,1024,128]{2,1,0:T(8,128)(2,1)S(1)}, u32[]{:S(2)}, u32[]{:S(2)}) collective-permute-start(bf16[2,1024,128]{2,1,0:T(8,128)(2,1)S(1)} %collective-permute-done.5.refs_2_), channel_id=1, source_target_pairs={{0,1},{1,0},{2,3},{3,2},{4,5},{5,4},{6,7},{7,6},{8,9},{9,8},{10,11... | collective-permute-start | bytes 1572872 | tf_op jit(solution)/shard_map/ppermute | solution.py:36
  32.5 9.6 %collective-permute-start.10 = (bf16[2,1024,128]{2,1,0:T(8,128)(2,1)S(1)}, bf16[2,1024,128]{2,1,0:T(8,128)(2,1)S(1)}, u32[]{:S(2)}, u32[]{:S(2)}) collective-permute-start(bf16[2,1024,128]{2,1,0:T(8,128)(2,1)S(1)} %collective-permute-done.4.refs_1_), channel_id=1, source_target_pairs={{0,1},{1,0},{2,3},{3,2},{4,5},{5,4},{6,7},{7,6},{8,9},{9,8},{10,11... | collective-permute-start | bytes 1572872 | tf_op jit(solution)/shard_map/ppermute | solution.py:36
  33.0 11.2 %collective-permute-start.9 = (bf16[2,1024,128]{2,1,0:T(8,128)(2,1)S(1)}, bf16[2,1024,128]{2,1,0:T(8,128)(2,1)S(1)}, u32[]{:S(2)}, u32[]{:S(2)}) collective-permute-start(bf16[2,1024,128]{2,1,0:T(8,128)(2,1)S(1)} %collective-permute-done.4.refs_1_), channel_id=1, source_target_pairs={{0,4},{1,13},{2,6},{3,15},{4,8},{5,1},{6,10},{7,3},{8,12},{9,5},{1... | collective-permute-start | bytes 1572872 | tf_op jit(solution)/shard_map/ppermute | solution.py:36
  35.0 19.0 %collective-permute-start.13 = (bf16[3072,128]{1,0:T(8,128)(2,1)S(1)}, bf16[3072,128]{1,0:T(8,128)(2,1)S(1)}, u32[]{:S(2)}, u32[]{:S(2)}) collective-permute-start(bf16[3072,128]{1,0:T(8,128)(2,1)S(1)} %collective-permute-done.3.wa), channel_id=1, source_target_pairs={{0,32},{1,97},{2,34},{3,99},{4,36},{5,101},{6,38},{7,103},{8,40},{... | collective-permute-start | bytes 2359304 | tf_op jit(solution)/shard_map/ppermute | solution.py:36
  37.0 20.2 %collective-permute-start.14 = (bf16[3072,128]{1,0:T(8,128)(2,1)S(1)}, bf16[3072,128]{1,0:T(8,128)(2,1)S(1)}, u32[]{:S(2)}, u32[]{:S(2)}) collective-permute-start(bf16[3072,128]{1,0:T(8,128)(2,1)S(1)} %collective-permute-done.7.wb), channel_id=1, source_target_pairs={{0,16},{1,17},{2,18},{3,19},{4,20},{5,21},{6,22},{7,23},{8,24},{9,... | collective-permute-start | bytes 2359304 | tf_op jit(solution)/shard_map/ppermute | solution.py:36
  44.2 2.2 %collective-permute-start.15 = (bf16[2,1024,128]{2,1,0:T(8,128)(2,1)S(1)}, bf16[2,1024,128]{2,1,0:T(8,128)(2,1)S(1)}, u32[]{:S(2)}, u32[]{:S(2)}) collective-permute-start(bf16[2,1024,128]{2,1,0:T(8,128)(2,1)S(1)} %collective-permute-done.9.refs_3_), channel_id=1, source_target_pairs={{0,1},{1,0},{2,3},{3,2},{4,5},{5,4},{6,7},{7,6},{8,9},{9,8},{10,11... | collective-permute-start | bytes 1572872 | tf_op jit(solution)/shard_map/ppermute | solution.py:36
  44.2 16.5 %collective-permute-start.8 = (bf16[4,2,128,256]{3,2,1,0:T(8,128)(2,1)S(1)}, bf16[4,2,128,256]{3,2,1,0:T(8,128)(2,1)S(1)}, u32[]{:S(2)}, u32[]{:S(2)}) collective-permute-start(bf16[4,2,128,256]{3,2,1,0:T(8,128)(2,1)S(1)} %get-tuple-element.119), channel_id=1, source_target_pairs={{0,1},{1,0},{2,3},{3,2},{4,5},{5,4},{6,7},{7,6},{8,9},{9,8},{10,11... | collective-permute-start | bytes 1572872 | tf_op jit(solution)/shard_map/ppermute | solution.py:36
  44.7 27.5 %collective-permute-start.16 = (bf16[3072,128]{1,0:T(8,128)(2,1)S(1)}, bf16[3072,128]{1,0:T(8,128)(2,1)S(1)}, u32[]{:S(2)}, u32[]{:S(2)}) collective-permute-start(bf16[3072,128]{1,0:T(8,128)(2,1)S(1)} %collective-permute-done.3.wa), channel_id=1, source_target_pairs={{0,96},{1,33},{2,98},{3,35},{4,100},{5,37},{6,102},{7,39},{8,104},... | collective-permute-start | bytes 2359304 | tf_op jit(solution)/shard_map/ppermute | solution.py:36
  57.1 22.5 %collective-permute-start.17 = (bf16[3,128,1024]{2,1,0:T(8,128)(2,1)S(1)}, bf16[3,128,1024]{2,1,0:T(8,128)(2,1)S(1)}, u32[]{:S(2)}, u32[]{:S(2)}) collective-permute-start(bf16[3,128,1024]{2,1,0:T(8,128)(2,1)S(1)} %get-tuple-element.145), channel_id=1, source_target_pairs={{0,16},{1,17},{2,18},{3,19},{4,20},{5,21},{6,22},{7,23},{8,24},{9,... | collective-permute-start | bytes 2359304 | tf_op jit(solution)/shard_map/ppermute | solution.py:36
  58.7 21.0 %collective-permute-start.18 = (bf16[3,128,1024]{2,1,0:T(8,128)(2,1)S(1)}, bf16[3,128,1024]{2,1,0:T(8,128)(2,1)S(1)}, u32[]{:S(2)}, u32[]{:S(2)}) collective-permute-start(bf16[3,128,1024]{2,1,0:T(8,128)(2,1)S(1)} %get-tuple-element.146), channel_id=1, source_target_pairs={{0,96},{1,33},{2,98},{3,35},{4,100},{5,37},{6,102},{7,39},{8,104},... | collective-permute-start | bytes 2359304 | tf_op jit(solution)/shard_map/ppermute | solution.py:36
  60.3 19.4 %collective-permute-start.19 = (bf16[3,128,1024]{2,1,0:T(8,128)(2,1)S(1)}, bf16[3,128,1024]{2,1,0:T(8,128)(2,1)S(1)}, u32[]{:S(2)}, u32[]{:S(2)}) collective-permute-start(bf16[3,128,1024]{2,1,0:T(8,128)(2,1)S(1)} %get-tuple-element.147), channel_id=1, source_target_pairs={{0,32},{1,97},{2,34},{3,99},{4,36},{5,101},{6,38},{7,103},{8,40},{... | collective-permute-start | bytes 2359304 | tf_op jit(solution)/shard_map/ppermute | solution.py:36
  60.7 8.0 %collective-permute-start.12 = (bf16[4,2,128,256]{3,2,1,0:T(8,128)(2,1)S(1)}, bf16[4,2,128,256]{3,2,1,0:T(8,128)(2,1)S(1)}, u32[]{:S(2)}, u32[]{:S(2)}) collective-permute-start(bf16[4,2,128,256]{3,2,1,0:T(8,128)(2,1)S(1)} %get-tuple-element.123), channel_id=1, source_target_pairs={{0,1},{1,0},{2,3},{3,2},{4,5},{5,4},{6,7},{7,6},{8,9},{9,8},{10,11... | collective-permute-start | bytes 1572872 | tf_op jit(solution)/shard_map/ppermute | solution.py:36
  69.0 10.7 %collective-permute-start.20 = (bf16[2,128,384]{2,1,0:T(8,128)(2,1)S(1)}, bf16[2,128,384]{2,1,0:T(8,128)(2,1)S(1)}, u32[]{:S(2)}, u32[]{:S(2)}) collective-permute-start(bf16[2,128,384]{2,1,0:T(8,128)(2,1)S(1)} %get-tuple-element.148), channel_id=1, source_target_pairs={{0,12},{1,5},{2,14},{3,7},{4,0},{5,9},{6,2},{7,11},{8,4},{9,13},{1... | collective-permute-start | bytes 589832 | tf_op jit(solution)/shard_map/ppermute | solution.py:36
  72.3 7.4 %collective-permute-start.21 = (bf16[2,128,384]{2,1,0:T(8,128)(2,1)S(1)}, bf16[2,128,384]{2,1,0:T(8,128)(2,1)S(1)}, u32[]{:S(2)}, u32[]{:S(2)}) collective-permute-start(bf16[2,128,384]{2,1,0:T(8,128)(2,1)S(1)} %get-tuple-element.149), channel_id=1, source_target_pairs={{0,4},{1,13},{2,6},{3,15},{4,8},{5,1},{6,10},{7,3},{8,12},{9,5},{1... | collective-permute-start | bytes 589832 | tf_op jit(solution)/shard_map/ppermute | solution.py:36
  79.7 4.3 %collective-permute-start.22 = (bf16[4,2,128,256]{3,2,1,0:T(8,128)(2,1)S(1)}, bf16[4,2,128,256]{3,2,1,0:T(8,128)(2,1)S(1)}, u32[]{:S(2)}, u32[]{:S(2)}) collective-permute-start(bf16[4,2,128,256]{3,2,1,0:T(8,128)(2,1)S(1)} %get-tuple-element.156), channel_id=1, source_target_pairs={{0,1},{1,0},{2,3},{3,2},{4,5},{5,4},{6,7},{7,6},{8,9},{9,8},{10,11... | collective-permute-start | bytes 1572872 | tf_op jit(solution)/shard_map/ppermute | solution.py:36
  80.2 3.7 %collective-permute-start.23 = (bf16[4,2,128,256]{3,2,1,0:T(8,128)(2,1)S(1)}, bf16[4,2,128,256]{3,2,1,0:T(8,128)(2,1)S(1)}, u32[]{:S(2)}, u32[]{:S(2)}) collective-permute-start(bf16[4,2,128,256]{3,2,1,0:T(8,128)(2,1)S(1)} %get-tuple-element.157), channel_id=1, source_target_pairs={{0,1},{1,0},{2,3},{3,2},{4,5},{5,4},{6,7},{7,6},{8,9},{9,8},{10,11... | collective-permute-start | bytes 1572872 | tf_op jit(solution)/shard_map/ppermute | solution.py:36
  80.6 16.7 %collective-permute-start.29 = (bf16[3,128,1024]{2,1,0:T(8,128)(2,1)S(1)}, bf16[3,128,1024]{2,1,0:T(8,128)(2,1)S(1)}, u32[]{:S(2)}, u32[]{:S(2)}) collective-permute-start(bf16[3,128,1024]{2,1,0:T(8,128)(2,1)S(1)} %add_convert_fusion.1), channel_id=1, source_target_pairs={{0,96},{1,33},{2,98},{3,35},{4,100},{5,37},{6,102},{7,39},{8,104},... | collective-permute-start | bytes 2359304 | tf_op jit(solution)/shard_map/ppermute | solution.py:36
  84.3 9.1 %collective-permute-start.24 = (bf16[2,128,640]{2,1,0:T(8,128)(2,1)S(1)}, bf16[2,128,640]{2,1,0:T(8,128)(2,1)S(1)}, u32[]{:S(2)}, u32[]{:S(2)}) collective-permute-start(bf16[2,128,640]{2,1,0:T(8,128)(2,1)S(1)} %get-tuple-element.159), channel_id=1, source_target_pairs={{0,12},{1,5},{2,14},{3,7},{4,0},{5,9},{6,2},{7,11},{8,4},{9,13},{1... | collective-permute-start | bytes 983048 | tf_op jit(solution)/shard_map/ppermute | solution.py:36
  87.5 8.3 %collective-permute-start.25 = (bf16[2,128,640]{2,1,0:T(8,128)(2,1)S(1)}, bf16[2,128,640]{2,1,0:T(8,128)(2,1)S(1)}, u32[]{:S(2)}, u32[]{:S(2)}) collective-permute-start(bf16[2,128,640]{2,1,0:T(8,128)(2,1)S(1)} %get-tuple-element.160), channel_id=1, source_target_pairs={{0,4},{1,13},{2,6},{3,15},{4,8},{5,1},{6,10},{7,3},{8,12},{9,5},{1... | collective-permute-start | bytes 983048 | tf_op jit(solution)/shard_map/ppermute | solution.py:36
  87.9 20.2 %collective-permute-start.28 = (bf16[3,128,1024]{2,1,0:T(8,128)(2,1)S(1)}, bf16[3,128,1024]{2,1,0:T(8,128)(2,1)S(1)}, u32[]{:S(2)}, u32[]{:S(2)}) collective-permute-start(bf16[3,128,1024]{2,1,0:T(8,128)(2,1)S(1)} %add_convert_fusion.2), channel_id=1, source_target_pairs={{0,16},{1,17},{2,18},{3,19},{4,20},{5,21},{6,22},{7,23},{8,24},{9,... | collective-permute-start | bytes 2359304 | tf_op jit(solution)/shard_map/ppermute | solution.py:36
  88.6 19.6 %collective-permute-start.31 = (bf16[3,128,1024]{2,1,0:T(8,128)(2,1)S(1)}, bf16[3,128,1024]{2,1,0:T(8,128)(2,1)S(1)}, u32[]{:S(2)}, u32[]{:S(2)}) collective-permute-start(bf16[3,128,1024]{2,1,0:T(8,128)(2,1)S(1)} %get-tuple-element.178), channel_id=1, source_target_pairs={{0,32},{1,97},{2,34},{3,99},{4,36},{5,101},{6,38},{7,103},{8,40},{... | collective-permute-start | bytes 2359304 | tf_op jit(solution)/shard_map/ppermute | solution.py:36
  95.9 9.3 %collective-permute-start.26 = (bf16[2,128,1024]{2,1,0:T(8,128)(2,1)S(1)}, bf16[2,128,1024]{2,1,0:T(8,128)(2,1)S(1)}, u32[]{:S(2)}, u32[]{:S(2)}) collective-permute-start(bf16[2,128,1024]{2,1,0:T(8,128)(2,1)S(1)} %pass_on.1), channel_id=1, source_target_pairs={{0,12},{1,5},{2,14},{3,7},{4,0},{5,9},{6,2},{7,11},{8,4},{9,13},{1... | collective-permute-start | bytes 1572872 | tf_op jit(solution)/shard_map/ppermute | solution.py:36
  97.6 12.8 %collective-permute-start.30 = (bf16[3,128,1024]{2,1,0:T(8,128)(2,1)S(1)}, bf16[3,128,1024]{2,1,0:T(8,128)(2,1)S(1)}, u32[]{:S(2)}, u32[]{:S(2)}) collective-permute-start(bf16[3,128,1024]{2,1,0:T(8,128)(2,1)S(1)} %add_convert_fusion), channel_id=1, source_target_pairs={{0,96},{1,33},{2,98},{3,35},{4,100},{5,37},{6,102},{7,39},{8,104},... | collective-permute-start | bytes 2359304 | tf_op jit(solution)/shard_map/ppermute | solution.py:36
  105.4 8.0 %collective-permute-start.27 = (bf16[128,1024]{1,0:T(8,128)(2,1)S(1)}, bf16[128,1024]{1,0:T(8,128)(2,1)S(1)}, u32[]{:S(2)}, u32[]{:S(2)}) collective-permute-start(bf16[128,1024]{1,0:T(8,128)(2,1)S(1)} %get-tuple-element.170), channel_id=1, source_target_pairs={{0,2},{1,3},{2,0},{3,1},{4,6},{5,7},{6,4},{7,5},{8,10},{9,11},{10,... | collective-permute-start | bytes 786440 | tf_op jit(solution)/shard_map/ppermute | solution.py:36
  (2 other events, 21.9 us)
